TPU v7x, 32 devices: a whole 2x2x4 slice. The times are simulated.
32 devices in a mesh: rep: 2 (over core), ty: 4 (over z), tx: 4 (over y, x).
Axes of the slice: x: 2, y: 2, z: 4, core: 2. Of those that a mesh axis runs over, the one named last changes fastest.
Arguments:
- tokens: bfloat16 [2, 256, 16, 512], P('rep', 'ty', 'tx'), may hold values from -160 to 160
- qkv_weight: bfloat16 [512, 1536], replicated, may hold values from -16 to 16
- cotangent: bfloat16 [2, 256, 16, 512], P('rep', 'ty', 'tx'), may hold values from -6 to 6
Outputs:
- token_grad: bfloat16 [2, 256, 16, 512], P('rep', 'ty', 'tx')
- weight_grad: float32 [512, 1536], P(('ty', 'tx'))
All inputs are finite; a program needn't handle non-finite values.
Results may differ from a plain program's by a relative error of at most 0.024.
Values may be sent and summed in bfloat16 or wider, within the bound.
No kernel may reach another device: no remote copies, remote signals or barrier semaphores. Data moves between devices by JAX's collectives and lax.ppermute only.
A program may use at most 64 MiB of HBM per device.

v0:
```python
import jax
import jax.numpy as jnp
from jax import lax
from jax.sharding import PartitionSpec as P

HEADS = 16
HEAD_DIM = 32
GRID = 8


eps_norm = 1e-05


def normalize(values):
    center = values - jnp.mean(values, axis=-1, keepdims=True)
    inv_std = lax.rsqrt(jnp.mean(center * center, axis=-1, keepdims=True) + eps_norm)
    return (center * inv_std, inv_std)


def window_grads(window_x, window_g, qkv_weight):
    win_count, win_tokens, channels = window_x.shape
    standard, inv_std = normalize(window_x.astype(jnp.float32))
    normed = standard.astype(jnp.bfloat16).reshape(win_count * win_tokens, channels)
    projection = jnp.dot(normed, qkv_weight, preferred_element_type=jnp.float32)
    head_shape = (win_count, win_tokens, HEADS, HEAD_DIM)
    query_heads = (
        (projection[:, :channels] * HEAD_DIM ** (-0.5)).astype(jnp.bfloat16).reshape(head_shape)
    )
    key_heads = projection[:, channels : 2 * channels].astype(jnp.bfloat16).reshape(head_shape)
    value_heads = projection[:, 2 * channels :].astype(jnp.bfloat16).reshape(head_shape)
    scores = jnp.einsum(
        "wqne,wkne->wnqk", query_heads, key_heads, preferred_element_type=jnp.float32
    )
    peak_score = jnp.max(scores, axis=-1, keepdims=True)
    exponent = jnp.exp(scores - peak_score)
    attn_probs = exponent / jnp.sum(exponent, axis=-1, keepdims=True)
    probs_low = attn_probs.astype(jnp.bfloat16)
    grad_heads = window_g.reshape(head_shape)
    attn_grad = jnp.einsum(
        "wqne,wkne->wnqk", grad_heads, value_heads, preferred_element_type=jnp.float32
    )
    value_grad = jnp.einsum(
        "wnqk,wqne->wkne", probs_low, grad_heads, preferred_element_type=jnp.float32
    ).astype(jnp.bfloat16)
    score_grad = (
        attn_probs * (attn_grad - jnp.sum(attn_probs * attn_grad, axis=-1, keepdims=True))
    ).astype(jnp.bfloat16)
    query_grad = (
        jnp.einsum("wnqk,wkne->wqne", score_grad, key_heads, preferred_element_type=jnp.float32)
        * HEAD_DIM ** (-0.5)
    ).astype(jnp.bfloat16)
    key_grad = jnp.einsum(
        "wnqk,wqne->wkne", score_grad, query_heads, preferred_element_type=jnp.float32
    ).astype(jnp.bfloat16)
    flat_shape = (win_count * win_tokens, channels)
    proj_grad = jnp.concatenate(
        [
            query_grad.reshape(flat_shape),
            key_grad.reshape(flat_shape),
            value_grad.reshape(flat_shape),
        ],
        axis=1,
    )
    normed_grad = lax.dot_general(
        proj_grad, qkv_weight, (((1,), (1,)), ((), ())), preferred_element_type=jnp.float32
    )
    normed_grad = normed_grad.reshape(win_count, win_tokens, channels)
    weight_term = lax.dot_general(
        normed, proj_grad, (((0,), (0,)), ((), ())), preferred_element_type=jnp.float32
    )
    inner_term = (
        normed_grad
        - jnp.mean(normed_grad, axis=-1, keepdims=True)
        - standard * jnp.mean(normed_grad * standard, axis=-1, keepdims=True)
    )
    token_grad = (window_g.astype(jnp.float32) + inv_std * inner_term).astype(jnp.bfloat16)
    return (token_grad, weight_term)


def shards(tokens, qkv_weight, cotangent):
    rep_count = lax.axis_size("rep")
    row_tiles = lax.axis_size("ty")
    col_tiles = lax.axis_size("tx")
    tile_count = row_tiles * col_tiles
    tile_height = tokens.shape[1]
    tile_width = tokens.shape[2]
    channels = tokens.shape[3]
    stride_rows = row_tiles * tile_height // GRID
    stride_cols = col_tiles * tile_width // GRID
    block_rows = min(tile_height, stride_rows)
    fold_rows = stride_rows // block_rows
    col_groups = tile_width // stride_cols
    outer_rows = tile_height // block_rows
    inner_rows = block_rows // tile_count
    split_shape = (outer_rows, tile_count, inner_rows, tile_width, channels)
    grid_x, grid_g = (
        lax.all_to_all(
            tokens.reshape(split_shape), ("ty", "tx"), split_axis=1, concat_axis=1, tiled=True
        ),
        lax.all_to_all(
            cotangent.reshape(split_shape), ("ty", "tx"), split_axis=1, concat_axis=1, tiled=True
        ),
    )
    token_shape = (
        outer_rows,
        row_tiles // fold_rows,
        fold_rows,
        col_tiles,
        inner_rows,
        col_groups,
        stride_cols,
        channels,
    )
    win_count = fold_rows * inner_rows * stride_cols

    def to_windows(values):
        return (
            values.reshape(token_shape)
            .transpose(2, 4, 6, 1, 0, 3, 5, 7)
            .reshape(win_count, GRID * GRID, channels)
        )

    grad_windows, weight_term = window_grads(to_windows(grid_x), to_windows(grid_g), qkv_weight)
    back_shape = (
        fold_rows,
        inner_rows,
        stride_cols,
        row_tiles // fold_rows,
        outer_rows,
        col_tiles,
        col_groups,
        channels,
    )
    spread = grad_windows.reshape(back_shape).transpose(4, 3, 0, 5, 1, 6, 2, 7).reshape(split_shape)
    returned = lax.all_to_all(spread, ("ty", "tx"), split_axis=1, concat_axis=1, tiled=True)
    token_grad = returned.reshape(1, tile_height, tile_width, channels)
    partial_rows = lax.psum_scatter(weight_term, ("ty", "tx"), scatter_dimension=0, tiled=True)
    weight_grad = lax.psum(partial_rows, "rep")
    weight_grad = weight_grad / (rep_count * tile_count)
    return (token_grad, weight_grad)


def solution(mesh):
    placed = (P("rep", "ty", "tx", None), P(), P("rep", "ty", "tx", None))
    return jax.shard_map(
        shards,
        mesh=mesh,
        in_specs=placed,
        out_specs=(P("rep", "ty", "tx", None), P(("ty", "tx"), None)),
        check_vma=False,
    )
```

profile of v0, /device:TPU:0, one launch (start us, length us, event | category | flops | bytes accessed | tf_op | source)
XLA Modules:
  0.0 233.9 jit_solution(3714009158223203744)
XLA Ops:
  7.2 2.0 copy.124
  9.2 8.3 %all-to-all-start.1 = ((bf16[2,16,2,4,512]{4,2,3,0,1:T(2,128)(2,1)}), bf16[2,16,2,4,512]{4,2,3,0,1:T(2,128)(2,1)S(1)}, u32[]{:S(2)}, u32[]{:S(2)}) async-start(bf16[2,16,2,4,512]{4,2,3,0,1:T(2,128)(2,1)} %copy.124), calls=%async_computation.1 | async-start | bytes 524288 | tf_op jit(solution)/shard_map/all_to_all | solution.py:97
  17.5 1.9 copy.122
  19.5 7.9 %all-to-all-done.1 = bf16[2,16,2,4,512]{4,2,3,0,1:T(2,128)(2,1)S(1)} async-done(((bf16[2,16,2,4,512]{4,2,3,0,1:T(2,128)(2,1)}), bf16[2,16,2,4,512]{4,2,3,0,1:T(2,128)(2,1)S(1)}, u32[]{:S(2)}, u32[]{:S(2)}) %all-to-all-start.1) | async-done | bytes 262176 | tf_op jit(solution)/shard_map/all_to_all | solution.py:97
  27.4 4.2 %all-to-all-start = ((bf16[2,16,2,4,512]{4,2,3,0,1:T(2,128)(2,1)}), bf16[2,16,2,4,512]{4,2,3,0,1:T(2,128)(2,1)}, u32[]{:S(2)}, u32[]{:S(2)}) async-start(bf16[2,16,2,4,512]{4,2,3,0,1:T(2,128)(2,1)} %copy.122), calls=%async_computation | async-start | bytes 524288 | tf_op jit(solution)/shard_map/all_to_all | solution.py:100
  35.6 1.8 fusion.32
  38.5 1.1 fusion.9
  40.4 2.0 reshape.137
  42.4 1.1 copy.123
  44.5 1.5 reshape_reshape.3
  46.0 2.8 %copy.141 = bf16[4,64,16,32]{1,3,2,0:T(8,128)(2,1)} copy(bf16[4,64,16,32]{3,2,1,0:T(8,128)(2,1)} %reshape_reshape.3) | data formatting | bytes 524288 | tf_op jit(solution)/shard_map/reshape;reshape | solution.py:38
  48.8 1.1 copy.138
  49.9 1.0 reshape.138
  50.9 3.2 %fusion.33 = (f32[4,16,64]{2,1,0:T(8,128)S(1)}, f32[4,16,64,64]{2,3,1,0:T(8,128)}) fusion(bf16[4,64,16,32]{1,0,3,2:T(4,128)(2,1)S(1)} %reshape.136, bf16[4,64,16,32]{1,0,3,2:T(4,128)(2,1)} %reshape.137), kind=kOutput, calls=%fused_computation.48 | convolution fusion | flops 17301568 | bytes 1589248 | tf_op jit(solution)/shard_map/sub | solution.py:35
  54.1 2.5 %fusion.6 = bf16[4,64,16,32]{1,3,2,0:T(8,128)(2,1)S(1)} fusion(bf16[4,64,16,32]{1,3,2,0:T(8,128)(2,1)} %copy.141, f32[4,16,64,64]{2,3,1,0:T(8,128)} %get-tuple-element.9, f32[4,16,64]{2,1,0:T(8,128)S(1)} %get-tuple-element.8), kind=kOutput, calls=%fused_computation.12 | convolution fusion | flops 17432576 | bytes 1589248 | tf_op jit(solution)/shard_map/wnqk,wqne->wkne/dot_general | solution.py:42
  58.5 1.5 fusion.5
  59.9 1.2 fusion.7
  61.5 1.1 reshape.141
  62.6 1.4 copy.147
  64.1 1.0 reshape.140
  65.1 1.4 copy.144
  66.6 1.0 reshape.139
  68.6 1.0 constant_dynamic-update-slice_fusion.1
  69.5 1.0 constant_dynamic-update-slice_fusion
  70.5 2.6 %fusion.26 = f32[512,1536]{1,0:T(8,128)} fusion(bf16[256,1536]{0,1:T(8,128)(2,1)S(1)} %constant_dynamic-update-slice_fusion, f32[256,512]{1,0:T(8,128)S(1)} %reshape.145, f32[256]{0:T(256)S(1)} %rsqrt.13, f32[256]{0:T(256)S(1)} %div.34), kind=kOutput, calls=%fused_computation.43 | convolution fusion | flops 403046400 | bytes 4458496 | tf_op jit(solution)/shard_map/dot_general | solution.py:68
  74.1 1.4 fusion.30
  76.9 1.4 reshape.142
  78.2 1.8 fusion.15
  81.0 6.8 %all-to-all-start.2 = ((bf16[2,16,2,4,512]{4,2,3,0,1:T(2,128)(2,1)}), bf16[2,16,2,4,512]{4,2,3,0,1:T(2,128)(2,1)S(1)}, u32[]{:S(2)}, u32[]{:S(2)}) async-start(bf16[2,16,2,4,512]{4,2,3,0,1:T(2,128)(2,1)} %copy.154), calls=%async_computation.2 | async-start | bytes 524288 | tf_op jit(solution)/shard_map/all_to_all | solution.py:135
  87.9 117.9 %reduce-scatter.2.cloned.1.call-done = f32[32,1536]{1,0:T(8,128)} async-done(((f32[512,1536]{1,0:T(8,128)}), f32[32,1536]{1,0:T(8,128)}) %reduce-scatter.2.cloned.1.call-update) | async-done | bytes 196624 | tf_op jit(solution)/shard_map/reduce_scatter | solution.py:137
  206.6 18.8 %all-reduce.2.cloned.1.call-done = f32[32,1536]{1,0:T(8,128)} async-done(((f32[32,1536]{1,0:T(8,128)}), f32[32,1536]{1,0:T(8,128)}) %all-reduce.2.cloned.1.call-update) | async-done | bytes 196624 | tf_op jit(solution)/shard_map/psum | solution.py:138
  225.5 1.6 broadcast_multiply_fusion
  (52 shorter events, 14.1 us)
Async XLA Ops:
  7.2 28.4 %copy-start = (bf16[512,1536]{1,0:T(8,128)(2,1)S(1)}, bf16[512,1536]{1,0:T(8,128)(2,1)}, u32[]{:S(2)}) copy-start(bf16[512,1536]{1,0:T(8,128)(2,1)} %param.4) | copy-start | bytes 4718596
  9.2 18.2 %all-to-all-start.1 = ((bf16[2,16,2,4,512]{4,2,3,0,1:T(2,128)(2,1)}), bf16[2,16,2,4,512]{4,2,3,0,1:T(2,128)(2,1)S(1)}, u32[]{:S(2)}, u32[]{:S(2)}) async-start(bf16[2,16,2,4,512]{4,2,3,0,1:T(2,128)(2,1)} %copy.124), calls=%async_computation.1 | async-start | bytes 524288 | tf_op jit(solution)/shard_map/all_to_all | solution.py:97
  27.4 15.0 %all-to-all-start = ((bf16[2,16,2,4,512]{4,2,3,0,1:T(2,128)(2,1)}), bf16[2,16,2,4,512]{4,2,3,0,1:T(2,128)(2,1)}, u32[]{:S(2)}, u32[]{:S(2)}) async-start(bf16[2,16,2,4,512]{4,2,3,0,1:T(2,128)(2,1)} %copy.122), calls=%async_computation | async-start | bytes 524288 | tf_op jit(solution)/shard_map/all_to_all | solution.py:100
  31.6 174.2 %reduce-scatter.2.cloned.1.call-start = ((), (), s32[]{:S(2)}) async-start(), calls=%async_computation.4 | async-start | bytes 3342336 | tf_op jit(solution)/shard_map/reduce_scatter | solution.py:137
  43.6 0.7 copy-start.1
  54.1 2.5 %copy-start.3 = (f32[4,16,64,64]{2,3,1,0:T(8,128)S(1)}, f32[4,16,64,64]{2,3,1,0:T(8,128)}, u32[]{:S(2)}) copy-start(f32[4,16,64,64]{2,3,1,0:T(8,128)} %get-tuple-element.9) | copy-start | bytes 3145732
  54.1 2.5 %copy-start.4 = (bf16[4,64,16,32]{1,3,2,0:T(8,128)(2,1)S(1)}, bf16[4,64,16,32]{1,3,2,0:T(8,128)(2,1)}, u32[]{:S(2)}) copy-start(bf16[4,64,16,32]{1,3,2,0:T(8,128)(2,1)} %copy.141) | copy-start | bytes 786436
  54.1 2.6 %copy-start.5 = (bf16[4,64,16,32]{1,0,3,2:T(4,128)(2,1)S(1)}, bf16[4,64,16,32]{1,0,3,2:T(4,128)(2,1)}, u32[]{:S(2)}) copy-start(bf16[4,64,16,32]{1,0,3,2:T(4,128)(2,1)} %reshape.138) | copy-start | bytes 786436
  57.4 1.0 copy-start.2
  74.1 4.1 %copy-start.6 = (f32[2,2,4,2,4,2]{0,1,5,4,2,3:T(2,128)S(1)}, f32[2,2,4,2,4,2]{0,1,5,4,2,3:T(2,128)}, u32[]{:S(2)}) copy-start(f32[2,2,4,2,4,2]{0,1,5,4,2,3:T(2,128)} %copy.130) | copy-start | bytes 3076
  81.0 124.8 %all-to-all-start.2 = ((bf16[2,16,2,4,512]{4,2,3,0,1:T(2,128)(2,1)}), bf16[2,16,2,4,512]{4,2,3,0,1:T(2,128)(2,1)S(1)}, u32[]{:S(2)}, u32[]{:S(2)}) async-start(bf16[2,16,2,4,512]{4,2,3,0,1:T(2,128)(2,1)} %copy.154), calls=%async_computation.2 | async-start | bytes 524288 | tf_op jit(solution)/shard_map/all_to_all | solution.py:135
  87.8 137.6 %all-reduce.2.cloned.1.call-start = ((), (), s32[]{:S(2)}) async-start(), calls=%async_computation.5 | async-start | bytes 393216 | tf_op jit(solution)/shard_map/psum | solution.py:138
Sparse Core Ops, SparseCore 0:
  73.3 132.4 reduce-scatter.1
  208.1 17.2 all-reduce.1
where the time goes:
time: 235 us; the launch traced here: 234 us
  waiting for transfers between devices  145 us (62%)
  local copies, waits for them, and re-layouts  34.5 us (15%)
  starting transfers between devices  19.4 us (8%)
  matrix products  14.8 us (6%)
  between operations  14.3 us (6%)
  other arithmetic  6.14 us (3%)
    reduce_scatter x1, waiting for transfers between devices, shards(): lax.psum_scatter(weight_term, ('ty', 'tx'), scatter_dimension=0, tiled=True)  118 us
    psum x1, waiting for transfers between devices, shards(): weight_grad = lax.psum(partial_rows, 'rep')  18.8 us
    all_to_all x1, starting transfers between devices, shards(): lax.all_to_all(tokens.reshape(split_shape), ('ty', 'tx'), split_axis=1, c...  8.31 us
    all_to_all x1, waiting for transfers between devices, shards(): lax.all_to_all(tokens.reshape(split_shape), ('ty', 'tx'), split_axis=1, c...  7.94 us
    all_to_all x1, starting transfers between devices, shards(): lax.all_to_all(spread, ('ty', 'tx'), split_axis=1, concat_axis=1, tiled=T...  6.83 us
  transfers between devices with their start and end apart: 5, of which 3 were waited for; matrix products, arithmetic and copies ran while one was open for 9% of the time, Pallas kernels for 0%

commit v1 on v0

v1 whole, which is shorter than its diff:
```python
import functools

import jax
import jax.numpy as jnp
import numpy as np
from jax import lax
from jax.experimental import pallas as pl
from jax.experimental.pallas import tpu as pltpu
from jax.sharding import PartitionSpec as P

HEADS = 16
HEAD_DIM = 32
GRID = 8
EPS = 1e-05
LANES = 128
BLOCK_HEADS = LANES // HEAD_DIM

BF16 = jnp.bfloat16
F32 = jnp.float32


def matmul(a, b, contract):
    return lax.dot_general(a, b, ((contract[:1], contract[1:]), ((), ())), preferred_element_type=F32)


def window_kernel(
    split_reps,
    pos_ref,
    pixels_ref,
    weight_ref,
    grad_ref,
    *refs,
):
    if split_reps:
        keep_ref, send_ref = refs[:2]
        refs = refs[2:]
    else:
        term_ref = refs[0]
        refs = refs[1:]
    normed_ref, standard_ref, cot_ref, query_ref, key_ref, value_ref, proj_ref = refs
    count, channels = cot_ref.shape
    win_tokens = GRID * GRID
    scale = HEAD_DIM**-0.5

    rows = lax.broadcasted_iota(jnp.int32, (count, count), 0)
    onehot = jnp.where(rows == pos_ref[...], 1.0, 0.0).astype(BF16)
    cot_ref[...] = matmul(onehot, pixels_ref[:, channels:], (1, 0)).astype(BF16)
    wide = matmul(onehot, pixels_ref[:, :channels], (1, 0))

    center = wide - jnp.mean(wide, axis=-1, keepdims=True)
    inv_std = lax.rsqrt(jnp.mean(center * center, axis=-1, keepdims=True) + EPS)
    standard = center * inv_std
    standard_ref[...] = standard
    normed = standard.astype(BF16)
    normed_ref[...] = normed

    query_ref[...] = (matmul(normed, weight_ref[:, :channels], (1, 0)) * scale).astype(BF16)
    key_ref[...] = matmul(normed, weight_ref[:, channels : 2 * channels], (1, 0)).astype(BF16)
    value_ref[...] = matmul(normed, weight_ref[:, 2 * channels :], (1, 0)).astype(BF16)

    stack_shape = (BLOCK_HEADS * win_tokens, LANES)
    own = lax.broadcasted_iota(jnp.int32, stack_shape, 0) // win_tokens == (
        lax.broadcasted_iota(jnp.int32, stack_shape, 1) // HEAD_DIM
    )
    mask = jnp.where(own, 1.0, 0.0)
    mask_low = mask.astype(BF16)

    def stack(block):
        return jnp.concatenate([block] * BLOCK_HEADS, axis=0) * mask_low

    for window in range(count // win_tokens):
        row = slice(window * win_tokens, (window + 1) * win_tokens)
        for block in range(channels // LANES):
            col = slice(block * LANES, (block + 1) * LANES)
            key = key_ref[row, col]
            queries = stack(query_ref[row, col])
            cots = stack(cot_ref[row, col])
            scores = matmul(key, queries, (1, 1))
            attn_grad = matmul(value_ref[row, col], cots, (1, 1))
            exponent = jnp.exp(scores - jnp.max(scores, axis=0, keepdims=True))
            probs = exponent * (1.0 / jnp.sum(exponent, axis=0, keepdims=True))
            score_grad = (
                probs * (attn_grad - jnp.sum(probs * attn_grad, axis=0, keepdims=True))
            ).astype(BF16)
            value_grad = matmul(probs.astype(BF16), cots, (1, 0))
            key_grad = matmul(score_grad, queries, (1, 0))
            spread = matmul(score_grad, key, (0, 0)) * mask
            query_grad = spread[:win_tokens]
            for head in range(1, BLOCK_HEADS):
                query_grad += spread[head * win_tokens : (head + 1) * win_tokens]
            base = block * LANES
            proj_ref[row, base : base + LANES] = (query_grad * scale).astype(BF16)
            base += channels
            proj_ref[row, base : base + LANES] = key_grad.astype(BF16)
            base += channels
            proj_ref[row, base : base + LANES] = value_grad.astype(BF16)

    if split_reps:
        half = 3 * channels // 2
        rep = lax.axis_index("rep")
        for ref, side in ((send_ref, 1 - rep), (keep_ref, rep)):
            start = pl.multiple_of(side * half, LANES)
            ref[...] = matmul(normed_ref[...], proj_ref[:, pl.ds(start, half)], (0, 0)).astype(BF16)
    else:
        term_ref[...] = matmul(normed_ref[...], proj_ref[...], (0, 0))

    normed_grad = matmul(proj_ref[...], weight_ref[...], (1, 1))
    standard = standard_ref[...]
    inner = (
        normed_grad
        - jnp.mean(normed_grad, axis=-1, keepdims=True)
        - standard * jnp.mean(normed_grad * standard, axis=-1, keepdims=True)
    )
    token_grad = (cot_ref[...].astype(F32) + inv_std * inner).astype(BF16)
    grad_ref[...] = matmul(onehot, token_grad, (0, 0)).astype(BF16)


def window_call(pos, pixels, weight, split_reps):
    count, channels = pixels.shape[0], pixels.shape[1] // 2
    vmem = pl.BlockSpec(memory_space=pltpu.VMEM)
    outs = [jax.ShapeDtypeStruct((count, channels), BF16)]
    if split_reps:
        outs += [jax.ShapeDtypeStruct((channels, 3 * channels // 2), BF16)] * 2
    else:
        outs += [jax.ShapeDtypeStruct((channels, 3 * channels), F32)]
    flat = (count, channels)
    return pl.pallas_call(
        functools.partial(window_kernel, split_reps),
        out_shape=outs,
        in_specs=[vmem] * 3,
        out_specs=[vmem] * len(outs),
        scratch_shapes=[
            pltpu.VMEM(flat, BF16),
            pltpu.VMEM(flat, F32),
            pltpu.VMEM(flat, BF16),
            pltpu.VMEM(flat, BF16),
            pltpu.VMEM(flat, BF16),
            pltpu.VMEM(flat, BF16),
            pltpu.VMEM((count, 3 * channels), BF16),
        ],
        compiler_params=pltpu.CompilerParams(vmem_limit_bytes=32 * 2**20),
        name="window_grads",
    )(pos, pixels, weight)


def swap_reps(values):
    return lax.ppermute(values, "rep", [(0, 1), (1, 0)])


def reduce_over(values, axis):
    size = lax.axis_size(axis)
    parts = values.reshape(size, values.shape[0] // size, *values.shape[1:])
    parts = lax.all_to_all(parts, axis, split_axis=0, concat_axis=0, tiled=True)
    return jnp.sum(parts.astype(F32), axis=0)


def shards(tokens, qkv_weight, cotangent):
    rep_count = lax.axis_size("rep")
    row_tiles = lax.axis_size("ty")
    col_tiles = lax.axis_size("tx")
    tile_count = row_tiles * col_tiles
    _, tile_height, tile_width, channels = tokens.shape
    stride_rows = row_tiles * tile_height // GRID
    stride_cols = col_tiles * tile_width // GRID
    block_rows = min(tile_height, stride_rows)
    fold_rows = stride_rows // block_rows
    col_groups = tile_width // stride_cols
    outer_rows = tile_height // block_rows
    inner_rows = block_rows // tile_count
    chunk = outer_rows * inner_rows * tile_width
    count = tile_count * chunk

    order = np.arange(count).reshape(
        row_tiles // fold_rows, fold_rows, col_tiles, outer_rows, inner_rows, col_groups, stride_cols
    )
    order = order.transpose(1, 4, 6, 0, 3, 2, 5).reshape(count)
    pos = np.zeros((1, count), np.int32)
    pos[0, order] = np.arange(count)

    def to_send(values):
        values = values.reshape(outer_rows, tile_count, inner_rows * tile_width, channels)
        return values.transpose(1, 0, 2, 3).reshape(tile_count, chunk, channels)

    sent = jnp.concatenate([to_send(tokens), to_send(cotangent)], axis=-1)
    pixels = lax.all_to_all(sent, ("ty", "tx"), split_axis=0, concat_axis=0, tiled=True)
    pixels = pixels.reshape(count, 2 * channels)
    split_reps = rep_count == 2
    outs = window_call(jnp.asarray(pos), pixels, qkv_weight, split_reps)
    spread = outs[0].reshape(tile_count, chunk, channels)

    total = rep_count * tile_count
    if split_reps:
        keep, send = outs[1:]
        half = keep.astype(F32) + swap_reps(send).astype(F32)
        half = half.astype(BF16).reshape(row_tiles, col_tiles, channels // tile_count, -1)
        rows = half.transpose(1, 0, 2, 3).reshape(channels, -1)
        rows = reduce_over(rows, "tx").astype(BF16)
        rows = reduce_over(rows, "ty") / total
        other = swap_reps(rows)
        first = lax.axis_index("rep") == 0
        weight_grad = jnp.concatenate(
            [jnp.where(first, rows, other), jnp.where(first, other, rows)], axis=1
        )
    else:
        weight_grad = lax.psum_scatter(outs[1], ("ty", "tx"), scatter_dimension=0, tiled=True)
        weight_grad = lax.psum(weight_grad, "rep") / total

    returned = lax.all_to_all(spread, ("ty", "tx"), split_axis=0, concat_axis=0, tiled=True)
    returned = returned.reshape(tile_count, outer_rows, inner_rows * tile_width, channels)
    token_grad = returned.transpose(1, 0, 2, 3).reshape(1, tile_height, tile_width, channels)
    return (token_grad, weight_grad)


def solution(mesh):
    placed = (P("rep", "ty", "tx", None), P(), P("rep", "ty", "tx", None))
    return jax.shard_map(
        shards,
        mesh=mesh,
        in_specs=placed,
        out_specs=(P("rep", "ty", "tx", None), P(("ty", "tx"), None)),
        check_vma=False,
    )
```

time: 235 us -> 73.8 us (0.31)
  waiting for transfers between devices: 145 us -> 11 us
  blocking collectives: 0 us -> 47.2 us
  local copies, waits for them, and re-layouts: 34.5 us -> 2.94 us
  starting transfers between devices: 19.4 us -> 3.61 us
  matrix products: 14.8 us -> 0 us
  between operations: 14.3 us -> 0.73 us
  Pallas kernels: 0 us -> 6.85 us
  other arithmetic: 6.14 us -> 1.13 us
    reduce_scatter x1 -> x0, waiting for transfers between devices: 118 us -> none  [shards(): lax.psum_scatter(weight_term, ('ty', 'tx'), scatter_dimension=0, tiled=True)]
    all_to_all x0 -> x3, blocking collectives: none -> 47.2 us  [the longest x2 23.8 us: reduce_over(): parts = lax.all_to_all(parts, axis, split_axis=0, concat_axis=0, tiled=True)]
    psum x1 -> x0, waiting for transfers between devices: 18.8 us -> none  [shards(): weight_grad = lax.psum(partial_rows, 'rep')]
    all_to_all x3 -> x1, starting transfers between devices: 19.3 us -> 3.53 us  [shards(): lax.all_to_all(spread, ('ty', 'tx'), split_axis=0, concat_axis=0, tiled=T...]
    dot_general x7 -> x0, matrix products: 11.6 us -> none  [the longest x1 2.61 us: window_grads(): lax.dot_general(normed, proj_grad, (((0,), (0,)), ((), ())), preferred_el...]
    reshape x10 -> x5, local copies, waits for them, and re-layouts: 12.7 us -> 2.91 us  [the longest x2 2.03 us: to_send(): values.reshape(outer_rows, tile_count, inner_rows * tile_width, channels)]
    pallas_call x0 -> x1, Pallas kernels: none -> 6.85 us  [window_call(): pl.pallas_call(functools.partial(window_kernel, split_reps), out_shape=ou...]
    convert_element_type x7 -> x0, local copies, waits for them, and re-layouts: 5.18 us -> none  [the longest x1 1.45 us: window_grads(): key_grad = jnp.einsum('wnqk,wqne->wkne', score_grad, query_heads, preferr...]
  transfers between devices with their start and end apart: 5 -> 3, of which waited for: 3 -> 2; matrix products, arithmetic and copies ran while one was open for 9% -> 1% of each run, Pallas kernels for 0% -> 0%
where the time goes in v1:
time: 73.8 us; the launch traced here: 73.4 us
  blocking collectives  47.2 us (64%)
  waiting for transfers between devices  11 us (15%)
  Pallas kernels  6.85 us (9%)
  starting transfers between devices  3.61 us (5%)
  local copies, waits for them, and re-layouts  2.94 us (4%)
  other arithmetic  1.13 us (2%)
    all_to_all x2, blocking collectives, reduce_over(): parts = lax.all_to_all(parts, axis, split_axis=0, concat_axis=0, tiled=True)  23.8 us
    all_to_all x1, blocking collectives, shards(): lax.all_to_all(sent, ('ty', 'tx'), split_axis=0, concat_axis=0, tiled=True)  23.4 us
    all_to_all x1, waiting for transfers between devices, shards(): lax.all_to_all(spread, ('ty', 'tx'), split_axis=0, concat_axis=0, tiled=T...  8.71 us
    pallas_call x1, Pallas kernels, window_call(): pl.pallas_call(functools.partial(window_kernel, split_reps), out_shape=ou...  6.85 us
    all_to_all x1, starting transfers between devices, shards(): lax.all_to_all(spread, ('ty', 'tx'), split_axis=0, concat_axis=0, tiled=T...  3.53 us
    ppermute x2, waiting for transfers between devices, swap_reps(): return lax.ppermute(values, 'rep', [(0, 1), (1, 0)])  2.29 us
    reshape x2, local copies, waits for them, and re-layouts, to_send(): values.reshape(outer_rows, tile_count, inner_rows * tile_width, channels)  2.03 us
  transfers between devices with their start and end apart: 3, of which 2 were waited for; matrix products, arithmetic and copies ran while one was open for 1% of the time, Pallas kernels for 0%

profile of v1, /device:TPU:0, one launch (start us, length us, event | category | flops | bytes accessed | tf_op | source)
XLA Modules:
  0.0 73.4 jit_solution(17123361666789002716)
XLA Ops:
  0.6 1.0 %reshape.34 = bf16[2,16,8,512]{3,2,1,0:T(8,128)(2,1)S(1)} reshape(bf16[1,64,4,512]{3,2,1,0:T(4,128)(2,1)} %param.4) | data formatting | bytes 524288 | tf_op jit(solution)/shard_map/reshape | solution.py:181
  1.6 1.0 %reshape.36 = bf16[2,16,8,512]{3,2,1,0:T(8,128)(2,1)S(1)} reshape(bf16[1,64,4,512]{3,2,1,0:T(4,128)(2,1)} %param.6) | data formatting | bytes 524288 | tf_op jit(solution)/shard_map/reshape | solution.py:181
  2.7 0.0 copy-start
  2.7 0.0 copy-start.1
  2.7 0.1 copy_bitcast_fusion.1
  2.8 0.1 pad_maximum_fusion
  2.8 23.4 %all_to_all.20 = bf16[16,16,1024]{2,1,0:T(8,128)(2,1)S(1)} all-to-all(bf16[16,16,1024]{2,1,0:T(8,128)(2,1)S(1)} %pad_maximum_fusion), channel_id=1, replica_groups=mesh['rep'=2,'ty'=4,'tx'=4] {'ty','tx'}, dimensions={0} | all-to-all | bytes 1048576 | tf_op jit(solution)/shard_map/all_to_all | solution.py:185
  26.2 0.0 copy-done
  26.2 0.0 copy-done.1
  26.2 6.9 %window_grads.1 = (bf16[256,512]{1,0:T(8,128)(2,1)}, bf16[512,768]{1,0:T(8,128)(2,1)S(1)}, bf16[512,768]{1,0:T(8,128)(2,1)S(1)}) custom-call(s32[1,256]{1,0:T(1,128)S(1)} %copy-done.1, bf16[256,1024]{1,0:T(8,128)(2,1)S(1)} %bitcast.24, bf16[512,1536]{1,0:T(8,128)(2,1)S(1)} %copy-done), custom_call_target="tpu_custom_call" | custom-call | tf_op jit(solution)/shard_map/window_grads/pallas_call | solution.py:127
  33.1 0.0 collective-permute-start
  33.1 2.3 %collective-permute-done = bf16[512,768]{1,0:T(8,128)(2,1)S(1)} collective-permute-done((bf16[512,768]{1,0:T(8,128)(2,1)S(1)}, bf16[512,768]{1,0:T(8,128)(2,1)S(1)}, u32[]{:S(2)}, u32[]{:S(2)}) %collective-permute-start) | collective-permute-done | bytes 786464 | tf_op jit(solution)/shard_map/ppermute | solution.py:147
  35.3 0.2 add_convert_fusion
  35.6 0.1 copy.16
  35.6 14.3 %all_to_all.21 = bf16[4,128,768]{2,1,0:T(8,128)(2,1)S(1)} all-to-all(bf16[4,128,768]{2,1,0:T(8,128)(2,1)S(1)} %bitcast.25), channel_id=1, replica_groups=mesh['rep'=2,'ty'=4,'tx'=4] {'tx'}, dimensions={0} | all-to-all | bytes 1572864 | tf_op jit(solution)/shard_map/all_to_all | solution.py:153
  49.9 0.1 reduce_sum.21
  50.1 9.5 %all_to_all.22 = bf16[4,32,768]{2,1,0:T(8,128)(2,1)S(1)} all-to-all(bf16[4,32,768]{2,1,0:T(8,128)(2,1)S(1)} %bitcast.27), channel_id=1, replica_groups=mesh['rep'=2,'ty'=4,'tx'=4] {'ty'}, dimensions={0} | all-to-all | bytes 393216 | tf_op jit(solution)/shard_map/all_to_all | solution.py:153
  59.5 3.5 %all-to-all-start.1 = ((bf16[16,16,512]{2,1,0:T(8,128)(2,1)}), bf16[16,16,512]{2,1,0:T(8,128)(2,1)S(1)}, u32[]{:S(2)}, u32[]{:S(2)}) async-start(bf16[16,16,512]{2,1,0:T(8,128)(2,1)} %bitcast.5), calls=%async_computation.1 | async-start | bytes 524288 | tf_op jit(solution)/shard_map/all_to_all | solution.py:208
  63.1 0.1 collective-permute-start.1
  63.2 8.7 %all-to-all-done.1 = bf16[16,16,512]{2,1,0:T(8,128)(2,1)S(1)} async-done(((bf16[16,16,512]{2,1,0:T(8,128)(2,1)}), bf16[16,16,512]{2,1,0:T(8,128)(2,1)S(1)}, u32[]{:S(2)}, u32[]{:S(2)}) %all-to-all-start.1) | async-done | bytes 262176 | tf_op jit(solution)/shard_map/all_to_all | solution.py:208
  71.9 0.8 %reshape.41 = bf16[1,64,4,512]{3,2,1,0:T(4,128)(2,1)} reshape(bf16[2,16,8,512]{3,2,1,0:T(8,128)(2,1)S(1)} %copy_bitcast_fusion) | data formatting | bytes 524288 | tf_op jit(solution)/shard_map/reshape | solution.py:210
  72.7 0.0 collective-permute-done.1
  72.7 0.7 pad_maximum_fusion.1
  (4 shorter events, 0.1 us)
Async XLA Ops:
  2.7 23.5 %copy-start = (bf16[512,1536]{1,0:T(8,128)(2,1)S(1)}, bf16[512,1536]{1,0:T(8,128)(2,1)}, u32[]{:S(2)}) copy-start(bf16[512,1536]{1,0:T(8,128)(2,1)} %weight_ref.1) | copy-start | bytes 4718596
  2.7 23.5 %copy-start.1 = (s32[1,256]{1,0:T(1,128)S(1)}, s32[1,256]{1,0:T(1,128)}, u32[]{:S(2)}) copy-start(s32[1,256]{1,0:T(1,128)} %constant.17.clone.pos_ref) | copy-start | bytes 3076
  33.1 2.3 %collective-permute-start = (bf16[512,768]{1,0:T(8,128)(2,1)S(1)}, bf16[512,768]{1,0:T(8,128)(2,1)S(1)}, u32[]{:S(2)}, u32[]{:S(2)}) collective-permute-start(bf16[512,768]{1,0:T(8,128)(2,1)S(1)} %get-tuple-element.7), channel_id=1, source_target_pairs={{0,16},{16,0},{1,17},{17,1},{2,18},{18,2},{3,19},{19,3},{4,20},{20... | collective-permute-start | bytes 2359304 | tf_op jit(solution)/shard_map/ppermute | solution.py:147
  59.5 12.4 %all-to-all-start.1 = ((bf16[16,16,512]{2,1,0:T(8,128)(2,1)}), bf16[16,16,512]{2,1,0:T(8,128)(2,1)S(1)}, u32[]{:S(2)}, u32[]{:S(2)}) async-start(bf16[16,16,512]{2,1,0:T(8,128)(2,1)} %bitcast.5), calls=%async_computation.1 | async-start | bytes 524288 | tf_op jit(solution)/shard_map/all_to_all | solution.py:208
  63.1 9.6 %collective-permute-start.1 = (f32[32,768]{1,0:T(8,128)S(1)}, f32[32,768]{1,0:T(8,128)S(1)}, u32[]{:S(2)}, u32[]{:S(2)}) collective-permute-start(f32[32,768]{1,0:T(8,128)S(1)} %broadcast_multiply_fusion), channel_id=1, source_target_pairs={{0,16},{16,0},{1,17},{17,1},{2,18},{18,2},{3,19},{19,3},{4,20},{20... | collective-permute-start | bytes 294920 | tf_op jit(solution)/shard_map/ppermute | solution.py:147

commit v2 on v1

--- a/solution.py
+++ b/solution.py
@@ -147,11 +147,14 @@
     return lax.ppermute(values, "rep", [(0, 1), (1, 0)])
 
 
-def reduce_over(values, axis):
+def reduce_over(parts, axis, dim):
     size = lax.axis_size(axis)
-    parts = values.reshape(size, values.shape[0] // size, *values.shape[1:])
-    parts = lax.all_to_all(parts, axis, split_axis=0, concat_axis=0, tiled=True)
-    return jnp.sum(parts.astype(F32), axis=0)
+    me = lax.axis_index(axis)
+    total = lax.dynamic_index_in_dim(parts, me, dim, keepdims=False).astype(F32)
+    for step in range(1, size):
+        part = lax.dynamic_index_in_dim(parts, me ^ step, dim, keepdims=False)
+        total += lax.ppermute(part, axis, [(i, i ^ step) for i in range(size)]).astype(F32)
+    return total
 
 
 def shards(tokens, qkv_weight, cotangent):
@@ -187,15 +190,16 @@
     split_reps = rep_count == 2
     outs = window_call(jnp.asarray(pos), pixels, qkv_weight, split_reps)
     spread = outs[0].reshape(tile_count, chunk, channels)
+    returned = lax.all_to_all(spread, ("ty", "tx"), split_axis=0, concat_axis=0, tiled=True)
 
     total = rep_count * tile_count
     if split_reps:
         keep, send = outs[1:]
         half = keep.astype(F32) + swap_reps(send).astype(F32)
         half = half.astype(BF16).reshape(row_tiles, col_tiles, channels // tile_count, -1)
-        rows = half.transpose(1, 0, 2, 3).reshape(channels, -1)
-        rows = reduce_over(rows, "tx").astype(BF16)
-        rows = reduce_over(rows, "ty") / total
+        rows = reduce_over(half, "tx", 1).astype(BF16)
+        rows, returned = lax.optimization_barrier((rows, returned))
+        rows = reduce_over(rows, "ty", 0) / total
         other = swap_reps(rows)
         first = lax.axis_index("rep") == 0
         weight_grad = jnp.concatenate(
@@ -205,7 +209,6 @@
         weight_grad = lax.psum_scatter(outs[1], ("ty", "tx"), scatter_dimension=0, tiled=True)
         weight_grad = lax.psum(weight_grad, "rep") / total
 
-    returned = lax.all_to_all(spread, ("ty", "tx"), split_axis=0, concat_axis=0, tiled=True)
     returned = returned.reshape(tile_count, outer_rows, inner_rows * tile_width, channels)
     token_grad = returned.transpose(1, 0, 2, 3).reshape(1, tile_height, tile_width, channels)
     return (token_grad, weight_grad)

time: 73.8 us -> 62.4 us (0.85)
  blocking collectives: 47.2 us -> 23.4 us
  starting transfers between devices: 3.61 us -> 12 us
  waiting for transfers between devices: 11 us -> 15.1 us
    all_to_all x2 -> x0, blocking collectives: 23.8 us -> none  [reduce_over(): parts = lax.all_to_all(parts, axis, split_axis=0, concat_axis=0, tiled=True)]
    ppermute x0 -> x6, waiting for transfers between devices: none -> 14.6 us  [reduce_over(): lax.ppermute(part, axis, [(i, i ^ step) for i in range(size)]).astype(F32)]
    all_to_all x1, waiting for transfers between devices: 8.71 us -> 0.01 us  [shards(): lax.all_to_all(spread, ('ty', 'tx'), split_axis=0, concat_axis=0, tiled=T...]
    ppermute x0 -> x6, starting transfers between devices: none -> 8.01 us  [reduce_over(): lax.ppermute(part, axis, [(i, i ^ step) for i in range(size)]).astype(F32)]
    ppermute x2, waiting for transfers between devices: 2.29 us -> 0.49 us  [swap_reps(): return lax.ppermute(values, 'rep', [(0, 1), (1, 0)])]
  transfers between devices with their start and end apart: 3 -> 9, of which waited for: 2 -> 6; matrix products, arithmetic and copies ran while one was open for 1% -> 2% of each run, Pallas kernels for 0% -> 0%
where the time goes in v2:
time: 62.4 us; the launch traced here: 62.1 us
  blocking collectives  23.4 us (38%)
  waiting for transfers between devices  15.1 us (24%)
  starting transfers between devices  12 us (19%)
  Pallas kernels  6.85 us (11%)
  local copies, waits for them, and re-layouts  2.96 us (5%)
  other arithmetic  1.08 us (2%)
  between operations  0.75 us (1%)
    all_to_all x1, blocking collectives, shards(): lax.all_to_all(sent, ('ty', 'tx'), split_axis=0, concat_axis=0, tiled=True)  23.4 us
    ppermute x6, waiting for transfers between devices, reduce_over(): lax.ppermute(part, axis, [(i, i ^ step) for i in range(size)]).astype(F32)  14.6 us
    ppermute x6, starting transfers between devices, reduce_over(): lax.ppermute(part, axis, [(i, i ^ step) for i in range(size)]).astype(F32)  8.01 us
    pallas_call x1, Pallas kernels, window_call(): pl.pallas_call(functools.partial(window_kernel, split_reps), out_shape=ou...  6.85 us
    all_to_all x1, starting transfers between devices, shards(): lax.all_to_all(spread, ('ty', 'tx'), split_axis=0, concat_axis=0, tiled=T...  3.89 us
    reshape x2, local copies, waits for them, and re-layouts, to_send(): values.reshape(outer_rows, tile_count, inner_rows * tile_width, channels)  2.03 us
  transfers between devices with their start and end apart: 9, of which 6 were waited for; matrix products, arithmetic and copies ran while one was open for 2% of the time, Pallas kernels for 0%

profile of v2, /device:TPU:0, one launch (start us, length us, event | category | flops | bytes accessed | tf_op | source)
XLA Modules:
  0.0 62.1 jit_solution(13140761973826928679)
XLA Ops:
  0.6 1.0 %reshape.35 = bf16[2,16,8,512]{3,2,1,0:T(8,128)(2,1)S(1)} reshape(bf16[1,64,4,512]{3,2,1,0:T(4,128)(2,1)} %param.4) | data formatting | bytes 524288 | tf_op jit(solution)/shard_map/reshape | solution.py:184
  1.6 1.0 %reshape.37 = bf16[2,16,8,512]{3,2,1,0:T(8,128)(2,1)S(1)} reshape(bf16[1,64,4,512]{3,2,1,0:T(4,128)(2,1)} %param.6) | data formatting | bytes 524288 | tf_op jit(solution)/shard_map/reshape | solution.py:184
  2.7 0.0 copy-start
  2.7 0.0 copy-start.1
  2.7 0.1 copy_bitcast_fusion.1
  2.8 0.1 pad_maximum_fusion
  2.8 23.4 %all_to_all.10 = bf16[16,16,1024]{2,1,0:T(8,128)(2,1)S(1)} all-to-all(bf16[16,16,1024]{2,1,0:T(8,128)(2,1)S(1)} %pad_maximum_fusion), channel_id=1, replica_groups=mesh['rep'=2,'ty'=4,'tx'=4] {'ty','tx'}, dimensions={0} | all-to-all | bytes 1048576 | tf_op jit(solution)/shard_map/all_to_all | solution.py:188
  26.2 0.0 copy-done
  26.2 0.0 copy-done.1
  26.2 6.9 %window_grads.1 = (bf16[256,512]{1,0:T(8,128)(2,1)}, bf16[512,768]{1,0:T(8,128)(2,1)S(1)}, bf16[512,768]{1,0:T(8,128)(2,1)S(1)}) custom-call(s32[1,256]{1,0:T(1,128)S(1)} %copy-done.1, bf16[256,1024]{1,0:T(8,128)(2,1)S(1)} %bitcast.40, bf16[512,1536]{1,0:T(8,128)(2,1)S(1)} %copy-done), custom_call_target="tpu_custom_call" | custom-call | tf_op jit(solution)/shard_map/window_grads/pallas_call | solution.py:127
  33.1 0.0 collective-permute-start
  33.1 3.9 %all-to-all-start.1 = ((bf16[16,16,512]{2,1,0:T(8,128)(2,1)}), bf16[16,16,512]{2,1,0:T(8,128)(2,1)S(1)}, u32[]{:S(2)}, u32[]{:S(2)}) async-start(bf16[16,16,512]{2,1,0:T(8,128)(2,1)} %bitcast.10), calls=%async_computation.1 | async-start | bytes 524288 | tf_op jit(solution)/shard_map/all_to_all | solution.py:193
  36.9 0.0 collective-permute-done
  37.0 0.2 add_convert_fusion
  37.2 2.9 %collective-permute-start.3 = (bf16[4,32,768]{2,1,0:T(8,128)(2,1)S(1)}, bf16[4,32,768]{2,1,0:T(8,128)(2,1)S(1)}, u32[]{:S(2)}, u32[]{:S(2)}) collective-permute-start(bf16[4,32,768]{2,1,0:T(8,128)(2,1)S(1)} %get-tuple-element.13), channel_id=1, source_target_pairs={{0,3},{1,2},{2,1},{3,0},{4,7},{5,6},{6,5},{7,4},{8,11},{9,10},{10,... | collective-permute-start | bytes 589832 | tf_op jit(solution)/shard_map/ppermute | solution.py:156
  40.1 0.6 collective-permute-start.2
  40.7 0.1 collective-permute-start.1
  40.8 7.9 %collective-permute-done.3 = bf16[4,32,768]{2,1,0:T(8,128)(2,1)S(1)} collective-permute-done((bf16[4,32,768]{2,1,0:T(8,128)(2,1)S(1)}, bf16[4,32,768]{2,1,0:T(8,128)(2,1)S(1)}, u32[]{:S(2)}, u32[]{:S(2)}) %collective-permute-start.3) | collective-permute-done | bytes 196640 | tf_op jit(solution)/shard_map/ppermute | solution.py:156
  48.7 3.0 %collective-permute-done.2 = bf16[4,32,768]{2,1,0:T(8,128)(2,1)S(1)} collective-permute-done((bf16[4,32,768]{2,1,0:T(8,128)(2,1)S(1)}, bf16[4,32,768]{2,1,0:T(8,128)(2,1)S(1)}, u32[]{:S(2)}, u32[]{:S(2)}) %collective-permute-start.2) | collective-permute-done | bytes 196640 | tf_op jit(solution)/shard_map/ppermute | solution.py:156
  51.7 0.1 collective-permute-done.1
  51.7 0.1 fusion.2
  51.9 0.0 all-to-all-done.1
  51.9 3.1 %collective-permute-start.6 = (bf16[32,768]{1,0:T(8,128)(2,1)S(1)}, bf16[32,768]{1,0:T(8,128)(2,1)S(1)}, u32[]{:S(2)}, u32[]{:S(2)}) collective-permute-start(bf16[32,768]{1,0:T(8,128)(2,1)S(1)} %get-tuple-element.18), channel_id=1, source_target_pairs={{0,12},{4,8},{8,4},{12,0},{1,13},{5,9},{9,5},{13,1},{2,14},{6,10},... | collective-permute-start | bytes 147464 | tf_op jit(solution)/shard_map/ppermute | solution.py:156
  55.0 0.0 collective-permute-start.5
  55.0 1.4 %collective-permute-start.4 = (bf16[32,768]{1,0:T(8,128)(2,1)S(1)}, bf16[32,768]{1,0:T(8,128)(2,1)S(1)}, u32[]{:S(2)}, u32[]{:S(2)}) collective-permute-start(bf16[32,768]{1,0:T(8,128)(2,1)S(1)} %get-tuple-element.17), channel_id=1, source_target_pairs={{0,4},{4,0},{8,12},{12,8},{1,5},{5,1},{9,13},{13,9},{2,6},{6,2},{1... | collective-permute-start | bytes 147464 | tf_op jit(solution)/shard_map/ppermute | solution.py:156
  56.3 2.0 %collective-permute-done.6 = bf16[32,768]{1,0:T(8,128)(2,1)S(1)} collective-permute-done((bf16[32,768]{1,0:T(8,128)(2,1)S(1)}, bf16[32,768]{1,0:T(8,128)(2,1)S(1)}, u32[]{:S(2)}, u32[]{:S(2)}) %collective-permute-start.6) | collective-permute-done | bytes 49184 | tf_op jit(solution)/shard_map/ppermute | solution.py:156
  58.3 1.7 %collective-permute-done.5 = bf16[32,768]{1,0:T(8,128)(2,1)S(1)} collective-permute-done((bf16[32,768]{1,0:T(8,128)(2,1)S(1)}, bf16[32,768]{1,0:T(8,128)(2,1)S(1)}, u32[]{:S(2)}, u32[]{:S(2)}) %collective-permute-start.5) | collective-permute-done | bytes 49184 | tf_op jit(solution)/shard_map/ppermute | solution.py:156
  60.0 0.0 collective-permute-done.4
  60.0 0.1 collective-permute-start.7
  60.2 0.8 %reshape.43 = bf16[1,64,4,512]{3,2,1,0:T(4,128)(2,1)} reshape(bf16[2,16,8,512]{3,2,1,0:T(8,128)(2,1)S(1)} %copy_bitcast_fusion) | data formatting | bytes 524288 | tf_op jit(solution)/shard_map/reshape | solution.py:213
  60.9 0.5 collective-permute-done.7
  61.4 0.7 %pad_maximum_fusion.1 = f32[32,1536]{1,0:T(8,128)} fusion(f32[32,768]{1,0:T(8,128)S(1)} %get-tuple-element.16, f32[32,768]{1,0:T(8,128)S(1)} %get-tuple-element.15), kind=kLoop, calls=%fused_computation.9 | loop fusion | flops 49152 | bytes 393216 | tf_op jit(solution)/shard_map/concatenate | solution.py:205
  (5 shorter events, 0.1 us)
Async XLA Ops:
  2.7 23.5 %copy-start = (bf16[512,1536]{1,0:T(8,128)(2,1)S(1)}, bf16[512,1536]{1,0:T(8,128)(2,1)}, u32[]{:S(2)}) copy-start(bf16[512,1536]{1,0:T(8,128)(2,1)} %weight_ref.1) | copy-start | bytes 4718596
  2.7 23.5 %copy-start.1 = (s32[1,256]{1,0:T(1,128)S(1)}, s32[1,256]{1,0:T(1,128)}, u32[]{:S(2)}) copy-start(s32[1,256]{1,0:T(1,128)} %constant.47.clone.pos_ref) | copy-start | bytes 3076
  33.1 3.9 %collective-permute-start = (bf16[512,768]{1,0:T(8,128)(2,1)S(1)}, bf16[512,768]{1,0:T(8,128)(2,1)S(1)}, u32[]{:S(2)}, u32[]{:S(2)}) collective-permute-start(bf16[512,768]{1,0:T(8,128)(2,1)S(1)} %get-tuple-element.8), channel_id=1, source_target_pairs={{0,16},{16,0},{1,17},{17,1},{2,18},{18,2},{3,19},{19,3},{4,20},{20... | collective-permute-start | bytes 2359304 | tf_op jit(solution)/shard_map/ppermute | solution.py:147
  33.1 18.8 %all-to-all-start.1 = ((bf16[16,16,512]{2,1,0:T(8,128)(2,1)}), bf16[16,16,512]{2,1,0:T(8,128)(2,1)S(1)}, u32[]{:S(2)}, u32[]{:S(2)}) async-start(bf16[16,16,512]{2,1,0:T(8,128)(2,1)} %bitcast.10), calls=%async_computation.1 | async-start | bytes 524288 | tf_op jit(solution)/shard_map/all_to_all | solution.py:193
  37.2 11.4 %collective-permute-start.3 = (bf16[4,32,768]{2,1,0:T(8,128)(2,1)S(1)}, bf16[4,32,768]{2,1,0:T(8,128)(2,1)S(1)}, u32[]{:S(2)}, u32[]{:S(2)}) collective-permute-start(bf16[4,32,768]{2,1,0:T(8,128)(2,1)S(1)} %get-tuple-element.13), channel_id=1, source_target_pairs={{0,3},{1,2},{2,1},{3,0},{4,7},{5,6},{6,5},{7,4},{8,11},{9,10},{10,... | collective-permute-start | bytes 589832 | tf_op jit(solution)/shard_map/ppermute | solution.py:156
  40.1 11.6 %collective-permute-start.2 = (bf16[4,32,768]{2,1,0:T(8,128)(2,1)S(1)}, bf16[4,32,768]{2,1,0:T(8,128)(2,1)S(1)}, u32[]{:S(2)}, u32[]{:S(2)}) collective-permute-start(bf16[4,32,768]{2,1,0:T(8,128)(2,1)S(1)} %get-tuple-element.14), channel_id=1, source_target_pairs={{0,2},{1,3},{2,0},{3,1},{4,6},{5,7},{6,4},{7,5},{8,10},{9,11},{10,... | collective-permute-start | bytes 589832 | tf_op jit(solution)/shard_map/ppermute | solution.py:156
  40.7 11.1 %collective-permute-start.1 = (bf16[4,32,768]{2,1,0:T(8,128)(2,1)S(1)}, bf16[4,32,768]{2,1,0:T(8,128)(2,1)S(1)}, u32[]{:S(2)}, u32[]{:S(2)}) collective-permute-start(bf16[4,32,768]{2,1,0:T(8,128)(2,1)S(1)} %get-tuple-element.12), channel_id=1, source_target_pairs={{0,1},{1,0},{2,3},{3,2},{4,5},{5,4},{6,7},{7,6},{8,9},{9,8},{10,11... | collective-permute-start | bytes 589832 | tf_op jit(solution)/shard_map/ppermute | solution.py:156
  51.9 6.4 %collective-permute-start.6 = (bf16[32,768]{1,0:T(8,128)(2,1)S(1)}, bf16[32,768]{1,0:T(8,128)(2,1)S(1)}, u32[]{:S(2)}, u32[]{:S(2)}) collective-permute-start(bf16[32,768]{1,0:T(8,128)(2,1)S(1)} %get-tuple-element.18), channel_id=1, source_target_pairs={{0,12},{4,8},{8,4},{12,0},{1,13},{5,9},{9,5},{13,1},{2,14},{6,10},... | collective-permute-start | bytes 147464 | tf_op jit(solution)/shard_map/ppermute | solution.py:156
  55.0 5.0 %collective-permute-start.5 = (bf16[32,768]{1,0:T(8,128)(2,1)S(1)}, bf16[32,768]{1,0:T(8,128)(2,1)S(1)}, u32[]{:S(2)}, u32[]{:S(2)}) collective-permute-start(bf16[32,768]{1,0:T(8,128)(2,1)S(1)} %get-tuple-element.19), channel_id=1, source_target_pairs={{0,8},{4,12},{8,0},{12,4},{1,9},{5,13},{9,1},{13,5},{2,10},{6,14},... | collective-permute-start | bytes 147464 | tf_op jit(solution)/shard_map/ppermute | solution.py:156
  55.0 5.0 %collective-permute-start.4 = (bf16[32,768]{1,0:T(8,128)(2,1)S(1)}, bf16[32,768]{1,0:T(8,128)(2,1)S(1)}, u32[]{:S(2)}, u32[]{:S(2)}) collective-permute-start(bf16[32,768]{1,0:T(8,128)(2,1)S(1)} %get-tuple-element.17), channel_id=1, source_target_pairs={{0,4},{4,0},{8,12},{12,8},{1,5},{5,1},{9,13},{13,9},{2,6},{6,2},{1... | collective-permute-start | bytes 147464 | tf_op jit(solution)/shard_map/ppermute | solution.py:156
  60.0 1.4 %collective-permute-start.7 = (f32[32,768]{1,0:T(8,128)S(1)}, f32[32,768]{1,0:T(8,128)S(1)}, u32[]{:S(2)}, u32[]{:S(2)}) collective-permute-start(f32[32,768]{1,0:T(8,128)S(1)} %fusion.5), channel_id=1, source_target_pairs={{0,16},{16,0},{1,17},{17,1},{2,18},{18,2},{3,19},{19,3},{4,20},{20... | collective-permute-start | bytes 294920 | tf_op jit(solution)/shard_map/ppermute | solution.py:147

commit v3 on v2

--- a/solution.py
+++ b/solution.py
@@ -14,6 +14,7 @@
 EPS = 1e-05
 LANES = 128
 BLOCK_HEADS = LANES // HEAD_DIM
+GROUP = 8
 
 BF16 = jnp.bfloat16
 F32 = jnp.float32
@@ -68,32 +69,34 @@
     def stack(block):
         return jnp.concatenate([block] * BLOCK_HEADS, axis=0) * mask_low
 
-    for window in range(count // win_tokens):
-        row = slice(window * win_tokens, (window + 1) * win_tokens)
-        for block in range(channels // LANES):
-            col = slice(block * LANES, (block + 1) * LANES)
-            key = key_ref[row, col]
-            queries = stack(query_ref[row, col])
-            cots = stack(cot_ref[row, col])
-            scores = matmul(key, queries, (1, 1))
-            attn_grad = matmul(value_ref[row, col], cots, (1, 1))
+    cells = [
+        (slice(row, row + win_tokens), slice(col, col + LANES))
+        for row in range(0, count, win_tokens)
+        for col in range(0, channels, LANES)
+    ]
+    for first in range(0, len(cells), GROUP):
+        group = cells[first : first + GROUP]
+        raw = []
+        for row, col in group:
+            scores = matmul(key_ref[row, col], stack(query_ref[row, col]), (1, 1))
+            attn_grad = matmul(value_ref[row, col], stack(cot_ref[row, col]), (1, 1))
+            raw.append((scores, attn_grad))
+        low = []
+        for scores, attn_grad in raw:
             exponent = jnp.exp(scores - jnp.max(scores, axis=0, keepdims=True))
             probs = exponent * (1.0 / jnp.sum(exponent, axis=0, keepdims=True))
-            score_grad = (
-                probs * (attn_grad - jnp.sum(probs * attn_grad, axis=0, keepdims=True))
-            ).astype(BF16)
-            value_grad = matmul(probs.astype(BF16), cots, (1, 0))
-            key_grad = matmul(score_grad, queries, (1, 0))
-            spread = matmul(score_grad, key, (0, 0)) * mask
+            score_grad = probs * (attn_grad - jnp.sum(probs * attn_grad, axis=0, keepdims=True))
+            low.append((probs.astype(BF16), score_grad.astype(BF16)))
+        for (row, col), (probs, score_grad) in zip(group, low):
+            value_grad = matmul(probs, stack(cot_ref[row, col]), (1, 0))
+            key_grad = matmul(score_grad, stack(query_ref[row, col]), (1, 0))
+            spread = matmul(score_grad, key_ref[row, col], (0, 0)) * mask
             query_grad = spread[:win_tokens]
             for head in range(1, BLOCK_HEADS):
                 query_grad += spread[head * win_tokens : (head + 1) * win_tokens]
-            base = block * LANES
-            proj_ref[row, base : base + LANES] = (query_grad * scale).astype(BF16)
-            base += channels
-            proj_ref[row, base : base + LANES] = key_grad.astype(BF16)
-            base += channels
-            proj_ref[row, base : base + LANES] = value_grad.astype(BF16)
+            for part, grad in enumerate((query_grad * scale, key_grad, value_grad)):
+                base = part * channels + col.start
+                proj_ref[row, base : base + LANES] = grad.astype(BF16)
 
     if split_reps:
         half = 3 * channels // 2
@@ -198,7 +201,6 @@
         half = keep.astype(F32) + swap_reps(send).astype(F32)
         half = half.astype(BF16).reshape(row_tiles, col_tiles, channels // tile_count, -1)
         rows = reduce_over(half, "tx", 1).astype(BF16)
-        rows, returned = lax.optimization_barrier((rows, returned))
         rows = reduce_over(rows, "ty", 0) / total
         other = swap_reps(rows)
         first = lax.axis_index("rep") == 0

time: 62.4 us -> 56.4 us (0.904)
  waiting for transfers between devices: 15.1 us -> 11.6 us
  Pallas kernels: 6.85 us -> 4.35 us
    ppermute x6, waiting for transfers between devices: 14.6 us -> 8.83 us  [reduce_over(): lax.ppermute(part, axis, [(i, i ^ step) for i in range(size)]).astype(F32)]
    pallas_call x1, Pallas kernels: 6.85 us -> 4.35 us  [window_call(): pl.pallas_call(functools.partial(window_kernel, split_reps), out_shape=ou...]
    ppermute x2, waiting for transfers between devices: 0.49 us -> 2.76 us  [swap_reps(): return lax.ppermute(values, 'rep', [(0, 1), (1, 0)])]
  transfers between devices with their start and end apart: 9 -> 9, of which waited for: 6 -> 7; matrix products, arithmetic and copies ran while one was open for 2% -> 2% of each run, Pallas kernels for 0% -> 0%
where the time goes in v3:
time: 56.4 us; the launch traced here: 56.1 us
  blocking collectives  23.4 us (41%)
  starting transfers between devices  12 us (21%)
  waiting for transfers between devices  11.6 us (21%)
  Pallas kernels  4.35 us (8%)
  local copies, waits for them, and re-layouts  2.96 us (5%)
  other arithmetic  1.08 us (2%)
  between operations  0.74 us (1%)
    all_to_all x1, blocking collectives, shards(): lax.all_to_all(sent, ('ty', 'tx'), split_axis=0, concat_axis=0, tiled=True)  23.4 us
    ppermute x6, waiting for transfers between devices, reduce_over(): lax.ppermute(part, axis, [(i, i ^ step) for i in range(size)]).astype(F32)  8.83 us
    ppermute x6, starting transfers between devices, reduce_over(): lax.ppermute(part, axis, [(i, i ^ step) for i in range(size)]).astype(F32)  8.01 us
    pallas_call x1, Pallas kernels, window_call(): pl.pallas_call(functools.partial(window_kernel, split_reps), out_shape=ou...  4.35 us
    all_to_all x1, starting transfers between devices, shards(): lax.all_to_all(spread, ('ty', 'tx'), split_axis=0, concat_axis=0, tiled=T...  3.89 us
    ppermute x2, waiting for transfers between devices, swap_reps(): return lax.ppermute(values, 'rep', [(0, 1), (1, 0)])  2.76 us
    reshape x2, local copies, waits for them, and re-layouts, to_send(): values.reshape(outer_rows, tile_count, inner_rows * tile_width, channels)  2.03 us
  transfers between devices with their start and end apart: 9, of which 7 were waited for; matrix products, arithmetic and copies ran while one was open for 2% of the time, Pallas kernels for 0%

profile of v3, /device:TPU:0, one launch (start us, length us, event | category | flops | bytes accessed | tf_op | source)
XLA Modules:
  0.0 56.1 jit_solution(2652057153732108880)
XLA Ops:
  0.6 1.0 %reshape.35 = bf16[2,16,8,512]{3,2,1,0:T(8,128)(2,1)S(1)} reshape(bf16[1,64,4,512]{3,2,1,0:T(4,128)(2,1)} %param.4) | data formatting | bytes 524288 | tf_op jit(solution)/shard_map/reshape | solution.py:187
  1.6 1.0 %reshape.37 = bf16[2,16,8,512]{3,2,1,0:T(8,128)(2,1)S(1)} reshape(bf16[1,64,4,512]{3,2,1,0:T(4,128)(2,1)} %param.6) | data formatting | bytes 524288 | tf_op jit(solution)/shard_map/reshape | solution.py:187
  2.7 0.0 copy-start
  2.7 0.0 copy-start.1
  2.7 0.1 copy_bitcast_fusion.1
  2.8 0.1 pad_maximum_fusion
  2.8 23.4 %all_to_all.10 = bf16[16,16,1024]{2,1,0:T(8,128)(2,1)S(1)} all-to-all(bf16[16,16,1024]{2,1,0:T(8,128)(2,1)S(1)} %pad_maximum_fusion), channel_id=1, replica_groups=mesh['rep'=2,'ty'=4,'tx'=4] {'ty','tx'}, dimensions={0} | all-to-all | bytes 1048576 | tf_op jit(solution)/shard_map/all_to_all | solution.py:191
  26.2 0.0 copy-done
  26.2 0.0 copy-done.1
  26.2 4.4 %window_grads.1 = (bf16[256,512]{1,0:T(8,128)(2,1)}, bf16[512,768]{1,0:T(8,128)(2,1)S(1)}, bf16[512,768]{1,0:T(8,128)(2,1)S(1)}) custom-call(s32[1,256]{1,0:T(1,128)S(1)} %copy-done.1, bf16[256,1024]{1,0:T(8,128)(2,1)S(1)} %bitcast.40, bf16[512,1536]{1,0:T(8,128)(2,1)S(1)} %copy-done), custom_call_target="tpu_custom_call" | custom-call | tf_op jit(solution)/shard_map/window_grads/pallas_call | solution.py:130
  30.6 0.0 collective-permute-start
  30.6 2.3 %collective-permute-done = bf16[512,768]{1,0:T(8,128)(2,1)S(1)} collective-permute-done((bf16[512,768]{1,0:T(8,128)(2,1)S(1)}, bf16[512,768]{1,0:T(8,128)(2,1)S(1)}, u32[]{:S(2)}, u32[]{:S(2)}) %collective-permute-start) | collective-permute-done | bytes 786464 | tf_op jit(solution)/shard_map/ppermute | solution.py:150
  32.8 0.2 add_convert_fusion
  33.1 1.0 %collective-permute-start.3 = (bf16[4,32,768]{2,1,0:T(8,128)(2,1)S(1)}, bf16[4,32,768]{2,1,0:T(8,128)(2,1)S(1)}, u32[]{:S(2)}, u32[]{:S(2)}) collective-permute-start(bf16[4,32,768]{2,1,0:T(8,128)(2,1)S(1)} %get-tuple-element.9), channel_id=1, source_target_pairs={{0,3},{1,2},{2,1},{3,0},{4,7},{5,6},{6,5},{7,4},{8,11},{9,10},{10,... | collective-permute-start | bytes 589832 | tf_op jit(solution)/shard_map/ppermute | solution.py:159
  34.1 1.1 %collective-permute-start.2 = (bf16[4,32,768]{2,1,0:T(8,128)(2,1)S(1)}, bf16[4,32,768]{2,1,0:T(8,128)(2,1)S(1)}, u32[]{:S(2)}, u32[]{:S(2)}) collective-permute-start(bf16[4,32,768]{2,1,0:T(8,128)(2,1)S(1)} %get-tuple-element.10), channel_id=1, source_target_pairs={{0,2},{1,3},{2,0},{3,1},{4,6},{5,7},{6,4},{7,5},{8,10},{9,11},{10,... | collective-permute-start | bytes 589832 | tf_op jit(solution)/shard_map/ppermute | solution.py:159
  35.2 1.5 %collective-permute-start.1 = (bf16[4,32,768]{2,1,0:T(8,128)(2,1)S(1)}, bf16[4,32,768]{2,1,0:T(8,128)(2,1)S(1)}, u32[]{:S(2)}, u32[]{:S(2)}) collective-permute-start(bf16[4,32,768]{2,1,0:T(8,128)(2,1)S(1)} %get-tuple-element.8), channel_id=1, source_target_pairs={{0,1},{1,0},{2,3},{3,2},{4,5},{5,4},{6,7},{7,6},{8,9},{9,8},{10,11... | collective-permute-start | bytes 589832 | tf_op jit(solution)/shard_map/ppermute | solution.py:159
  36.6 3.9 %all-to-all-start.1 = ((bf16[16,16,512]{2,1,0:T(8,128)(2,1)}), bf16[16,16,512]{2,1,0:T(8,128)(2,1)S(1)}, u32[]{:S(2)}, u32[]{:S(2)}) async-start(bf16[16,16,512]{2,1,0:T(8,128)(2,1)} %bitcast.5), calls=%async_computation.1 | async-start | bytes 524288 | tf_op jit(solution)/shard_map/all_to_all | solution.py:196
  40.5 1.3 %collective-permute-done.3 = bf16[4,32,768]{2,1,0:T(8,128)(2,1)S(1)} collective-permute-done((bf16[4,32,768]{2,1,0:T(8,128)(2,1)S(1)}, bf16[4,32,768]{2,1,0:T(8,128)(2,1)S(1)}, u32[]{:S(2)}, u32[]{:S(2)}) %collective-permute-start.3) | collective-permute-done | bytes 196640 | tf_op jit(solution)/shard_map/ppermute | solution.py:159
  41.8 4.3 %collective-permute-done.2 = bf16[4,32,768]{2,1,0:T(8,128)(2,1)S(1)} collective-permute-done((bf16[4,32,768]{2,1,0:T(8,128)(2,1)S(1)}, bf16[4,32,768]{2,1,0:T(8,128)(2,1)S(1)}, u32[]{:S(2)}, u32[]{:S(2)}) %collective-permute-start.2) | collective-permute-done | bytes 196640 | tf_op jit(solution)/shard_map/ppermute | solution.py:159
  46.2 0.0 collective-permute-done.1
  46.2 0.1 fusion.2
  46.3 1.8 %collective-permute-start.6 = (bf16[32,768]{1,0:T(8,128)(2,1)S(1)}, bf16[32,768]{1,0:T(8,128)(2,1)S(1)}, u32[]{:S(2)}, u32[]{:S(2)}) collective-permute-start(bf16[32,768]{1,0:T(8,128)(2,1)S(1)} %get-tuple-element.14), channel_id=1, source_target_pairs={{0,12},{4,8},{8,4},{12,0},{1,13},{5,9},{9,5},{13,1},{2,14},{6,10},... | collective-permute-start | bytes 147464 | tf_op jit(solution)/shard_map/ppermute | solution.py:159
  48.1 1.1 %collective-permute-start.5 = (bf16[32,768]{1,0:T(8,128)(2,1)S(1)}, bf16[32,768]{1,0:T(8,128)(2,1)S(1)}, u32[]{:S(2)}, u32[]{:S(2)}) collective-permute-start(bf16[32,768]{1,0:T(8,128)(2,1)S(1)} %get-tuple-element.15), channel_id=1, source_target_pairs={{0,8},{4,12},{8,0},{12,4},{1,9},{5,13},{9,1},{13,5},{2,10},{6,14},... | collective-permute-start | bytes 147464 | tf_op jit(solution)/shard_map/ppermute | solution.py:159
  49.2 1.6 %collective-permute-start.4 = (bf16[32,768]{1,0:T(8,128)(2,1)S(1)}, bf16[32,768]{1,0:T(8,128)(2,1)S(1)}, u32[]{:S(2)}, u32[]{:S(2)}) collective-permute-start(bf16[32,768]{1,0:T(8,128)(2,1)S(1)} %get-tuple-element.13), channel_id=1, source_target_pairs={{0,4},{4,0},{8,12},{12,8},{1,5},{5,1},{9,13},{13,9},{2,6},{6,2},{1... | collective-permute-start | bytes 147464 | tf_op jit(solution)/shard_map/ppermute | solution.py:159
  50.8 1.6 %collective-permute-done.6 = bf16[32,768]{1,0:T(8,128)(2,1)S(1)} collective-permute-done((bf16[32,768]{1,0:T(8,128)(2,1)S(1)}, bf16[32,768]{1,0:T(8,128)(2,1)S(1)}, u32[]{:S(2)}, u32[]{:S(2)}) %collective-permute-start.6) | collective-permute-done | bytes 49184 | tf_op jit(solution)/shard_map/ppermute | solution.py:159
  52.4 1.5 %collective-permute-done.5 = bf16[32,768]{1,0:T(8,128)(2,1)S(1)} collective-permute-done((bf16[32,768]{1,0:T(8,128)(2,1)S(1)}, bf16[32,768]{1,0:T(8,128)(2,1)S(1)}, u32[]{:S(2)}, u32[]{:S(2)}) %collective-permute-start.5) | collective-permute-done | bytes 49184 | tf_op jit(solution)/shard_map/ppermute | solution.py:159
  53.9 0.1 collective-permute-done.4
  54.0 0.1 collective-permute-start.7
  54.1 0.0 all-to-all-done.1
  54.1 0.8 %reshape.42 = bf16[1,64,4,512]{3,2,1,0:T(4,128)(2,1)} reshape(bf16[2,16,8,512]{3,2,1,0:T(8,128)(2,1)S(1)} %copy_bitcast_fusion) | data formatting | bytes 524288 | tf_op jit(solution)/shard_map/reshape | solution.py:215
  54.9 0.5 collective-permute-done.7
  55.4 0.7 %pad_maximum_fusion.1 = f32[32,1536]{1,0:T(8,128)} fusion(f32[32,768]{1,0:T(8,128)S(1)} %get-tuple-element.12, f32[32,768]{1,0:T(8,128)S(1)} %get-tuple-element.11), kind=kLoop, calls=%fused_computation.9 | loop fusion | flops 49152 | bytes 393216 | tf_op jit(solution)/shard_map/concatenate | solution.py:207
  (5 shorter events, 0.1 us)
Async XLA Ops:
  2.7 23.5 %copy-start = (bf16[512,1536]{1,0:T(8,128)(2,1)S(1)}, bf16[512,1536]{1,0:T(8,128)(2,1)}, u32[]{:S(2)}) copy-start(bf16[512,1536]{1,0:T(8,128)(2,1)} %weight_ref.1) | copy-start | bytes 4718596
  2.7 23.5 %copy-start.1 = (s32[1,256]{1,0:T(1,128)S(1)}, s32[1,256]{1,0:T(1,128)}, u32[]{:S(2)}) copy-start(s32[1,256]{1,0:T(1,128)} %constant.47.clone.pos_ref) | copy-start | bytes 3076
  30.6 2.3 %collective-permute-start = (bf16[512,768]{1,0:T(8,128)(2,1)S(1)}, bf16[512,768]{1,0:T(8,128)(2,1)S(1)}, u32[]{:S(2)}, u32[]{:S(2)}) collective-permute-start(bf16[512,768]{1,0:T(8,128)(2,1)S(1)} %get-tuple-element.7), channel_id=1, source_target_pairs={{0,16},{16,0},{1,17},{17,1},{2,18},{18,2},{3,19},{19,3},{4,20},{20... | collective-permute-start | bytes 2359304 | tf_op jit(solution)/shard_map/ppermute | solution.py:150
  33.1 8.8 %collective-permute-start.3 = (bf16[4,32,768]{2,1,0:T(8,128)(2,1)S(1)}, bf16[4,32,768]{2,1,0:T(8,128)(2,1)S(1)}, u32[]{:S(2)}, u32[]{:S(2)}) collective-permute-start(bf16[4,32,768]{2,1,0:T(8,128)(2,1)S(1)} %get-tuple-element.9), channel_id=1, source_target_pairs={{0,3},{1,2},{2,1},{3,0},{4,7},{5,6},{6,5},{7,4},{8,11},{9,10},{10,... | collective-permute-start | bytes 589832 | tf_op jit(solution)/shard_map/ppermute | solution.py:159
  34.1 12.1 %collective-permute-start.2 = (bf16[4,32,768]{2,1,0:T(8,128)(2,1)S(1)}, bf16[4,32,768]{2,1,0:T(8,128)(2,1)S(1)}, u32[]{:S(2)}, u32[]{:S(2)}) collective-permute-start(bf16[4,32,768]{2,1,0:T(8,128)(2,1)S(1)} %get-tuple-element.10), channel_id=1, source_target_pairs={{0,2},{1,3},{2,0},{3,1},{4,6},{5,7},{6,4},{7,5},{8,10},{9,11},{10,... | collective-permute-start | bytes 589832 | tf_op jit(solution)/shard_map/ppermute | solution.py:159
  35.2 11.0 %collective-permute-start.1 = (bf16[4,32,768]{2,1,0:T(8,128)(2,1)S(1)}, bf16[4,32,768]{2,1,0:T(8,128)(2,1)S(1)}, u32[]{:S(2)}, u32[]{:S(2)}) collective-permute-start(bf16[4,32,768]{2,1,0:T(8,128)(2,1)S(1)} %get-tuple-element.8), channel_id=1, source_target_pairs={{0,1},{1,0},{2,3},{3,2},{4,5},{5,4},{6,7},{7,6},{8,9},{9,8},{10,11... | collective-permute-start | bytes 589832 | tf_op jit(solution)/shard_map/ppermute | solution.py:159
  36.6 17.4 %all-to-all-start.1 = ((bf16[16,16,512]{2,1,0:T(8,128)(2,1)}), bf16[16,16,512]{2,1,0:T(8,128)(2,1)S(1)}, u32[]{:S(2)}, u32[]{:S(2)}) async-start(bf16[16,16,512]{2,1,0:T(8,128)(2,1)} %bitcast.5), calls=%async_computation.1 | async-start | bytes 524288 | tf_op jit(solution)/shard_map/all_to_all | solution.py:196
  46.3 6.1 %collective-permute-start.6 = (bf16[32,768]{1,0:T(8,128)(2,1)S(1)}, bf16[32,768]{1,0:T(8,128)(2,1)S(1)}, u32[]{:S(2)}, u32[]{:S(2)}) collective-permute-start(bf16[32,768]{1,0:T(8,128)(2,1)S(1)} %get-tuple-element.14), channel_id=1, source_target_pairs={{0,12},{4,8},{8,4},{12,0},{1,13},{5,9},{9,5},{13,1},{2,14},{6,10},... | collective-permute-start | bytes 147464 | tf_op jit(solution)/shard_map/ppermute | solution.py:159
  48.1 5.8 %collective-permute-start.5 = (bf16[32,768]{1,0:T(8,128)(2,1)S(1)}, bf16[32,768]{1,0:T(8,128)(2,1)S(1)}, u32[]{:S(2)}, u32[]{:S(2)}) collective-permute-start(bf16[32,768]{1,0:T(8,128)(2,1)S(1)} %get-tuple-element.15), channel_id=1, source_target_pairs={{0,8},{4,12},{8,0},{12,4},{1,9},{5,13},{9,1},{13,5},{2,10},{6,14},... | collective-permute-start | bytes 147464 | tf_op jit(solution)/shard_map/ppermute | solution.py:159
  49.2 4.8 %collective-permute-start.4 = (bf16[32,768]{1,0:T(8,128)(2,1)S(1)}, bf16[32,768]{1,0:T(8,128)(2,1)S(1)}, u32[]{:S(2)}, u32[]{:S(2)}) collective-permute-start(bf16[32,768]{1,0:T(8,128)(2,1)S(1)} %get-tuple-element.13), channel_id=1, source_target_pairs={{0,4},{4,0},{8,12},{12,8},{1,5},{5,1},{9,13},{13,9},{2,6},{6,2},{1... | collective-permute-start | bytes 147464 | tf_op jit(solution)/shard_map/ppermute | solution.py:159
  54.0 1.4 %collective-permute-start.7 = (f32[32,768]{1,0:T(8,128)S(1)}, f32[32,768]{1,0:T(8,128)S(1)}, u32[]{:S(2)}, u32[]{:S(2)}) collective-permute-start(f32[32,768]{1,0:T(8,128)S(1)} %fusion.5), channel_id=1, source_target_pairs={{0,16},{16,0},{1,17},{17,1},{2,18},{18,2},{3,19},{19,3},{4,20},{20... | collective-permute-start | bytes 294920 | tf_op jit(solution)/shard_map/ppermute | solution.py:150

commit v4 on v3

v4 whole, which is shorter than its diff:
```python
import functools

import jax
import jax.numpy as jnp
import numpy as np
from jax import lax
from jax.experimental import pallas as pl
from jax.experimental.pallas import tpu as pltpu
from jax.sharding import PartitionSpec as P

HEADS = 16
HEAD_DIM = 32
GRID = 8
EPS = 1e-05
LANES = 128
BLOCK_HEADS = LANES // HEAD_DIM
GROUP = 8

BF16 = jnp.bfloat16
F32 = jnp.float32


def matmul(a, b, contract):
    return lax.dot_general(a, b, ((contract[:1], contract[1:]), ((), ())), preferred_element_type=F32)


def normalize(pixels):
    center = pixels - jnp.mean(pixels, axis=-1, keepdims=True)
    inv_std = lax.rsqrt(jnp.mean(center * center, axis=-1, keepdims=True) + EPS)
    return center * inv_std, inv_std


def vmem_call(kernel, outs, name, *args, scratch=(), mib=8, remote=()):
    vmem = pl.BlockSpec(memory_space=pltpu.VMEM)
    hbm = pl.BlockSpec(memory_space=pltpu.HBM)
    return pl.pallas_call(
        kernel,
        out_shape=outs,
        in_specs=[hbm if index in remote else vmem for index in range(len(args))],
        out_specs=[vmem] * len(outs),
        scratch_shapes=scratch,
        compiler_params=pltpu.CompilerParams(vmem_limit_bytes=mib * 2**20),
        name=name,
    )(*args)


def pack_kernel(shape, tokens_ref, cot_ref, sent_ref, tokens_buf, cot_buf, sems):
    outer, tiles, size = shape
    channels = sent_ref.shape[2] // 2
    height = tokens_buf.shape[0] // outer
    copies = []
    for index in range(outer):
        rows = pl.ds(index * height, height)
        for part, (ref, buf) in enumerate(((tokens_ref, tokens_buf), (cot_ref, cot_buf))):
            copy = pltpu.make_async_copy(ref.at[rows], buf.at[rows], sems.at[part, index])
            copy.start()
            copies.append(copy)
    for index in range(outer):
        rows = slice(index * height, (index + 1) * height)
        out = slice(index * size, (index + 1) * size)
        copies[2 * index].wait()
        pixels = tokens_buf[rows].reshape(tiles * size, channels).astype(F32)
        normed = normalize(pixels)[0].astype(BF16)
        sent_ref[:, out, :channels] = normed.reshape(tiles, size, channels)
        copies[2 * index + 1].wait()
        sent_ref[:, out, channels:] = cot_buf[rows].reshape(tiles, size, channels)


def unpack_kernel(shape, returned_ref, tokens_ref, cot_ref, grad_ref):
    height, width, channels = tokens_ref.shape
    outer, _, size = shape
    flat = (height * width, channels)
    standard, inv_std = normalize(tokens_ref[...].reshape(flat).astype(F32))
    normed_grad = jnp.concatenate(
        [
            returned_ref[:, index * size : (index + 1) * size].reshape(-1, channels)
            for index in range(outer)
        ],
        axis=0,
    ).astype(F32)
    inner = (
        normed_grad
        - jnp.mean(normed_grad, axis=-1, keepdims=True)
        - standard * jnp.mean(normed_grad * standard, axis=-1, keepdims=True)
    )
    token_grad = cot_ref[...].reshape(flat).astype(F32) + inv_std * inner
    grad_ref[...] = token_grad.astype(BF16).reshape(height, width, channels)


def window_order(pos_ref):
    count = pos_ref.shape[1]
    rows = lax.broadcasted_iota(jnp.int32, (count, count), 0)
    return jnp.where(rows == pos_ref[...], 1.0, 0.0).astype(BF16)


def weight_term(normed_ref, proj_ref, side):
    half = proj_ref.shape[1] // 2
    start = pl.multiple_of(side * half, LANES)
    return matmul(normed_ref[...], proj_ref[:, pl.ds(start, half)], (0, 0))


def window_kernel(
    split_reps,
    pos_ref,
    pixels_ref,
    weight_ref,
    proj_ref,
    normed_ref,
    term_ref,
    cot_ref,
    query_ref,
    key_ref,
    value_ref,
):
    count, channels = cot_ref.shape
    win_tokens = GRID * GRID
    scale = HEAD_DIM**-0.5

    onehot = window_order(pos_ref)
    normed = matmul(onehot, pixels_ref[:, :channels], (1, 0)).astype(BF16)
    normed_ref[...] = normed
    cot_ref[...] = matmul(onehot, pixels_ref[:, channels:], (1, 0)).astype(BF16)

    query_ref[...] = (matmul(normed, weight_ref[:, :channels], (1, 0)) * scale).astype(BF16)
    key_ref[...] = matmul(normed, weight_ref[:, channels : 2 * channels], (1, 0)).astype(BF16)
    value_ref[...] = matmul(normed, weight_ref[:, 2 * channels :], (1, 0)).astype(BF16)

    stack_shape = (BLOCK_HEADS * win_tokens, LANES)
    own = lax.broadcasted_iota(jnp.int32, stack_shape, 0) // win_tokens == (
        lax.broadcasted_iota(jnp.int32, stack_shape, 1) // HEAD_DIM
    )
    mask = jnp.where(own, 1.0, 0.0)
    mask_low = mask.astype(BF16)

    def stack(block):
        return jnp.concatenate([block] * BLOCK_HEADS, axis=0) * mask_low

    cells = [
        (slice(row, row + win_tokens), slice(col, col + LANES))
        for row in range(0, count, win_tokens)
        for col in range(0, channels, LANES)
    ]
    for first in range(0, len(cells), GROUP):
        group = cells[first : first + GROUP]
        raw = []
        for row, col in group:
            scores = matmul(key_ref[row, col], stack(query_ref[row, col]), (1, 1))
            attn_grad = matmul(value_ref[row, col], stack(cot_ref[row, col]), (1, 1))
            raw.append((scores, attn_grad))
        low = []
        for scores, attn_grad in raw:
            exponent = jnp.exp(scores - jnp.max(scores, axis=0, keepdims=True))
            probs = exponent * (1.0 / jnp.sum(exponent, axis=0, keepdims=True))
            score_grad = probs * (attn_grad - jnp.sum(probs * attn_grad, axis=0, keepdims=True))
            low.append((probs.astype(BF16), score_grad.astype(BF16)))
        for (row, col), (probs, score_grad) in zip(group, low):
            value_grad = matmul(probs, stack(cot_ref[row, col]), (1, 0))
            key_grad = matmul(score_grad, stack(query_ref[row, col]), (1, 0))
            spread = matmul(score_grad, key_ref[row, col], (0, 0)) * mask
            query_grad = spread[:win_tokens]
            for head in range(1, BLOCK_HEADS):
                query_grad += spread[head * win_tokens : (head + 1) * win_tokens]
            for part, grad in enumerate((query_grad * scale, key_grad, value_grad)):
                base = part * channels + col.start
                proj_ref[row, base : base + LANES] = grad.astype(BF16)

    if split_reps:
        term_ref[...] = weight_term(normed_ref, proj_ref, 1 - lax.axis_index("rep")).astype(BF16)
    else:
        term_ref[...] = matmul(normed_ref[...], proj_ref[...], (0, 0))


def back_kernel(split_reps, pos_ref, proj_ref, normed_ref, weight_ref, grad_ref, *keep_refs):
    if split_reps:
        keep_refs[0][...] = weight_term(normed_ref, proj_ref, lax.axis_index("rep")).astype(BF16)
    normed_grad = matmul(proj_ref[...], weight_ref[...], (1, 1)).astype(BF16)
    grad_ref[...] = matmul(window_order(pos_ref), normed_grad, (0, 0)).astype(BF16)


def swap_reps(values):
    return lax.ppermute(values, "rep", [(0, 1), (1, 0)])


def split_kernel(axis, keep_ref, got_ref, *part_refs):
    me = lax.axis_index(axis)
    for step, ref in enumerate(part_refs):
        ref[...] = (keep_ref[:, me ^ step].astype(F32) + got_ref[:, me ^ step].astype(F32)).astype(BF16)


def exchange(parts, axis):
    size = len(parts)
    total = parts[0].astype(F32)
    for step in range(1, size):
        total += lax.ppermute(parts[step], axis, [(i, i ^ step) for i in range(size)]).astype(F32)
    return total


def reduce_over(parts, axis, dim):
    size = lax.axis_size(axis)
    me = lax.axis_index(axis)
    total = lax.dynamic_index_in_dim(parts, me, dim, keepdims=False).astype(F32)
    for step in reversed(range(1, size)):
        part = lax.dynamic_index_in_dim(parts, me ^ step, dim, keepdims=False)
        total += lax.ppermute(part, axis, [(i, i ^ step) for i in range(size)]).astype(F32)
    return total


def shards(tokens, qkv_weight, cotangent):
    rep_count = lax.axis_size("rep")
    row_tiles = lax.axis_size("ty")
    col_tiles = lax.axis_size("tx")
    tile_count = row_tiles * col_tiles
    _, tile_height, tile_width, channels = tokens.shape
    stride_rows = row_tiles * tile_height // GRID
    stride_cols = col_tiles * tile_width // GRID
    block_rows = min(tile_height, stride_rows)
    fold_rows = stride_rows // block_rows
    col_groups = tile_width // stride_cols
    outer_rows = tile_height // block_rows
    inner_rows = block_rows // tile_count
    chunk = outer_rows * inner_rows * tile_width
    count = tile_count * chunk

    order = np.arange(count).reshape(
        row_tiles // fold_rows, fold_rows, col_tiles, outer_rows, inner_rows, col_groups, stride_cols
    )
    order = order.transpose(1, 4, 6, 0, 3, 2, 5).reshape(count)
    pos = np.zeros((1, count), np.int32)
    pos[0, order] = np.arange(count)

    local = (tile_height, tile_width, channels)
    split_shape = (outer_rows, tile_count, inner_rows * tile_width)
    tokens, cotangent = tokens.reshape(local), cotangent.reshape(local)
    (sent,) = vmem_call(
        functools.partial(pack_kernel, split_shape),
        [jax.ShapeDtypeStruct((tile_count, chunk, 2 * channels), BF16)],
        "pack",
        pltpu.with_memory_space_constraint(tokens, pltpu.HBM),
        pltpu.with_memory_space_constraint(cotangent, pltpu.HBM),
        scratch=[
            pltpu.VMEM(local, BF16),
            pltpu.VMEM(local, BF16),
            pltpu.SemaphoreType.DMA((2, outer_rows)),
        ],
        remote=(0, 1),
    )
    pixels = lax.all_to_all(sent, ("ty", "tx"), split_axis=0, concat_axis=0, tiled=True)
    pixels = pixels.reshape(count, 2 * channels)

    split_reps = rep_count == 2
    flat = jax.ShapeDtypeStruct((count, channels), BF16)
    term = jax.ShapeDtypeStruct((channels, 3 * channels // 2), BF16)
    whole = jax.ShapeDtypeStruct((channels, 3 * channels), F32)
    proj_grad, normed, send = vmem_call(
        functools.partial(window_kernel, split_reps),
        [
            jax.ShapeDtypeStruct((count, 3 * channels), BF16),
            flat,
            term if split_reps else whole,
        ],
        "window_grads",
        jnp.asarray(pos),
        pixels,
        qkv_weight,
        scratch=[pltpu.VMEM((count, channels), BF16)] * 4,
        mib=16,
    )
    normed_grad, *keep = vmem_call(
        functools.partial(back_kernel, split_reps),
        [flat] + [term] * split_reps,
        "normed_grad",
        jnp.asarray(pos),
        proj_grad,
        normed,
        qkv_weight,
    )
    spread = normed_grad.reshape(tile_count, chunk, channels)
    returned = lax.all_to_all(spread, ("ty", "tx"), split_axis=0, concat_axis=0, tiled=True)

    total = rep_count * tile_count
    if split_reps:
        shape = (row_tiles, col_tiles, channels // tile_count, 3 * channels // 2)
        part = jax.ShapeDtypeStruct((shape[0], *shape[2:]), BF16)
        parts = vmem_call(
            functools.partial(split_kernel, "tx"),
            [part] * col_tiles,
            "split_tx",
            keep[0].reshape(shape),
            swap_reps(send).reshape(shape),
        )
        rows = exchange(parts, "tx").astype(BF16)
        rows = reduce_over(rows, "ty", 0) / total
        other = swap_reps(rows)
        first = lax.axis_index("rep") == 0
        weight_grad = jnp.concatenate(
            [jnp.where(first, rows, other), jnp.where(first, other, rows)], axis=1
        )
    else:
        weight_grad = lax.psum_scatter(send, ("ty", "tx"), scatter_dimension=0, tiled=True)
        weight_grad = lax.psum(weight_grad, "rep") / total

    (token_grad,) = vmem_call(
        functools.partial(unpack_kernel, split_shape),
        [jax.ShapeDtypeStruct(local, BF16)],
        "token_grad",
        returned,
        tokens,
        cotangent,
    )
    token_grad = token_grad.reshape(1, *local)
    return (token_grad, weight_grad)


def solution(mesh):
    placed = (P("rep", "ty", "tx", None), P(), P("rep", "ty", "tx", None))
    return jax.shard_map(
        shards,
        mesh=mesh,
        in_specs=placed,
        out_specs=(P("rep", "ty", "tx", None), P(("ty", "tx"), None)),
        check_vma=False,
    )
```

time: 56.4 us -> 52.9 us (0.938)
  waiting for transfers between devices: 11.6 us -> 8.62 us
  local copies, waits for them, and re-layouts: 2.96 us -> 0.04 us
  Pallas kernels: 4.35 us -> 7.04 us
    ppermute x6 -> x3, waiting for transfers between devices: 8.83 us -> 2.89 us  [reduce_over(): lax.ppermute(part, axis, [(i, i ^ step) for i in range(size)]).astype(F32)]
    ppermute x0 -> x3, waiting for transfers between devices: none -> 5.16 us  [exchange(): lax.ppermute(parts[step], axis, [(i, i ^ step) for i in range(size)])]
    ppermute x6 -> x3, starting transfers between devices: 8.01 us -> 4.45 us  [reduce_over(): lax.ppermute(part, axis, [(i, i ^ step) for i in range(size)]).astype(F32)]
    ppermute x0 -> x3, starting transfers between devices: none -> 3.55 us  [exchange(): lax.ppermute(parts[step], axis, [(i, i ^ step) for i in range(size)])]
    reshape x4 -> x0, local copies, waits for them, and re-layouts: 2.85 us -> none  [the longest x2 2.03 us: to_send(): values.reshape(outer_rows, tile_count, inner_rows * tile_width, channels)]
    pallas_call x1 -> x5, Pallas kernels: 4.35 us -> 7.04 us  [vmem_call(): pl.pallas_call(kernel, out_shape=outs, in_specs=[hbm if index in remote e...]
    ppermute x2, waiting for transfers between devices: 2.76 us -> 0.56 us  [swap_reps(): return lax.ppermute(values, 'rep', [(0, 1), (1, 0)])]
  transfers between devices with their start and end apart: 9 -> 9, of which waited for: 7 -> 8; matrix products, arithmetic and copies ran while one was open for 2% -> 0% of each run, Pallas kernels for 0% -> 6%
where the time goes in v4:
time: 52.9 us; the launch traced here: 52.6 us
  blocking collectives  23.2 us (44%)
  starting transfers between devices  12 us (23%)
  waiting for transfers between devices  8.62 us (16%)
  Pallas kernels  7.04 us (13%)
  other arithmetic  0.84 us (2%)
  between operations  0.74 us (1%)
    all_to_all x1, blocking collectives, shards(): lax.all_to_all(sent, ('ty', 'tx'), split_axis=0, concat_axis=0, tiled=True)  23.2 us
    pallas_call x5, Pallas kernels, vmem_call(): pl.pallas_call(kernel, out_shape=outs, in_specs=[hbm if index in remote e...  7.04 us
    ppermute x3, waiting for transfers between devices, exchange(): lax.ppermute(parts[step], axis, [(i, i ^ step) for i in range(size)])  5.16 us
    ppermute x3, starting transfers between devices, reduce_over(): lax.ppermute(part, axis, [(i, i ^ step) for i in range(size)]).astype(F32)  4.45 us
    all_to_all x1, starting transfers between devices, shards(): lax.all_to_all(spread, ('ty', 'tx'), split_axis=0, concat_axis=0, tiled=T...  3.9 us
    ppermute x3, starting transfers between devices, exchange(): lax.ppermute(parts[step], axis, [(i, i ^ step) for i in range(size)])  3.55 us
    ppermute x3, waiting for transfers between devices, reduce_over(): lax.ppermute(part, axis, [(i, i ^ step) for i in range(size)]).astype(F32)  2.89 us
  transfers between devices with their start and end apart: 9, of which 8 were waited for; matrix products, arithmetic and copies ran while one was open for 0% of the time, Pallas kernels for 6%

profile of v4, /device:TPU:0, one launch (start us, length us, event | category | flops | bytes accessed | tf_op | source)
XLA Modules:
  0.0 52.6 jit_solution(17474804365316876871)
XLA Ops:
  0.6 0.0 copy-start.3
  0.6 0.0 copy-start
  0.7 1.5 %pack.1 = bf16[16,16,1024]{2,1,0:T(8,128)(2,1)S(1)} custom-call(bf16[64,4,512]{2,1,0:T(4,128)(2,1)} %bitcast.17, bf16[64,4,512]{2,1,0:T(4,128)(2,1)} %bitcast.19), custom_call_target="tpu_custom_call" | custom-call | tf_op jit(solution)/shard_map/pack/pallas_call | solution.py:36
  2.2 23.2 %all_to_all.10 = bf16[16,16,1024]{2,1,0:T(8,128)(2,1)S(1)} all-to-all(bf16[16,16,1024]{2,1,0:T(8,128)(2,1)S(1)} %pack.1), channel_id=1, replica_groups=mesh['rep'=2,'ty'=4,'tx'=4] {'ty','tx'}, dimensions={0} | all-to-all | bytes 1048576 | tf_op jit(solution)/shard_map/all_to_all | solution.py:247
  25.4 0.0 copy-done.3
  25.4 0.0 copy-done
  25.4 2.4 %window_grads.1 = (bf16[256,1536]{1,0:T(8,128)(2,1)S(1)}, bf16[256,512]{1,0:T(8,128)(2,1)S(1)}, bf16[512,768]{1,0:T(8,128)(2,1)S(1)}) custom-call(s32[1,256]{1,0:T(1,128)S(1)} %copy-done.3, bf16[256,1024]{1,0:T(8,128)(2,1)S(1)} %bitcast.16, bf16[512,1536]{1,0:T(8,128)(2,1)S(1)} %copy-done), custom_call_target="tpu_custom_call" | custom-call | tf_op jit(solution)/shard_map/window_grads/pallas_call | solution.py:36
  27.8 0.1 collective-permute-start
  27.9 1.8 %normed_grad.1 = (bf16[256,512]{1,0:T(8,128)(2,1)}, bf16[512,768]{1,0:T(8,128)(2,1)S(1)}) custom-call(s32[1,256]{1,0:T(1,128)S(1)} %copy-done.3, bf16[256,1536]{1,0:T(8,128)(2,1)S(1)} %get-tuple-element.11.proj_ref, bf16[256,512]{1,0:T(8,128)(2,1)S(1)} %get-tuple-element.12.normed_ref, bf16[512,1536]{1,0:T(8,128)(2,1)S(1)} %copy-done), custom_call_target="tpu_custom_call" | custom-call | tf_op jit(solution)/shard_map/normed_grad/pallas_call | solution.py:36
  29.7 0.5 collective-permute-done
  30.2 0.2 split_tx.1
  30.4 0.6 %collective-permute-start.1 = (bf16[4,32,768]{2,1,0:T(8,128)(2,1)S(1)}, bf16[4,32,768]{2,1,0:T(8,128)(2,1)S(1)}, u32[]{:S(2)}, u32[]{:S(2)}) collective-permute-start(bf16[4,32,768]{2,1,0:T(8,128)(2,1)S(1)} %get-tuple-element.17), channel_id=1, source_target_pairs={{0,1},{1,0},{2,3},{3,2},{4,5},{5,4},{6,7},{7,6},{8,9},{9,8},{10,11... | collective-permute-start | bytes 589832 | tf_op jit(solution)/shard_map/ppermute | solution.py:194
  31.0 0.9 %collective-permute-start.2 = (bf16[4,32,768]{2,1,0:T(8,128)(2,1)S(1)}, bf16[4,32,768]{2,1,0:T(8,128)(2,1)S(1)}, u32[]{:S(2)}, u32[]{:S(2)}) collective-permute-start(bf16[4,32,768]{2,1,0:T(8,128)(2,1)S(1)} %get-tuple-element.18), channel_id=1, source_target_pairs={{0,2},{1,3},{2,0},{3,1},{4,6},{5,7},{6,4},{7,5},{8,10},{9,11},{10,... | collective-permute-start | bytes 589832 | tf_op jit(solution)/shard_map/ppermute | solution.py:194
  31.9 2.0 %collective-permute-start.3 = (bf16[4,32,768]{2,1,0:T(8,128)(2,1)S(1)}, bf16[4,32,768]{2,1,0:T(8,128)(2,1)S(1)}, u32[]{:S(2)}, u32[]{:S(2)}) collective-permute-start(bf16[4,32,768]{2,1,0:T(8,128)(2,1)S(1)} %get-tuple-element.19), channel_id=1, source_target_pairs={{0,3},{1,2},{2,1},{3,0},{4,7},{5,6},{6,5},{7,4},{8,11},{9,10},{10,... | collective-permute-start | bytes 589832 | tf_op jit(solution)/shard_map/ppermute | solution.py:194
  33.9 3.9 %all-to-all-start.1 = ((bf16[16,16,512]{2,1,0:T(8,128)(2,1)}), bf16[16,16,512]{2,1,0:T(8,128)(2,1)S(1)}, u32[]{:S(2)}, u32[]{:S(2)}) async-start(bf16[16,16,512]{2,1,0:T(8,128)(2,1)} %bitcast.3), calls=%async_computation.1 | async-start | bytes 524288 | tf_op jit(solution)/shard_map/all_to_all | solution.py:278
  37.8 0.4 collective-permute-done.1
  38.2 0.2 collective-permute-done.2
  38.4 4.6 %collective-permute-done.3 = bf16[4,32,768]{2,1,0:T(8,128)(2,1)S(1)} collective-permute-done((bf16[4,32,768]{2,1,0:T(8,128)(2,1)S(1)}, bf16[4,32,768]{2,1,0:T(8,128)(2,1)S(1)}, u32[]{:S(2)}, u32[]{:S(2)}) %collective-permute-start.3) | collective-permute-done | bytes 196640 | tf_op jit(solution)/shard_map/ppermute | solution.py:194
  43.0 0.1 add_convert_fusion
  43.1 2.2 %collective-permute-start.4 = (bf16[32,768]{1,0:T(8,128)(2,1)S(1)}, bf16[32,768]{1,0:T(8,128)(2,1)S(1)}, u32[]{:S(2)}, u32[]{:S(2)}) collective-permute-start(bf16[32,768]{1,0:T(8,128)(2,1)S(1)} %get-tuple-element.22), channel_id=1, source_target_pairs={{0,12},{4,8},{8,4},{12,0},{1,13},{5,9},{9,5},{13,1},{2,14},{6,10},... | collective-permute-start | bytes 147464 | tf_op jit(solution)/shard_map/ppermute | solution.py:204
  45.3 0.6 %collective-permute-start.5 = (bf16[32,768]{1,0:T(8,128)(2,1)S(1)}, bf16[32,768]{1,0:T(8,128)(2,1)S(1)}, u32[]{:S(2)}, u32[]{:S(2)}) collective-permute-start(bf16[32,768]{1,0:T(8,128)(2,1)S(1)} %get-tuple-element.24), channel_id=1, source_target_pairs={{0,8},{4,12},{8,0},{12,4},{1,9},{5,13},{9,1},{13,5},{2,10},{6,14},... | collective-permute-start | bytes 147464 | tf_op jit(solution)/shard_map/ppermute | solution.py:204
  45.8 1.7 %collective-permute-start.6 = (bf16[32,768]{1,0:T(8,128)(2,1)S(1)}, bf16[32,768]{1,0:T(8,128)(2,1)S(1)}, u32[]{:S(2)}, u32[]{:S(2)}) collective-permute-start(bf16[32,768]{1,0:T(8,128)(2,1)S(1)} %get-tuple-element.23), channel_id=1, source_target_pairs={{0,4},{4,0},{8,12},{12,8},{1,5},{5,1},{9,13},{13,9},{2,6},{6,2},{1... | collective-permute-start | bytes 147464 | tf_op jit(solution)/shard_map/ppermute | solution.py:204
  47.6 1.6 %collective-permute-done.4 = bf16[32,768]{1,0:T(8,128)(2,1)S(1)} collective-permute-done((bf16[32,768]{1,0:T(8,128)(2,1)S(1)}, bf16[32,768]{1,0:T(8,128)(2,1)S(1)}, u32[]{:S(2)}, u32[]{:S(2)}) %collective-permute-start.4) | collective-permute-done | bytes 49184 | tf_op jit(solution)/shard_map/ppermute | solution.py:204
  49.2 1.2 %collective-permute-done.5 = bf16[32,768]{1,0:T(8,128)(2,1)S(1)} collective-permute-done((bf16[32,768]{1,0:T(8,128)(2,1)S(1)}, bf16[32,768]{1,0:T(8,128)(2,1)S(1)}, u32[]{:S(2)}, u32[]{:S(2)}) %collective-permute-start.5) | collective-permute-done | bytes 49184 | tf_op jit(solution)/shard_map/ppermute | solution.py:204
  50.4 0.1 collective-permute-done.6
  50.5 0.1 collective-permute-start.7
  50.6 0.0 all-to-all-done.1.returned_ref
  50.6 0.0 copy-done.1
  50.6 0.0 copy-done.2
  50.6 1.2 %token_grad.1 = bf16[64,4,512]{2,1,0:T(4,128)(2,1)} custom-call(bf16[16,16,512]{2,1,0:T(8,128)(2,1)S(1)} %all-to-all-done.1.returned_ref, bf16[64,4,512]{2,1,0:T(4,128)(2,1)S(1)} %bitcast.18, bf16[64,4,512]{2,1,0:T(4,128)(2,1)S(1)} %bitcast.20), custom_call_target="tpu_custom_call" | custom-call | tf_op jit(solution)/shard_map/token_grad/pallas_call | solution.py:36
  51.8 0.1 collective-permute-done.7
  51.9 0.7 %pad_maximum_fusion = f32[32,1536]{1,0:T(8,128)} fusion(f32[32,768]{1,0:T(8,128)S(1)} %get-tuple-element.21, f32[32,768]{1,0:T(8,128)S(1)} %get-tuple-element.20), kind=kLoop, calls=%fused_computation.1 | loop fusion | flops 49152 | bytes 393216 | tf_op jit(solution)/shard_map/concatenate | solution.py:295
  (5 shorter events, 0.1 us)
Async XLA Ops:
  0.6 24.8 %copy-start.3 = (s32[1,256]{1,0:T(1,128)S(1)}, s32[1,256]{1,0:T(1,128)}, u32[]{:S(2)}) copy-start(s32[1,256]{1,0:T(1,128)} %constant.35.clone.pos_ref) | copy-start | bytes 3076
  0.6 24.8 %copy-start = (bf16[512,1536]{1,0:T(8,128)(2,1)S(1)}, bf16[512,1536]{1,0:T(8,128)(2,1)}, u32[]{:S(2)}) copy-start(bf16[512,1536]{1,0:T(8,128)(2,1)} %weight_ref.3) | copy-start | bytes 4718596
  27.8 2.4 %collective-permute-start = (bf16[512,768]{1,0:T(8,128)(2,1)S(1)}, bf16[512,768]{1,0:T(8,128)(2,1)S(1)}, u32[]{:S(2)}, u32[]{:S(2)}) collective-permute-start(bf16[512,768]{1,0:T(8,128)(2,1)S(1)} %get-tuple-element.15), channel_id=1, source_target_pairs={{0,16},{16,0},{1,17},{17,1},{2,18},{18,2},{3,19},{19,3},{4,20},{20... | collective-permute-start | bytes 2359304 | tf_op jit(solution)/shard_map/ppermute | solution.py:181
  30.2 20.4 %copy-start.1 = (bf16[1,64,4,512]{3,2,1,0:T(4,128)(2,1)S(1)}, bf16[1,64,4,512]{3,2,1,0:T(4,128)(2,1)}, u32[]{:S(2)}) copy-start(bf16[1,64,4,512]{3,2,1,0:T(4,128)(2,1)} %param.4) | copy-start | bytes 786436
  30.2 20.4 %copy-start.2 = (bf16[1,64,4,512]{3,2,1,0:T(4,128)(2,1)S(1)}, bf16[1,64,4,512]{3,2,1,0:T(4,128)(2,1)}, u32[]{:S(2)}) copy-start(bf16[1,64,4,512]{3,2,1,0:T(4,128)(2,1)} %param.6) | copy-start | bytes 786436
  30.4 7.8 %collective-permute-start.1 = (bf16[4,32,768]{2,1,0:T(8,128)(2,1)S(1)}, bf16[4,32,768]{2,1,0:T(8,128)(2,1)S(1)}, u32[]{:S(2)}, u32[]{:S(2)}) collective-permute-start(bf16[4,32,768]{2,1,0:T(8,128)(2,1)S(1)} %get-tuple-element.17), channel_id=1, source_target_pairs={{0,1},{1,0},{2,3},{3,2},{4,5},{5,4},{6,7},{7,6},{8,9},{9,8},{10,11... | collective-permute-start | bytes 589832 | tf_op jit(solution)/shard_map/ppermute | solution.py:194
  31.0 7.4 %collective-permute-start.2 = (bf16[4,32,768]{2,1,0:T(8,128)(2,1)S(1)}, bf16[4,32,768]{2,1,0:T(8,128)(2,1)S(1)}, u32[]{:S(2)}, u32[]{:S(2)}) collective-permute-start(bf16[4,32,768]{2,1,0:T(8,128)(2,1)S(1)} %get-tuple-element.18), channel_id=1, source_target_pairs={{0,2},{1,3},{2,0},{3,1},{4,6},{5,7},{6,4},{7,5},{8,10},{9,11},{10,... | collective-permute-start | bytes 589832 | tf_op jit(solution)/shard_map/ppermute | solution.py:194
  31.9 11.1 %collective-permute-start.3 = (bf16[4,32,768]{2,1,0:T(8,128)(2,1)S(1)}, bf16[4,32,768]{2,1,0:T(8,128)(2,1)S(1)}, u32[]{:S(2)}, u32[]{:S(2)}) collective-permute-start(bf16[4,32,768]{2,1,0:T(8,128)(2,1)S(1)} %get-tuple-element.19), channel_id=1, source_target_pairs={{0,3},{1,2},{2,1},{3,0},{4,7},{5,6},{6,5},{7,4},{8,11},{9,10},{10,... | collective-permute-start | bytes 589832 | tf_op jit(solution)/shard_map/ppermute | solution.py:194
  33.9 16.7 %all-to-all-start.1 = ((bf16[16,16,512]{2,1,0:T(8,128)(2,1)}), bf16[16,16,512]{2,1,0:T(8,128)(2,1)S(1)}, u32[]{:S(2)}, u32[]{:S(2)}) async-start(bf16[16,16,512]{2,1,0:T(8,128)(2,1)} %bitcast.3), calls=%async_computation.1 | async-start | bytes 524288 | tf_op jit(solution)/shard_map/all_to_all | solution.py:278
  43.1 6.1 %collective-permute-start.4 = (bf16[32,768]{1,0:T(8,128)(2,1)S(1)}, bf16[32,768]{1,0:T(8,128)(2,1)S(1)}, u32[]{:S(2)}, u32[]{:S(2)}) collective-permute-start(bf16[32,768]{1,0:T(8,128)(2,1)S(1)} %get-tuple-element.22), channel_id=1, source_target_pairs={{0,12},{4,8},{8,4},{12,0},{1,13},{5,9},{9,5},{13,1},{2,14},{6,10},... | collective-permute-start | bytes 147464 | tf_op jit(solution)/shard_map/ppermute | solution.py:204
  45.3 5.1 %collective-permute-start.5 = (bf16[32,768]{1,0:T(8,128)(2,1)S(1)}, bf16[32,768]{1,0:T(8,128)(2,1)S(1)}, u32[]{:S(2)}, u32[]{:S(2)}) collective-permute-start(bf16[32,768]{1,0:T(8,128)(2,1)S(1)} %get-tuple-element.24), channel_id=1, source_target_pairs={{0,8},{4,12},{8,0},{12,4},{1,9},{5,13},{9,1},{13,5},{2,10},{6,14},... | collective-permute-start | bytes 147464 | tf_op jit(solution)/shard_map/ppermute | solution.py:204
  45.8 4.6 %collective-permute-start.6 = (bf16[32,768]{1,0:T(8,128)(2,1)S(1)}, bf16[32,768]{1,0:T(8,128)(2,1)S(1)}, u32[]{:S(2)}, u32[]{:S(2)}) collective-permute-start(bf16[32,768]{1,0:T(8,128)(2,1)S(1)} %get-tuple-element.23), channel_id=1, source_target_pairs={{0,4},{4,0},{8,12},{12,8},{1,5},{5,1},{9,13},{13,9},{2,6},{6,2},{1... | collective-permute-start | bytes 147464 | tf_op jit(solution)/shard_map/ppermute | solution.py:204
  50.5 1.4 %collective-permute-start.7 = (f32[32,768]{1,0:T(8,128)S(1)}, f32[32,768]{1,0:T(8,128)S(1)}, u32[]{:S(2)}, u32[]{:S(2)}) collective-permute-start(f32[32,768]{1,0:T(8,128)S(1)} %fusion.2), channel_id=1, source_target_pairs={{0,16},{16,0},{1,17},{17,1},{2,18},{18,2},{3,19},{19,3},{4,20},{20... | collective-permute-start | bytes 294920 | tf_op jit(solution)/shard_map/ppermute | solution.py:181

commit v5 on v4

v5 whole, which is shorter than its diff:
```python
import functools

import jax
import jax.numpy as jnp
import numpy as np
from jax import lax
from jax.experimental import pallas as pl
from jax.experimental.pallas import tpu as pltpu
from jax.sharding import PartitionSpec as P

HEADS = 16
HEAD_DIM = 32
GRID = 8
EPS = 1e-05
LANES = 128
BLOCK_HEADS = LANES // HEAD_DIM
GROUP = 8

BF16 = jnp.bfloat16
F32 = jnp.float32


def matmul(a, b, contract):
    return lax.dot_general(a, b, ((contract[:1], contract[1:]), ((), ())), preferred_element_type=F32)


def normalize(pixels):
    center = pixels - jnp.mean(pixels, axis=-1, keepdims=True)
    inv_std = lax.rsqrt(jnp.mean(center * center, axis=-1, keepdims=True) + EPS)
    return center * inv_std, inv_std


def vmem_call(kernel, outs, name, *args, scratch=(), mib=8, remote=()):
    vmem = pl.BlockSpec(memory_space=pltpu.VMEM)
    hbm = pl.BlockSpec(memory_space=pltpu.HBM)
    return pl.pallas_call(
        kernel,
        out_shape=outs,
        in_specs=[hbm if index in remote else vmem for index in range(len(args))],
        out_specs=[vmem] * len(outs),
        scratch_shapes=scratch,
        compiler_params=pltpu.CompilerParams(vmem_limit_bytes=mib * 2**20),
        name=name,
    )(*args)


def in_chunks(shape, pixels):
    channels = pixels.shape[-1]
    pixels = pixels.astype(F32).reshape(*shape, channels)
    return jnp.concatenate([pixels[index] for index in range(shape[0])], axis=1)


def pack_kernel(shape, tokens_ref, cot_ref, sent_ref, tokens_buf, cot_buf, sems):
    channels = tokens_buf.shape[2]
    copies = [
        pltpu.make_async_copy(tokens_ref, tokens_buf, sems.at[0]),
        pltpu.make_async_copy(cot_ref, cot_buf, sems.at[1]),
    ]
    for copy in copies:
        copy.start()
    copies[0].wait()
    sent_ref[:, :, :channels] = normalize(in_chunks(shape, tokens_buf[...]))[0].astype(BF16)
    copies[1].wait()
    sent_ref[:, :, channels:] = in_chunks(shape, cot_buf[...]).astype(BF16)


def unpack_kernel(shape, returned_ref, tokens_ref, cot_ref, grad_ref):
    outer, tiles, size = shape
    standard, inv_std = normalize(in_chunks(shape, tokens_ref[...]))
    normed_grad = returned_ref[...].astype(F32)
    inner = (
        normed_grad
        - jnp.mean(normed_grad, axis=-1, keepdims=True)
        - standard * jnp.mean(normed_grad * standard, axis=-1, keepdims=True)
    )
    grad = in_chunks(shape, cot_ref[...]) + inv_std * inner
    rows = grad_ref.shape[0] // outer
    for index in range(outer):
        part = grad[:, index * size : (index + 1) * size].astype(BF16)
        grad_ref[index * rows : (index + 1) * rows] = part.reshape(rows, *grad_ref.shape[1:])


def window_order(pos_ref):
    count = pos_ref.shape[1]
    rows = lax.broadcasted_iota(jnp.int32, (count, count), 0)
    return jnp.where(rows == pos_ref[...], 1.0, 0.0).astype(BF16)


def half_slices(halves, side, channels):
    width = channels // halves
    return [pl.ds(pl.multiple_of(part * channels + side * width, LANES), width) for part in range(3)]


def attend(weight_ref, columns, normed, scratch, proj_ref):
    cot_ref, query_ref, key_ref, value_ref = scratch
    count, width = cot_ref.shape
    win_tokens = GRID * GRID
    scale = HEAD_DIM**-0.5

    query_ref[...] = (matmul(normed, weight_ref[:, columns[0]], (1, 0)) * scale).astype(BF16)
    key_ref[...] = matmul(normed, weight_ref[:, columns[1]], (1, 0)).astype(BF16)
    value_ref[...] = matmul(normed, weight_ref[:, columns[2]], (1, 0)).astype(BF16)

    stack_shape = (BLOCK_HEADS * win_tokens, LANES)
    own = lax.broadcasted_iota(jnp.int32, stack_shape, 0) // win_tokens == (
        lax.broadcasted_iota(jnp.int32, stack_shape, 1) // HEAD_DIM
    )
    mask = jnp.where(own, 1.0, 0.0)
    mask_low = mask.astype(BF16)

    def stack(block):
        return jnp.concatenate([block] * BLOCK_HEADS, axis=0) * mask_low

    cells = [
        (slice(row, row + win_tokens), slice(col, col + LANES))
        for row in range(0, count, win_tokens)
        for col in range(0, width, LANES)
    ]
    for first in range(0, len(cells), GROUP):
        group = cells[first : first + GROUP]
        raw = []
        for row, col in group:
            scores = matmul(key_ref[row, col], stack(query_ref[row, col]), (1, 1))
            attn_grad = matmul(value_ref[row, col], stack(cot_ref[row, col]), (1, 1))
            raw.append((scores, attn_grad))
        low = []
        for scores, attn_grad in raw:
            exponent = jnp.exp(scores - jnp.max(scores, axis=0, keepdims=True))
            probs = exponent * (1.0 / jnp.sum(exponent, axis=0, keepdims=True))
            score_grad = probs * (attn_grad - jnp.sum(probs * attn_grad, axis=0, keepdims=True))
            low.append((probs.astype(BF16), score_grad.astype(BF16)))
        for (row, col), (probs, score_grad) in zip(group, low):
            value_grad = matmul(probs, stack(cot_ref[row, col]), (1, 0))
            key_grad = matmul(score_grad, stack(query_ref[row, col]), (1, 0))
            spread = matmul(score_grad, key_ref[row, col], (0, 0)) * mask
            query_grad = spread[:win_tokens]
            for head in range(1, BLOCK_HEADS):
                query_grad += spread[head * win_tokens : (head + 1) * win_tokens]
            for part, grad in enumerate((query_grad * scale, key_grad, value_grad)):
                base = part * width + col.start
                proj_ref[row, base : base + LANES] = grad.astype(BF16)


def first_kernel(halves, pos_ref, pixels_ref, weight_ref, proj_ref, normed_ref, term_ref, cot_ref, *scratch):
    channels = normed_ref.shape[1]
    side = 1 - lax.axis_index("rep") if halves > 1 else 0
    columns = half_slices(halves, side, channels)
    onehot = window_order(pos_ref)
    normed = matmul(onehot, pixels_ref[:, :channels], (1, 0)).astype(BF16)
    normed_ref[...] = normed
    start = pl.multiple_of(columns[0].start + channels, LANES)
    cot = pixels_ref[:, pl.ds(start, columns[0].size)]
    cot_ref[...] = matmul(onehot, cot, (1, 0)).astype(BF16)
    attend(weight_ref, columns, normed, (cot_ref, *scratch), proj_ref)
    term_ref[...] = matmul(normed, proj_ref[...], (0, 0)).astype(term_ref.dtype)


def second_kernel(pos_ref, pixels_ref, weight_ref, normed_ref, proj_ref, term_ref, cot_ref, *scratch):
    channels = normed_ref.shape[1]
    columns = half_slices(2, lax.axis_index("rep"), channels)
    start = pl.multiple_of(columns[0].start + channels, LANES)
    cot = pixels_ref[:, pl.ds(start, columns[0].size)]
    cot_ref[...] = matmul(window_order(pos_ref), cot, (1, 0)).astype(BF16)
    normed = normed_ref[...]
    attend(weight_ref, columns, normed, (cot_ref, *scratch), proj_ref)
    term_ref[...] = matmul(normed, proj_ref[...], (0, 0)).astype(BF16)


def back_kernel(pos_ref, weight_ref, *refs):
    *proj_refs, grad_ref = refs
    halves = len(proj_refs)
    channels = weight_ref.shape[0]
    width = channels // halves
    total = 0.0
    for index, ref in enumerate(proj_refs):
        side = lax.axis_index("rep") if halves > 1 else 0
        side = 1 - side if index == 0 and halves > 1 else side
        for part, column in enumerate(half_slices(halves, side, channels)):
            total += matmul(ref[:, part * width : (part + 1) * width], weight_ref[:, column], (1, 1))
    grad_ref[...] = matmul(window_order(pos_ref), total.astype(BF16), (0, 0)).astype(BF16)


def join_kernel(own_ref, other_ref, out_ref):
    width = own_ref.shape[1] // 3
    side = lax.axis_index("rep")
    for ref, half in ((own_ref, side), (other_ref, 1 - side)):
        for part in range(3):
            start = pl.multiple_of((2 * part + half) * width, LANES)
            out_ref[:, pl.ds(start, width)] = ref[:, part * width : (part + 1) * width]


def swap_reps(values):
    return lax.ppermute(values, "rep", [(0, 1), (1, 0)])


def split_kernel(axis, along, count, steps, *refs):
    me = lax.axis_index(axis)
    sources, parts = refs[:count], refs[count:]
    for step, ref in zip(steps, parts):
        index = (slice(None),) * along + (me ^ step,)
        ref[...] = sum(source[index].astype(F32) for source in sources).astype(BF16)


def split(axis, along, steps, name, *sources):
    shape = sources[0].shape
    part = jax.ShapeDtypeStruct(shape[:along] + shape[along + 1 :], BF16)
    kernel = functools.partial(split_kernel, axis, along, len(sources), steps)
    return vmem_call(kernel, [part] * len(steps), name, *sources)


def travel(parts, axis, steps):
    size = len(parts)
    return [parts[0]] + [
        lax.ppermute(part, axis, [(i, i ^ step) for i in range(size)])
        for part, step in zip(parts[1:], steps[1:])
    ]


def shards(tokens, qkv_weight, cotangent):
    rep_count = lax.axis_size("rep")
    row_tiles = lax.axis_size("ty")
    col_tiles = lax.axis_size("tx")
    tile_count = row_tiles * col_tiles
    _, tile_height, tile_width, channels = tokens.shape
    stride_rows = row_tiles * tile_height // GRID
    stride_cols = col_tiles * tile_width // GRID
    block_rows = min(tile_height, stride_rows)
    fold_rows = stride_rows // block_rows
    col_groups = tile_width // stride_cols
    outer_rows = tile_height // block_rows
    axes = ("tx", "rep", "ty") if rep_count == 2 else ("tx", "ty")
    samples = rep_count if "rep" in axes else 1
    group_count = tile_count * samples
    inner_rows = block_rows // group_count
    chunk = outer_rows * inner_rows * tile_width
    count = group_count * chunk

    cuts = {"tx": [("tx", col_tiles)], "rep": [("rep", samples)]}
    cuts["ty"] = [("ty", row_tiles // fold_rows), ("fold", fold_rows)]
    dims = [cut for axis in axes for cut in cuts[axis]]
    dims += [("outer", outer_rows), ("inner", inner_rows), ("group", col_groups), ("col", stride_cols)]
    names = [name for name, _ in dims]
    window = [name for name in ("rep", "fold", "inner", "col") if name in names]
    token = [name for name in names if name not in window]
    order = np.arange(count).reshape([size for _, size in dims])
    order = order.transpose([names.index(name) for name in window + token]).reshape(count)
    pos = np.zeros((1, count), np.int32)
    pos[0, order] = np.arange(count)

    local = (tile_height, tile_width, channels)
    split_shape = (outer_rows, group_count, inner_rows * tile_width)
    tokens, cotangent = tokens.reshape(local), cotangent.reshape(local)
    (sent,) = vmem_call(
        functools.partial(pack_kernel, split_shape),
        [jax.ShapeDtypeStruct((group_count, chunk, 2 * channels), BF16)],
        "pack",
        pltpu.with_memory_space_constraint(tokens, pltpu.HBM),
        pltpu.with_memory_space_constraint(cotangent, pltpu.HBM),
        scratch=[
            pltpu.VMEM(local, BF16),
            pltpu.VMEM(local, BF16),
            pltpu.SemaphoreType.DMA((2,)),
        ],
        remote=(0, 1),
    )
    pixels = lax.all_to_all(sent, axes, split_axis=0, concat_axis=0, tiled=True)
    pixels = pixels.reshape(count, 2 * channels)

    halves = 2 if rep_count == 2 else 1
    width = channels // halves
    order = jnp.asarray(pos)
    flat = jax.ShapeDtypeStruct((count, channels), BF16)
    proj = jax.ShapeDtypeStruct((count, 3 * width), BF16)
    term = jax.ShapeDtypeStruct((channels, 3 * width), BF16 if halves == 2 else F32)
    scratch = [pltpu.VMEM((count, width), BF16)] * 4
    first_proj, normed, send = vmem_call(
        functools.partial(first_kernel, halves),
        [proj, flat, term],
        "first_heads",
        order,
        pixels,
        qkv_weight,
        scratch=scratch,
        mib=16,
    )
    projs = [first_proj]
    if halves == 2:
        second_proj, keep = vmem_call(
            second_kernel,
            [proj, term],
            "second_heads",
            order,
            pixels,
            qkv_weight,
            normed,
            scratch=scratch,
            mib=16,
        )
        projs.append(second_proj)
        near = tuple(range(col_tiles))
        far = (0, 2, 3, 1)
        shape = (row_tiles, col_tiles, channels // tile_count, 3 * width)
        parts = split("tx", 1, near, "split_tx", keep.reshape(shape), swap_reps(send).reshape(shape))
    (normed_grad,) = vmem_call(back_kernel, [flat], "normed_grad", order, qkv_weight, *projs)
    spread = normed_grad.reshape(group_count, chunk, channels)
    returned = lax.all_to_all(spread, axes, split_axis=0, concat_axis=0, tiled=True)

    total = rep_count * tile_count
    if halves == 2:
        parts = split("ty", 0, far, "split_ty", *travel(parts, "tx", near))
        rows = sum(part.astype(F32) for part in travel(parts, "ty", far)) / total
        (weight_grad,) = vmem_call(
            join_kernel,
            [jax.ShapeDtypeStruct((rows.shape[0], 3 * channels), F32)],
            "weight_grad",
            rows,
            swap_reps(rows),
        )
    else:
        weight_grad = lax.psum_scatter(send, ("ty", "tx"), scatter_dimension=0, tiled=True)
        weight_grad = lax.psum(weight_grad, "rep") / total

    (token_grad,) = vmem_call(
        functools.partial(unpack_kernel, split_shape),
        [jax.ShapeDtypeStruct(local, BF16)],
        "token_grad",
        returned,
        tokens,
        cotangent,
    )
    token_grad = token_grad.reshape(1, *local)
    return (token_grad, weight_grad)


def solution(mesh):
    placed = (P("rep", "ty", "tx", None), P(), P("rep", "ty", "tx", None))
    return jax.shard_map(
        shards,
        mesh=mesh,
        in_specs=placed,
        out_specs=(P("rep", "ty", "tx", None), P(("ty", "tx"), None)),
        check_vma=False,
    )
```

time: 52.9 us -> 52.2 us (0.987)
  blocking collectives: 23.2 us -> 21.5 us
  waiting for transfers between devices: 8.62 us -> 9.87 us
  Pallas kernels: 7.04 us -> 8.16 us
  other arithmetic: 0.84 us -> 0.03 us
    all_to_all x1, blocking collectives: 23.2 us -> 21.5 us  [shards(): pixels = lax.all_to_all(sent, axes, split_axis=0, concat_axis=0, tiled=True)]
    ppermute x6, waiting for transfers between devices: 8.05 us -> 9.35 us  [travel(): lax.ppermute(part, axis, [(i, i ^ step) for i in range(size)])]
    ppermute x2, starting transfers between devices: 0.14 us -> 1.31 us  [swap_reps(): return lax.ppermute(values, 'rep', [(0, 1), (1, 0)])]
    pallas_call x5 -> x8, Pallas kernels: 7.04 us -> 8.16 us  [vmem_call(): pl.pallas_call(kernel, out_shape=outs, in_specs=[hbm if index in remote e...]
    ppermute x6, starting transfers between devices: 8.01 us -> 7.11 us  [travel(): lax.ppermute(part, axis, [(i, i ^ step) for i in range(size)])]
    concatenate x1 -> x0, other arithmetic: 0.69 us -> none  [shards(): jnp.concatenate([jnp.where(first, rows, other), jnp.where(first, other, r...]
    all_to_all x1, starting transfers between devices: 3.9 us -> 3.26 us  [shards(): lax.all_to_all(spread, axes, split_axis=0, concat_axis=0, tiled=True)]
  transfers between devices with their start and end apart: 9 -> 9, of which waited for: 8 -> 4; matrix products, arithmetic and copies ran while one was open for 0% -> 0% of each run, Pallas kernels for 6% -> 8%
where the time goes in v5:
time: 52.2 us; the launch traced here: 52 us
  blocking collectives  21.5 us (41%)
  starting transfers between devices  11.7 us (22%)
  waiting for transfers between devices  9.87 us (19%)
  Pallas kernels  8.16 us (16%)
  between operations  0.74 us (1%)
    all_to_all x1, blocking collectives, shards(): pixels = lax.all_to_all(sent, axes, split_axis=0, concat_axis=0, tiled=True)  21.5 us
    ppermute x6, waiting for transfers between devices, travel(): lax.ppermute(part, axis, [(i, i ^ step) for i in range(size)])  9.35 us
    pallas_call x8, Pallas kernels, vmem_call(): pl.pallas_call(kernel, out_shape=outs, in_specs=[hbm if index in remote e...  8.16 us
    ppermute x6, starting transfers between devices, travel(): lax.ppermute(part, axis, [(i, i ^ step) for i in range(size)])  7.11 us
    all_to_all x1, starting transfers between devices, shards(): lax.all_to_all(spread, axes, split_axis=0, concat_axis=0, tiled=True)  3.26 us
    ppermute x2, starting transfers between devices, swap_reps(): return lax.ppermute(values, 'rep', [(0, 1), (1, 0)])  1.31 us
  transfers between devices with their start and end apart: 9, of which 4 were waited for; matrix products, arithmetic and copies ran while one was open for 0% of the time, Pallas kernels for 8%

profile of v5, /device:TPU:0, one launch (start us, length us, event | category | flops | bytes accessed | tf_op | source)
XLA Modules:
  0.0 52.0 jit_solution(16369857723663535596)
XLA Ops:
  0.6 0.0 copy-start.3
  0.6 0.0 copy-start
  0.7 1.4 %pack.1 = bf16[32,8,1024]{2,1,0:T(8,128)(2,1)S(1)} custom-call(bf16[64,4,512]{2,1,0:T(4,128)(2,1)} %bitcast.9, bf16[64,4,512]{2,1,0:T(4,128)(2,1)} %bitcast.11), custom_call_target="tpu_custom_call" | custom-call | tf_op jit(solution)/shard_map/pack/pallas_call | solution.py:36
  2.0 21.5 %all_to_all.10 = bf16[32,8,1024]{2,1,0:T(8,128)(2,1)S(1)} all-to-all(bf16[32,8,1024]{2,1,0:T(8,128)(2,1)S(1)} %pack.1), channel_id=1, replica_groups=mesh['rep'=2,'ty'=4,'tx'=4] {'tx','rep','ty'}, dimensions={0} | all-to-all | bytes 1048576 | tf_op jit(solution)/shard_map/all_to_all | solution.py:266
  23.5 0.0 copy-done.3
  23.5 0.0 copy-done
  23.5 1.6 %first_heads.1 = (bf16[256,768]{1,0:T(8,128)(2,1)S(1)}, bf16[256,512]{1,0:T(8,128)(2,1)S(1)}, bf16[512,768]{1,0:T(8,128)(2,1)S(1)}) custom-call(s32[1,256]{1,0:T(1,128)S(1)} %copy-done.3, bf16[256,1024]{1,0:T(8,128)(2,1)S(1)} %bitcast.7, bf16[512,1536]{1,0:T(8,128)(2,1)S(1)} %copy-done), custom_call_target="tpu_custom_call" | custom-call | tf_op jit(solution)/shard_map/first_heads/pallas_call | solution.py:36
  25.2 1.2 %collective-permute-start = (bf16[512,768]{1,0:T(8,128)(2,1)S(1)}, bf16[512,768]{1,0:T(8,128)(2,1)S(1)}, u32[]{:S(2)}, u32[]{:S(2)}) collective-permute-start(bf16[512,768]{1,0:T(8,128)(2,1)S(1)} %get-tuple-element.19), channel_id=1, source_target_pairs={{0,16},{16,0},{1,17},{17,1},{2,18},{18,2},{3,19},{19,3},{4,20},{20... | collective-permute-start | bytes 2359304 | tf_op jit(solution)/shard_map/ppermute | solution.py:193
  26.4 1.5 %second_heads.1 = (bf16[256,768]{1,0:T(8,128)(2,1)S(1)}, bf16[512,768]{1,0:T(8,128)(2,1)S(1)}) custom-call(s32[1,256]{1,0:T(1,128)S(1)} %copy-done.3, bf16[256,1024]{1,0:T(8,128)(2,1)S(1)} %bitcast.8, bf16[512,1536]{1,0:T(8,128)(2,1)S(1)} %copy-done, bf16[256,512]{1,0:T(8,128)(2,1)S(1)} %get-tuple-element.16.normed_ref), custom_call_target="tpu_custom_call" | custom-call | tf_op jit(solution)/shard_map/second_heads/pallas_call | solution.py:36
  28.0 0.4 collective-permute-done
  28.3 0.2 split_tx.1
  28.5 1.6 %collective-permute-start.1 = (bf16[4,32,768]{2,1,0:T(8,128)(2,1)S(1)}, bf16[4,32,768]{2,1,0:T(8,128)(2,1)S(1)}, u32[]{:S(2)}, u32[]{:S(2)}) collective-permute-start(bf16[4,32,768]{2,1,0:T(8,128)(2,1)S(1)} %get-tuple-element.21), channel_id=1, source_target_pairs={{0,1},{1,0},{2,3},{3,2},{4,5},{5,4},{6,7},{7,6},{8,9},{9,8},{10,11... | collective-permute-start | bytes 589832 | tf_op jit(solution)/shard_map/ppermute | solution.py:214
  30.1 0.6 %collective-permute-start.2 = (bf16[4,32,768]{2,1,0:T(8,128)(2,1)S(1)}, bf16[4,32,768]{2,1,0:T(8,128)(2,1)S(1)}, u32[]{:S(2)}, u32[]{:S(2)}) collective-permute-start(bf16[4,32,768]{2,1,0:T(8,128)(2,1)S(1)} %get-tuple-element.22), channel_id=1, source_target_pairs={{0,2},{1,3},{2,0},{3,1},{4,6},{5,7},{6,4},{7,5},{8,10},{9,11},{10,... | collective-permute-start | bytes 589832 | tf_op jit(solution)/shard_map/ppermute | solution.py:214
  30.6 1.5 %collective-permute-start.3 = (bf16[4,32,768]{2,1,0:T(8,128)(2,1)S(1)}, bf16[4,32,768]{2,1,0:T(8,128)(2,1)S(1)}, u32[]{:S(2)}, u32[]{:S(2)}) collective-permute-start(bf16[4,32,768]{2,1,0:T(8,128)(2,1)S(1)} %get-tuple-element.23), channel_id=1, source_target_pairs={{0,3},{1,2},{2,1},{3,0},{4,7},{5,6},{6,5},{7,4},{8,11},{9,10},{10,... | collective-permute-start | bytes 589832 | tf_op jit(solution)/shard_map/ppermute | solution.py:214
  32.1 1.5 %normed_grad.1 = bf16[256,512]{1,0:T(8,128)(2,1)} custom-call(s32[1,256]{1,0:T(1,128)S(1)} %copy-done.3, bf16[512,1536]{1,0:T(8,128)(2,1)S(1)} %copy-done, bf16[256,768]{1,0:T(8,128)(2,1)S(1)} %get-tuple-element.15.refs_0_, bf16[256,768]{1,0:T(8,128)(2,1)S(1)} %get-tuple-element.17.refs_1_), custom_call_target="tpu_custom_call" | custom-call | tf_op jit(solution)/shard_map/normed_grad/pallas_call | solution.py:36
  33.6 3.3 %all-to-all-start.1 = ((bf16[32,8,512]{2,1,0:T(8,128)(2,1)}), bf16[32,8,512]{2,1,0:T(8,128)(2,1)S(1)}, u32[]{:S(2)}, u32[]{:S(2)}) async-start(bf16[32,8,512]{2,1,0:T(8,128)(2,1)} %bitcast.3), calls=%async_computation.1 | async-start | bytes 524288 | tf_op jit(solution)/shard_map/all_to_all | solution.py:306
  36.9 0.0 collective-permute-done.1.refs_1_
  36.9 5.4 %collective-permute-done.2.refs_2_ = bf16[4,32,768]{2,1,0:T(8,128)(2,1)S(1)} collective-permute-done((bf16[4,32,768]{2,1,0:T(8,128)(2,1)S(1)}, bf16[4,32,768]{2,1,0:T(8,128)(2,1)S(1)}, u32[]{:S(2)}, u32[]{:S(2)}) %collective-permute-start.2) | collective-permute-done | bytes 196640 | tf_op jit(solution)/shard_map/ppermute | solution.py:214
  42.2 0.0 collective-permute-done.3.refs_3_
  42.2 0.1 split_ty.1
  42.3 0.1 collective-permute-start.4
  42.4 1.7 %collective-permute-start.5 = (bf16[32,768]{1,0:T(8,128)(2,1)S(1)}, bf16[32,768]{1,0:T(8,128)(2,1)S(1)}, u32[]{:S(2)}, u32[]{:S(2)}) collective-permute-start(bf16[32,768]{1,0:T(8,128)(2,1)S(1)} %get-tuple-element.26), channel_id=1, source_target_pairs={{0,12},{4,8},{8,4},{12,0},{1,13},{5,9},{9,5},{13,1},{2,14},{6,10},... | collective-permute-start | bytes 147464 | tf_op jit(solution)/shard_map/ppermute | solution.py:214
  44.1 1.8 %collective-permute-start.6 = (bf16[32,768]{1,0:T(8,128)(2,1)S(1)}, bf16[32,768]{1,0:T(8,128)(2,1)S(1)}, u32[]{:S(2)}, u32[]{:S(2)}) collective-permute-start(bf16[32,768]{1,0:T(8,128)(2,1)S(1)} %get-tuple-element.27), channel_id=1, source_target_pairs={{0,4},{4,0},{8,12},{12,8},{1,5},{5,1},{9,13},{13,9},{2,6},{6,2},{1... | collective-permute-start | bytes 147464 | tf_op jit(solution)/shard_map/ppermute | solution.py:214
  45.9 4.0 %collective-permute-done.4 = bf16[32,768]{1,0:T(8,128)(2,1)S(1)} collective-permute-done((bf16[32,768]{1,0:T(8,128)(2,1)S(1)}, bf16[32,768]{1,0:T(8,128)(2,1)S(1)}, u32[]{:S(2)}, u32[]{:S(2)}) %collective-permute-start.4) | collective-permute-done | bytes 49184 | tf_op jit(solution)/shard_map/ppermute | solution.py:214
  49.9 0.0 collective-permute-done.5
  49.9 0.0 collective-permute-done.6
  49.9 0.1 collective-permute-start.7
  50.0 0.0 all-to-all-done.1.returned_ref
  50.0 0.0 copy-done.1
  50.0 1.1 %token_grad.1 = bf16[64,4,512]{2,1,0:T(4,128)(2,1)} custom-call(bf16[32,8,512]{2,1,0:T(8,128)(2,1)S(1)} %all-to-all-done.1.returned_ref, bf16[64,4,512]{2,1,0:T(4,128)(2,1)S(1)} %bitcast.10, bf16[64,4,512]{2,1,0:T(4,128)(2,1)S(1)} %bitcast.12), custom_call_target="tpu_custom_call" | custom-call | tf_op jit(solution)/shard_map/token_grad/pallas_call | solution.py:36
  51.1 0.1 collective-permute-done.7.other_ref
  51.3 0.7 %weight_grad.1 = f32[32,1536]{1,0:T(8,128)} custom-call(f32[32,768]{1,0:T(8,128)S(1)} %add_multiply_fusion.own_ref, f32[32,768]{1,0:T(8,128)S(1)} %collective-permute-done.7.other_ref), custom_call_target="tpu_custom_call" | custom-call | tf_op jit(solution)/shard_map/weight_grad/pallas_call | solution.py:36
  (4 shorter events, 0.0 us)
Async XLA Ops:
  0.6 22.9 %copy-start.3 = (s32[1,256]{1,0:T(1,128)S(1)}, s32[1,256]{1,0:T(1,128)}, u32[]{:S(2)}) copy-start(s32[1,256]{1,0:T(1,128)} %constant.5.clone.pos_ref) | copy-start | bytes 3076
  0.6 22.9 %copy-start = (bf16[512,1536]{1,0:T(8,128)(2,1)S(1)}, bf16[512,1536]{1,0:T(8,128)(2,1)}, u32[]{:S(2)}) copy-start(bf16[512,1536]{1,0:T(8,128)(2,1)} %weight_ref.5) | copy-start | bytes 4718596
  25.2 3.2 %collective-permute-start = (bf16[512,768]{1,0:T(8,128)(2,1)S(1)}, bf16[512,768]{1,0:T(8,128)(2,1)S(1)}, u32[]{:S(2)}, u32[]{:S(2)}) collective-permute-start(bf16[512,768]{1,0:T(8,128)(2,1)S(1)} %get-tuple-element.19), channel_id=1, source_target_pairs={{0,16},{16,0},{1,17},{17,1},{2,18},{18,2},{3,19},{19,3},{4,20},{20... | collective-permute-start | bytes 2359304 | tf_op jit(solution)/shard_map/ppermute | solution.py:193
  28.5 8.4 %collective-permute-start.1 = (bf16[4,32,768]{2,1,0:T(8,128)(2,1)S(1)}, bf16[4,32,768]{2,1,0:T(8,128)(2,1)S(1)}, u32[]{:S(2)}, u32[]{:S(2)}) collective-permute-start(bf16[4,32,768]{2,1,0:T(8,128)(2,1)S(1)} %get-tuple-element.21), channel_id=1, source_target_pairs={{0,1},{1,0},{2,3},{3,2},{4,5},{5,4},{6,7},{7,6},{8,9},{9,8},{10,11... | collective-permute-start | bytes 589832 | tf_op jit(solution)/shard_map/ppermute | solution.py:214
  30.1 12.2 %collective-permute-start.2 = (bf16[4,32,768]{2,1,0:T(8,128)(2,1)S(1)}, bf16[4,32,768]{2,1,0:T(8,128)(2,1)S(1)}, u32[]{:S(2)}, u32[]{:S(2)}) collective-permute-start(bf16[4,32,768]{2,1,0:T(8,128)(2,1)S(1)} %get-tuple-element.22), channel_id=1, source_target_pairs={{0,2},{1,3},{2,0},{3,1},{4,6},{5,7},{6,4},{7,5},{8,10},{9,11},{10,... | collective-permute-start | bytes 589832 | tf_op jit(solution)/shard_map/ppermute | solution.py:214
  30.6 11.6 %collective-permute-start.3 = (bf16[4,32,768]{2,1,0:T(8,128)(2,1)S(1)}, bf16[4,32,768]{2,1,0:T(8,128)(2,1)S(1)}, u32[]{:S(2)}, u32[]{:S(2)}) collective-permute-start(bf16[4,32,768]{2,1,0:T(8,128)(2,1)S(1)} %get-tuple-element.23), channel_id=1, source_target_pairs={{0,3},{1,2},{2,1},{3,0},{4,7},{5,6},{6,5},{7,4},{8,11},{9,10},{10,... | collective-permute-start | bytes 589832 | tf_op jit(solution)/shard_map/ppermute | solution.py:214
  32.1 17.9 %copy-start.1 = (bf16[1,64,4,512]{3,2,1,0:T(4,128)(2,1)S(1)}, bf16[1,64,4,512]{3,2,1,0:T(4,128)(2,1)}, u32[]{:S(2)}) copy-start(bf16[1,64,4,512]{3,2,1,0:T(4,128)(2,1)} %param.4) | copy-start | bytes 786436
  32.1 17.9 %copy-start.2 = (bf16[1,64,4,512]{3,2,1,0:T(4,128)(2,1)S(1)}, bf16[1,64,4,512]{3,2,1,0:T(4,128)(2,1)}, u32[]{:S(2)}) copy-start(bf16[1,64,4,512]{3,2,1,0:T(4,128)(2,1)} %param.6) | copy-start | bytes 786436
  33.6 16.4 %all-to-all-start.1 = ((bf16[32,8,512]{2,1,0:T(8,128)(2,1)}), bf16[32,8,512]{2,1,0:T(8,128)(2,1)S(1)}, u32[]{:S(2)}, u32[]{:S(2)}) async-start(bf16[32,8,512]{2,1,0:T(8,128)(2,1)} %bitcast.3), calls=%async_computation.1 | async-start | bytes 524288 | tf_op jit(solution)/shard_map/all_to_all | solution.py:306
  42.3 7.5 %collective-permute-start.4 = (bf16[32,768]{1,0:T(8,128)(2,1)S(1)}, bf16[32,768]{1,0:T(8,128)(2,1)S(1)}, u32[]{:S(2)}, u32[]{:S(2)}) collective-permute-start(bf16[32,768]{1,0:T(8,128)(2,1)S(1)} %get-tuple-element.25), channel_id=1, source_target_pairs={{0,8},{4,12},{8,0},{12,4},{1,9},{5,13},{9,1},{13,5},{2,10},{6,14},... | collective-permute-start | bytes 147464 | tf_op jit(solution)/shard_map/ppermute | solution.py:214
  42.4 7.5 %collective-permute-start.5 = (bf16[32,768]{1,0:T(8,128)(2,1)S(1)}, bf16[32,768]{1,0:T(8,128)(2,1)S(1)}, u32[]{:S(2)}, u32[]{:S(2)}) collective-permute-start(bf16[32,768]{1,0:T(8,128)(2,1)S(1)} %get-tuple-element.26), channel_id=1, source_target_pairs={{0,12},{4,8},{8,4},{12,0},{1,13},{5,9},{9,5},{13,1},{2,14},{6,10},... | collective-permute-start | bytes 147464 | tf_op jit(solution)/shard_map/ppermute | solution.py:214
  44.1 5.8 %collective-permute-start.6 = (bf16[32,768]{1,0:T(8,128)(2,1)S(1)}, bf16[32,768]{1,0:T(8,128)(2,1)S(1)}, u32[]{:S(2)}, u32[]{:S(2)}) collective-permute-start(bf16[32,768]{1,0:T(8,128)(2,1)S(1)} %get-tuple-element.27), channel_id=1, source_target_pairs={{0,4},{4,0},{8,12},{12,8},{1,5},{5,1},{9,13},{13,9},{2,6},{6,2},{1... | collective-permute-start | bytes 147464 | tf_op jit(solution)/shard_map/ppermute | solution.py:214
  49.9 1.4 %collective-permute-start.7 = (f32[32,768]{1,0:T(8,128)S(1)}, f32[32,768]{1,0:T(8,128)S(1)}, u32[]{:S(2)}, u32[]{:S(2)}) collective-permute-start(f32[32,768]{1,0:T(8,128)S(1)} %add_multiply_fusion.own_ref), channel_id=1, source_target_pairs={{0,16},{16,0},{1,17},{17,1},{2,18},{18,2},{3,19},{19,3},{4,20},{20... | collective-permute-start | bytes 294920 | tf_op jit(solution)/shard_map/ppermute | solution.py:193

commit v6 on v5

--- a/solution.py
+++ b/solution.py
@@ -228,19 +228,30 @@
     fold_rows = stride_rows // block_rows
     col_groups = tile_width // stride_cols
     outer_rows = tile_height // block_rows
-    axes = ("tx", "rep", "ty") if rep_count == 2 else ("tx", "ty")
-    samples = rep_count if "rep" in axes else 1
+    samples = rep_count if rep_count == 2 and fold_rows == 1 else 1
     group_count = tile_count * samples
+    digits = {"rep": samples, "z": row_tiles // 2, "row": 2, "y": col_tiles // 2, "column": 2}
+    natural = list(digits)
+    turned = ["y", "column", "row", "rep", "z"] if samples == 2 else natural
+    devices = np.arange(group_count).reshape(list(digits.values()))
+    devices = devices.transpose([natural.index(name) for name in turned]).reshape(-1).tolist()
+    groups = [[rep * tile_count + device for device in devices] for rep in range(rep_count // samples)]
+    exchange = functools.partial(
+        lax.all_to_all,
+        axis_name=("rep", "ty", "tx"),
+        split_axis=0,
+        concat_axis=0,
+        tiled=True,
+        axis_index_groups=groups,
+    )
     inner_rows = block_rows // group_count
     chunk = outer_rows * inner_rows * tile_width
     count = group_count * chunk
 
-    cuts = {"tx": [("tx", col_tiles)], "rep": [("rep", samples)]}
-    cuts["ty"] = [("ty", row_tiles // fold_rows), ("fold", fold_rows)]
-    dims = [cut for axis in axes for cut in cuts[axis]]
+    dims = [(name, digits[name]) for name in turned]
     dims += [("outer", outer_rows), ("inner", inner_rows), ("group", col_groups), ("col", stride_cols)]
     names = [name for name, _ in dims]
-    window = [name for name in ("rep", "fold", "inner", "col") if name in names]
+    window = ["rep", "inner", "col"] + ["row"] * (fold_rows == 2)
     token = [name for name in names if name not in window]
     order = np.arange(count).reshape([size for _, size in dims])
     order = order.transpose([names.index(name) for name in window + token]).reshape(count)
@@ -263,10 +274,10 @@
         ],
         remote=(0, 1),
     )
-    pixels = lax.all_to_all(sent, axes, split_axis=0, concat_axis=0, tiled=True)
+    pixels = exchange(sent)
     pixels = pixels.reshape(count, 2 * channels)
 
-    halves = 2 if rep_count == 2 else 1
+    halves = samples
     width = channels // halves
     order = jnp.asarray(pos)
     flat = jax.ShapeDtypeStruct((count, channels), BF16)
@@ -303,7 +314,7 @@
         parts = split("tx", 1, near, "split_tx", keep.reshape(shape), swap_reps(send).reshape(shape))
     (normed_grad,) = vmem_call(back_kernel, [flat], "normed_grad", order, qkv_weight, *projs)
     spread = normed_grad.reshape(group_count, chunk, channels)
-    returned = lax.all_to_all(spread, axes, split_axis=0, concat_axis=0, tiled=True)
+    returned = exchange(spread)
 
     total = rep_count * tile_count
     if halves == 2:

time: 52.2 us -> 51.8 us (level)
  starting transfers between devices: 11.7 us -> 10.3 us
  blocking collectives: 21.5 us -> 22.2 us
    ppermute x2, starting transfers between devices: 1.31 us -> 0.14 us  [swap_reps(): return lax.ppermute(values, 'rep', [(0, 1), (1, 0)])]
    all_to_all x1, blocking collectives: 21.5 us -> 22.2 us  [shards(): pixels = exchange(sent)]
where the time goes in v6:
time: 51.8 us; the launch traced here: 51.6 us
  blocking collectives  22.2 us (43%)
  starting transfers between devices  10.3 us (20%)
  waiting for transfers between devices  10.2 us (20%)
  Pallas kernels  8.17 us (16%)
  between operations  0.74 us (1%)
    all_to_all x1, blocking collectives, shards(): pixels = exchange(sent)  22.2 us
    ppermute x6, waiting for transfers between devices, travel(): lax.ppermute(part, axis, [(i, i ^ step) for i in range(size)])  9.35 us
    pallas_call x8, Pallas kernels, vmem_call(): pl.pallas_call(kernel, out_shape=outs, in_specs=[hbm if index in remote e...  8.17 us
    ppermute x6, starting transfers between devices, travel(): lax.ppermute(part, axis, [(i, i ^ step) for i in range(size)])  7.11 us
    all_to_all x1, starting transfers between devices, shards(): returned = exchange(spread)  3 us
  transfers between devices with their start and end apart: 9, of which 4 were waited for; matrix products, arithmetic and copies ran while one was open for 0% of the time, Pallas kernels for 8%

profile of v6, /device:TPU:0, one launch (start us, length us, event | category | flops | bytes accessed | tf_op | source)
XLA Modules:
  0.0 51.6 jit_solution(12631426184339477297)
XLA Ops:
  0.6 0.0 copy-start.3
  0.6 0.0 copy-start
  0.7 1.4 %pack.1 = bf16[32,8,1024]{2,1,0:T(8,128)(2,1)S(1)} custom-call(bf16[64,4,512]{2,1,0:T(4,128)(2,1)} %bitcast.9, bf16[64,4,512]{2,1,0:T(4,128)(2,1)} %bitcast.11), custom_call_target="tpu_custom_call" | custom-call | tf_op jit(solution)/shard_map/pack/pallas_call | solution.py:36
  2.0 22.2 %all_to_all.10 = bf16[32,8,1024]{2,1,0:T(8,128)(2,1)S(1)} all-to-all(bf16[32,8,1024]{2,1,0:T(8,128)(2,1)S(1)} %pack.1), channel_id=1, replica_groups={{0,8,16,24,4,12,20,28,1,9,17,25,5,13,21,29,2,10,18,26,6,14,22,30,3,11,1..., dimensions={0} | all-to-all | bytes 1048576 | tf_op jit(solution)/shard_map/all_to_all | solution.py:277
  24.2 0.0 copy-done.3
  24.2 1.7 %first_heads.1 = (bf16[256,768]{1,0:T(8,128)(2,1)S(1)}, bf16[256,512]{1,0:T(8,128)(2,1)S(1)}, bf16[512,768]{1,0:T(8,128)(2,1)S(1)}) custom-call(s32[1,256]{1,0:T(1,128)S(1)} %copy-done.3, bf16[256,1024]{1,0:T(8,128)(2,1)S(1)} %bitcast.7, bf16[512,1536]{1,0:T(8,128)(2,1)S(1)} %copy-done), custom_call_target="tpu_custom_call" | custom-call | tf_op jit(solution)/shard_map/first_heads/pallas_call | solution.py:36
  25.9 0.1 collective-permute-start
  26.0 1.5 %second_heads.1 = (bf16[256,768]{1,0:T(8,128)(2,1)S(1)}, bf16[512,768]{1,0:T(8,128)(2,1)S(1)}) custom-call(s32[1,256]{1,0:T(1,128)S(1)} %copy-done.3, bf16[256,1024]{1,0:T(8,128)(2,1)S(1)} %bitcast.8, bf16[512,1536]{1,0:T(8,128)(2,1)S(1)} %copy-done, bf16[256,512]{1,0:T(8,128)(2,1)S(1)} %get-tuple-element.16.normed_ref), custom_call_target="tpu_custom_call" | custom-call | tf_op jit(solution)/shard_map/second_heads/pallas_call | solution.py:36
  27.5 0.7 %collective-permute-done = bf16[512,768]{1,0:T(8,128)(2,1)S(1)} collective-permute-done((bf16[512,768]{1,0:T(8,128)(2,1)S(1)}, bf16[512,768]{1,0:T(8,128)(2,1)S(1)}, u32[]{:S(2)}, u32[]{:S(2)}) %collective-permute-start) | collective-permute-done | bytes 786464 | tf_op jit(solution)/shard_map/ppermute | solution.py:193
  28.2 0.2 split_tx.1
  28.4 1.5 %collective-permute-start.1 = (bf16[4,32,768]{2,1,0:T(8,128)(2,1)S(1)}, bf16[4,32,768]{2,1,0:T(8,128)(2,1)S(1)}, u32[]{:S(2)}, u32[]{:S(2)}) collective-permute-start(bf16[4,32,768]{2,1,0:T(8,128)(2,1)S(1)} %get-tuple-element.21), channel_id=1, source_target_pairs={{0,1},{1,0},{2,3},{3,2},{4,5},{5,4},{6,7},{7,6},{8,9},{9,8},{10,11... | collective-permute-start | bytes 589832 | tf_op jit(solution)/shard_map/ppermute | solution.py:214
  30.0 0.8 %collective-permute-start.2 = (bf16[4,32,768]{2,1,0:T(8,128)(2,1)S(1)}, bf16[4,32,768]{2,1,0:T(8,128)(2,1)S(1)}, u32[]{:S(2)}, u32[]{:S(2)}) collective-permute-start(bf16[4,32,768]{2,1,0:T(8,128)(2,1)S(1)} %get-tuple-element.22), channel_id=1, source_target_pairs={{0,2},{1,3},{2,0},{3,1},{4,6},{5,7},{6,4},{7,5},{8,10},{9,11},{10,... | collective-permute-start | bytes 589832 | tf_op jit(solution)/shard_map/ppermute | solution.py:214
  30.8 1.2 %collective-permute-start.3 = (bf16[4,32,768]{2,1,0:T(8,128)(2,1)S(1)}, bf16[4,32,768]{2,1,0:T(8,128)(2,1)S(1)}, u32[]{:S(2)}, u32[]{:S(2)}) collective-permute-start(bf16[4,32,768]{2,1,0:T(8,128)(2,1)S(1)} %get-tuple-element.23), channel_id=1, source_target_pairs={{0,3},{1,2},{2,1},{3,0},{4,7},{5,6},{6,5},{7,4},{8,11},{9,10},{10,... | collective-permute-start | bytes 589832 | tf_op jit(solution)/shard_map/ppermute | solution.py:214
  32.0 1.5 %normed_grad.1 = bf16[256,512]{1,0:T(8,128)(2,1)} custom-call(s32[1,256]{1,0:T(1,128)S(1)} %copy-done.3, bf16[512,1536]{1,0:T(8,128)(2,1)S(1)} %copy-done, bf16[256,768]{1,0:T(8,128)(2,1)S(1)} %get-tuple-element.15.refs_0_, bf16[256,768]{1,0:T(8,128)(2,1)S(1)} %get-tuple-element.17.refs_1_), custom_call_target="tpu_custom_call" | custom-call | tf_op jit(solution)/shard_map/normed_grad/pallas_call | solution.py:36
  33.5 3.0 %all-to-all-start.1 = ((bf16[32,8,512]{2,1,0:T(8,128)(2,1)}), bf16[32,8,512]{2,1,0:T(8,128)(2,1)S(1)}, u32[]{:S(2)}, u32[]{:S(2)}) async-start(bf16[32,8,512]{2,1,0:T(8,128)(2,1)} %bitcast.3), calls=%async_computation.1 | async-start | bytes 524288 | tf_op jit(solution)/shard_map/all_to_all | solution.py:317
  36.5 0.0 collective-permute-done.1.refs_1_
  36.5 5.4 %collective-permute-done.2.refs_2_ = bf16[4,32,768]{2,1,0:T(8,128)(2,1)S(1)} collective-permute-done((bf16[4,32,768]{2,1,0:T(8,128)(2,1)S(1)}, bf16[4,32,768]{2,1,0:T(8,128)(2,1)S(1)}, u32[]{:S(2)}, u32[]{:S(2)}) %collective-permute-start.2) | collective-permute-done | bytes 196640 | tf_op jit(solution)/shard_map/ppermute | solution.py:214
  41.9 0.0 collective-permute-done.3.refs_3_
  41.9 0.1 split_ty.1
  42.0 0.1 collective-permute-start.4
  42.1 2.6 %collective-permute-start.5 = (bf16[32,768]{1,0:T(8,128)(2,1)S(1)}, bf16[32,768]{1,0:T(8,128)(2,1)S(1)}, u32[]{:S(2)}, u32[]{:S(2)}) collective-permute-start(bf16[32,768]{1,0:T(8,128)(2,1)S(1)} %get-tuple-element.26), channel_id=1, source_target_pairs={{0,12},{4,8},{8,4},{12,0},{1,13},{5,9},{9,5},{13,1},{2,14},{6,10},... | collective-permute-start | bytes 147464 | tf_op jit(solution)/shard_map/ppermute | solution.py:214
  44.7 0.8 %collective-permute-start.6 = (bf16[32,768]{1,0:T(8,128)(2,1)S(1)}, bf16[32,768]{1,0:T(8,128)(2,1)S(1)}, u32[]{:S(2)}, u32[]{:S(2)}) collective-permute-start(bf16[32,768]{1,0:T(8,128)(2,1)S(1)} %get-tuple-element.27), channel_id=1, source_target_pairs={{0,4},{4,0},{8,12},{12,8},{1,5},{5,1},{9,13},{13,9},{2,6},{6,2},{1... | collective-permute-start | bytes 147464 | tf_op jit(solution)/shard_map/ppermute | solution.py:214
  45.6 3.9 %collective-permute-done.4 = bf16[32,768]{1,0:T(8,128)(2,1)S(1)} collective-permute-done((bf16[32,768]{1,0:T(8,128)(2,1)S(1)}, bf16[32,768]{1,0:T(8,128)(2,1)S(1)}, u32[]{:S(2)}, u32[]{:S(2)}) %collective-permute-start.4) | collective-permute-done | bytes 49184 | tf_op jit(solution)/shard_map/ppermute | solution.py:214
  49.5 0.0 collective-permute-done.5
  49.5 0.0 collective-permute-done.6
  49.6 0.1 collective-permute-start.7
  49.6 0.0 all-to-all-done.1.returned_ref
  49.6 0.0 copy-done.1
  49.7 0.0 copy-done.2
  49.7 1.1 %token_grad.1 = bf16[64,4,512]{2,1,0:T(4,128)(2,1)} custom-call(bf16[32,8,512]{2,1,0:T(8,128)(2,1)S(1)} %all-to-all-done.1.returned_ref, bf16[64,4,512]{2,1,0:T(4,128)(2,1)S(1)} %bitcast.10, bf16[64,4,512]{2,1,0:T(4,128)(2,1)S(1)} %bitcast.12), custom_call_target="tpu_custom_call" | custom-call | tf_op jit(solution)/shard_map/token_grad/pallas_call | solution.py:36
  50.8 0.1 collective-permute-done.7.other_ref
  50.9 0.7 %weight_grad.1 = f32[32,1536]{1,0:T(8,128)} custom-call(f32[32,768]{1,0:T(8,128)S(1)} %add_multiply_fusion.own_ref, f32[32,768]{1,0:T(8,128)S(1)} %collective-permute-done.7.other_ref), custom_call_target="tpu_custom_call" | custom-call | tf_op jit(solution)/shard_map/weight_grad/pallas_call | solution.py:36
  (4 shorter events, 0.0 us)
Async XLA Ops:
  0.6 23.6 %copy-start.3 = (s32[1,256]{1,0:T(1,128)S(1)}, s32[1,256]{1,0:T(1,128)}, u32[]{:S(2)}) copy-start(s32[1,256]{1,0:T(1,128)} %constant.5.clone.pos_ref) | copy-start | bytes 3076
  0.6 23.6 %copy-start = (bf16[512,1536]{1,0:T(8,128)(2,1)S(1)}, bf16[512,1536]{1,0:T(8,128)(2,1)}, u32[]{:S(2)}) copy-start(bf16[512,1536]{1,0:T(8,128)(2,1)} %weight_ref.5) | copy-start | bytes 4718596
  25.9 2.4 %collective-permute-start = (bf16[512,768]{1,0:T(8,128)(2,1)S(1)}, bf16[512,768]{1,0:T(8,128)(2,1)S(1)}, u32[]{:S(2)}, u32[]{:S(2)}) collective-permute-start(bf16[512,768]{1,0:T(8,128)(2,1)S(1)} %get-tuple-element.19), channel_id=1, source_target_pairs={{0,16},{16,0},{1,17},{17,1},{2,18},{18,2},{3,19},{19,3},{4,20},{20... | collective-permute-start | bytes 2359304 | tf_op jit(solution)/shard_map/ppermute | solution.py:193
  28.4 8.1 %collective-permute-start.1 = (bf16[4,32,768]{2,1,0:T(8,128)(2,1)S(1)}, bf16[4,32,768]{2,1,0:T(8,128)(2,1)S(1)}, u32[]{:S(2)}, u32[]{:S(2)}) collective-permute-start(bf16[4,32,768]{2,1,0:T(8,128)(2,1)S(1)} %get-tuple-element.21), channel_id=1, source_target_pairs={{0,1},{1,0},{2,3},{3,2},{4,5},{5,4},{6,7},{7,6},{8,9},{9,8},{10,11... | collective-permute-start | bytes 589832 | tf_op jit(solution)/shard_map/ppermute | solution.py:214
  30.0 11.9 %collective-permute-start.2 = (bf16[4,32,768]{2,1,0:T(8,128)(2,1)S(1)}, bf16[4,32,768]{2,1,0:T(8,128)(2,1)S(1)}, u32[]{:S(2)}, u32[]{:S(2)}) collective-permute-start(bf16[4,32,768]{2,1,0:T(8,128)(2,1)S(1)} %get-tuple-element.22), channel_id=1, source_target_pairs={{0,2},{1,3},{2,0},{3,1},{4,6},{5,7},{6,4},{7,5},{8,10},{9,11},{10,... | collective-permute-start | bytes 589832 | tf_op jit(solution)/shard_map/ppermute | solution.py:214
  30.8 11.1 %collective-permute-start.3 = (bf16[4,32,768]{2,1,0:T(8,128)(2,1)S(1)}, bf16[4,32,768]{2,1,0:T(8,128)(2,1)S(1)}, u32[]{:S(2)}, u32[]{:S(2)}) collective-permute-start(bf16[4,32,768]{2,1,0:T(8,128)(2,1)S(1)} %get-tuple-element.23), channel_id=1, source_target_pairs={{0,3},{1,2},{2,1},{3,0},{4,7},{5,6},{6,5},{7,4},{8,11},{9,10},{10,... | collective-permute-start | bytes 589832 | tf_op jit(solution)/shard_map/ppermute | solution.py:214
  32.0 17.7 %copy-start.1 = (bf16[1,64,4,512]{3,2,1,0:T(4,128)(2,1)S(1)}, bf16[1,64,4,512]{3,2,1,0:T(4,128)(2,1)}, u32[]{:S(2)}) copy-start(bf16[1,64,4,512]{3,2,1,0:T(4,128)(2,1)} %param.4) | copy-start | bytes 786436
  32.0 17.7 %copy-start.2 = (bf16[1,64,4,512]{3,2,1,0:T(4,128)(2,1)S(1)}, bf16[1,64,4,512]{3,2,1,0:T(4,128)(2,1)}, u32[]{:S(2)}) copy-start(bf16[1,64,4,512]{3,2,1,0:T(4,128)(2,1)} %param.6) | copy-start | bytes 786436
  33.5 16.1 %all-to-all-start.1 = ((bf16[32,8,512]{2,1,0:T(8,128)(2,1)}), bf16[32,8,512]{2,1,0:T(8,128)(2,1)S(1)}, u32[]{:S(2)}, u32[]{:S(2)}) async-start(bf16[32,8,512]{2,1,0:T(8,128)(2,1)} %bitcast.3), calls=%async_computation.1 | async-start | bytes 524288 | tf_op jit(solution)/shard_map/all_to_all | solution.py:317
  42.0 7.5 %collective-permute-start.4 = (bf16[32,768]{1,0:T(8,128)(2,1)S(1)}, bf16[32,768]{1,0:T(8,128)(2,1)S(1)}, u32[]{:S(2)}, u32[]{:S(2)}) collective-permute-start(bf16[32,768]{1,0:T(8,128)(2,1)S(1)} %get-tuple-element.25), channel_id=1, source_target_pairs={{0,8},{4,12},{8,0},{12,4},{1,9},{5,13},{9,1},{13,5},{2,10},{6,14},... | collective-permute-start | bytes 147464 | tf_op jit(solution)/shard_map/ppermute | solution.py:214
  42.1 7.4 %collective-permute-start.5 = (bf16[32,768]{1,0:T(8,128)(2,1)S(1)}, bf16[32,768]{1,0:T(8,128)(2,1)S(1)}, u32[]{:S(2)}, u32[]{:S(2)}) collective-permute-start(bf16[32,768]{1,0:T(8,128)(2,1)S(1)} %get-tuple-element.26), channel_id=1, source_target_pairs={{0,12},{4,8},{8,4},{12,0},{1,13},{5,9},{9,5},{13,1},{2,14},{6,10},... | collective-permute-start | bytes 147464 | tf_op jit(solution)/shard_map/ppermute | solution.py:214
  44.7 4.8 %collective-permute-start.6 = (bf16[32,768]{1,0:T(8,128)(2,1)S(1)}, bf16[32,768]{1,0:T(8,128)(2,1)S(1)}, u32[]{:S(2)}, u32[]{:S(2)}) collective-permute-start(bf16[32,768]{1,0:T(8,128)(2,1)S(1)} %get-tuple-element.27), channel_id=1, source_target_pairs={{0,4},{4,0},{8,12},{12,8},{1,5},{5,1},{9,13},{13,9},{2,6},{6,2},{1... | collective-permute-start | bytes 147464 | tf_op jit(solution)/shard_map/ppermute | solution.py:214
  49.6 1.4 %collective-permute-start.7 = (f32[32,768]{1,0:T(8,128)S(1)}, f32[32,768]{1,0:T(8,128)S(1)}, u32[]{:S(2)}, u32[]{:S(2)}) collective-permute-start(f32[32,768]{1,0:T(8,128)S(1)} %add_multiply_fusion.own_ref), channel_id=1, source_target_pairs={{0,16},{16,0},{1,17},{17,1},{2,18},{18,2},{3,19},{19,3},{4,20},{20... | collective-permute-start | bytes 294920 | tf_op jit(solution)/shard_map/ppermute | solution.py:193

commit v7 on v6

--- a/solution.py
+++ b/solution.py
@@ -155,29 +155,37 @@
     term_ref[...] = matmul(normed, proj_ref[...], (0, 0)).astype(term_ref.dtype)
 
 
-def second_kernel(pos_ref, pixels_ref, weight_ref, normed_ref, proj_ref, term_ref, cot_ref, *scratch):
+def input_grad(weight_ref, columns, proj_ref):
+    width = columns[0].size
+    return sum(
+        matmul(proj_ref[:, part * width : (part + 1) * width], weight_ref[:, column], (1, 1))
+        for part, column in enumerate(columns)
+    )
+
+
+def second_kernel(
+    pos_ref, pixels_ref, weight_ref, first_ref, normed_ref, grad_ref, term_ref, proj_ref, cot_ref, *scratch
+):
     channels = normed_ref.shape[1]
-    columns = half_slices(2, lax.axis_index("rep"), channels)
+    side = lax.axis_index("rep")
+    columns = half_slices(2, side, channels)
     start = pl.multiple_of(columns[0].start + channels, LANES)
     cot = pixels_ref[:, pl.ds(start, columns[0].size)]
     cot_ref[...] = matmul(window_order(pos_ref), cot, (1, 0)).astype(BF16)
     normed = normed_ref[...]
     attend(weight_ref, columns, normed, (cot_ref, *scratch), proj_ref)
+    grad = input_grad(weight_ref, columns, proj_ref)
+    grad += input_grad(weight_ref, half_slices(2, 1 - side, channels), first_ref)
+    grad_ref[...] = grad.astype(BF16)
     term_ref[...] = matmul(normed, proj_ref[...], (0, 0)).astype(BF16)
 
 
-def back_kernel(pos_ref, weight_ref, *refs):
-    *proj_refs, grad_ref = refs
-    halves = len(proj_refs)
-    channels = weight_ref.shape[0]
-    width = channels // halves
-    total = 0.0
-    for index, ref in enumerate(proj_refs):
-        side = lax.axis_index("rep") if halves > 1 else 0
-        side = 1 - side if index == 0 and halves > 1 else side
-        for part, column in enumerate(half_slices(halves, side, channels)):
-            total += matmul(ref[:, part * width : (part + 1) * width], weight_ref[:, column], (1, 1))
-    grad_ref[...] = matmul(window_order(pos_ref), total.astype(BF16), (0, 0)).astype(BF16)
+def back_kernel(weight_ref, proj_ref, grad_ref):
+    grad_ref[...] = matmul(proj_ref[...], weight_ref[...], (1, 1)).astype(BF16)
+
+
+def spread_kernel(pos_ref, grad_ref, out_ref):
+    out_ref[...] = matmul(window_order(pos_ref), grad_ref[...], (0, 0)).astype(BF16)
 
 
 def join_kernel(own_ref, other_ref, out_ref):
@@ -294,25 +302,26 @@
         scratch=scratch,
         mib=16,
     )
-    projs = [first_proj]
     if halves == 2:
-        second_proj, keep = vmem_call(
+        grad, keep = vmem_call(
             second_kernel,
-            [proj, term],
+            [flat, term],
             "second_heads",
             order,
             pixels,
             qkv_weight,
+            first_proj,
             normed,
-            scratch=scratch,
+            scratch=[pltpu.VMEM((count, 3 * width), BF16)] + scratch,
             mib=16,
         )
-        projs.append(second_proj)
         near = tuple(range(col_tiles))
-        far = (0, 2, 3, 1)
+        far = (0, 1, 2, 3)
         shape = (row_tiles, col_tiles, channels // tile_count, 3 * width)
         parts = split("tx", 1, near, "split_tx", keep.reshape(shape), swap_reps(send).reshape(shape))
-    (normed_grad,) = vmem_call(back_kernel, [flat], "normed_grad", order, qkv_weight, *projs)
+    else:
+        (grad,) = vmem_call(back_kernel, [flat], "normed_grad", qkv_weight, first_proj)
+    (normed_grad,) = vmem_call(spread_kernel, [flat], "spread", order, grad)
     spread = normed_grad.reshape(group_count, chunk, channels)
     returned = exchange(spread)
 

time: 51.8 us -> 51.8 us (level)
  starting transfers between devices: 10.3 us -> 11.2 us
  waiting for transfers between devices: 10.2 us -> 9.55 us
    ppermute x6, starting transfers between devices: 7.11 us -> 8.01 us  [travel(): lax.ppermute(part, axis, [(i, i ^ step) for i in range(size)])]
  transfers between devices with their start and end apart: 9 -> 9, of which waited for: 4 -> 5; matrix products, arithmetic and copies ran while one was open for 0% -> 0% of each run, Pallas kernels for 8% -> 8%
where the time goes in v7:
time: 51.8 us; the launch traced here: 51.6 us
  blocking collectives  22.2 us (43%)
  starting transfers between devices  11.2 us (22%)
  waiting for transfers between devices  9.55 us (18%)
  Pallas kernels  7.9 us (15%)
  between operations  0.73 us (1%)
    all_to_all x1, blocking collectives, shards(): pixels = exchange(sent)  22.2 us
    ppermute x6, waiting for transfers between devices, travel(): lax.ppermute(part, axis, [(i, i ^ step) for i in range(size)])  8.96 us
    ppermute x6, starting transfers between devices, travel(): lax.ppermute(part, axis, [(i, i ^ step) for i in range(size)])  8.01 us
    pallas_call x8, Pallas kernels, vmem_call(): pl.pallas_call(kernel, out_shape=outs, in_specs=[hbm if index in remote e...  7.9 us
    all_to_all x1, starting transfers between devices, shards(): returned = exchange(spread)  3 us
  transfers between devices with their start and end apart: 9, of which 5 were waited for; matrix products, arithmetic and copies ran while one was open for 0% of the time, Pallas kernels for 8%

profile of v7, /device:TPU:0, one launch (start us, length us, event | category | flops | bytes accessed | tf_op | source)
XLA Modules:
  0.0 51.6 jit_solution(8584801500107055595)
XLA Ops:
  0.6 0.0 copy-start.3
  0.6 0.0 copy-start
  0.7 1.4 %pack.1 = bf16[32,8,1024]{2,1,0:T(8,128)(2,1)S(1)} custom-call(bf16[64,4,512]{2,1,0:T(4,128)(2,1)} %bitcast.9, bf16[64,4,512]{2,1,0:T(4,128)(2,1)} %bitcast.11), custom_call_target="tpu_custom_call" | custom-call | tf_op jit(solution)/shard_map/pack/pallas_call | solution.py:36
  2.0 22.2 %all_to_all.10 = bf16[32,8,1024]{2,1,0:T(8,128)(2,1)S(1)} all-to-all(bf16[32,8,1024]{2,1,0:T(8,128)(2,1)S(1)} %pack.1), channel_id=1, replica_groups={{0,8,16,24,4,12,20,28,1,9,17,25,5,13,21,29,2,10,18,26,6,14,22,30,3,11,1..., dimensions={0} | all-to-all | bytes 1048576 | tf_op jit(solution)/shard_map/all_to_all | solution.py:285
  24.2 0.0 copy-done.3
  24.2 1.7 %first_heads.1 = (bf16[256,768]{1,0:T(8,128)(2,1)S(1)}, bf16[256,512]{1,0:T(8,128)(2,1)S(1)}, bf16[512,768]{1,0:T(8,128)(2,1)S(1)}) custom-call(s32[1,256]{1,0:T(1,128)S(1)} %copy-done.3, bf16[256,1024]{1,0:T(8,128)(2,1)S(1)} %bitcast.7, bf16[512,1536]{1,0:T(8,128)(2,1)S(1)} %copy-done), custom_call_target="tpu_custom_call" | custom-call | tf_op jit(solution)/shard_map/first_heads/pallas_call | solution.py:36
  25.9 0.1 collective-permute-start
  26.0 1.8 %second_heads.1 = (bf16[256,512]{1,0:T(8,128)(2,1)S(1)}, bf16[512,768]{1,0:T(8,128)(2,1)S(1)}) custom-call(s32[1,256]{1,0:T(1,128)S(1)} %copy-done.3, bf16[256,1024]{1,0:T(8,128)(2,1)S(1)} %bitcast.8, bf16[512,1536]{1,0:T(8,128)(2,1)S(1)} %copy-done, bf16[256,768]{1,0:T(8,128)(2,1)S(1)} %get-tuple-element.15.first_ref, ...), custom_call_target="tpu_custom_call" | custom-call | tf_op jit(solution)/shard_map/second_heads/pallas_call | solution.py:36
  27.8 0.4 collective-permute-done
  28.2 0.2 split_tx.1
  28.4 1.5 %collective-permute-start.1 = (bf16[4,32,768]{2,1,0:T(8,128)(2,1)S(1)}, bf16[4,32,768]{2,1,0:T(8,128)(2,1)S(1)}, u32[]{:S(2)}, u32[]{:S(2)}) collective-permute-start(bf16[4,32,768]{2,1,0:T(8,128)(2,1)S(1)} %get-tuple-element.21), channel_id=1, source_target_pairs={{0,1},{1,0},{2,3},{3,2},{4,5},{5,4},{6,7},{7,6},{8,9},{9,8},{10,11... | collective-permute-start | bytes 589832 | tf_op jit(solution)/shard_map/ppermute | solution.py:222
  30.0 0.8 %collective-permute-start.2 = (bf16[4,32,768]{2,1,0:T(8,128)(2,1)S(1)}, bf16[4,32,768]{2,1,0:T(8,128)(2,1)S(1)}, u32[]{:S(2)}, u32[]{:S(2)}) collective-permute-start(bf16[4,32,768]{2,1,0:T(8,128)(2,1)S(1)} %get-tuple-element.22), channel_id=1, source_target_pairs={{0,2},{1,3},{2,0},{3,1},{4,6},{5,7},{6,4},{7,5},{8,10},{9,11},{10,... | collective-permute-start | bytes 589832 | tf_op jit(solution)/shard_map/ppermute | solution.py:222
  30.8 1.2 %collective-permute-start.3 = (bf16[4,32,768]{2,1,0:T(8,128)(2,1)S(1)}, bf16[4,32,768]{2,1,0:T(8,128)(2,1)S(1)}, u32[]{:S(2)}, u32[]{:S(2)}) collective-permute-start(bf16[4,32,768]{2,1,0:T(8,128)(2,1)S(1)} %get-tuple-element.23), channel_id=1, source_target_pairs={{0,3},{1,2},{2,1},{3,0},{4,7},{5,6},{6,5},{7,4},{8,11},{9,10},{10,... | collective-permute-start | bytes 589832 | tf_op jit(solution)/shard_map/ppermute | solution.py:222
  32.0 1.0 %spread.1 = bf16[256,512]{1,0:T(8,128)(2,1)} custom-call(s32[1,256]{1,0:T(1,128)S(1)} %copy-done.3, bf16[256,512]{1,0:T(8,128)(2,1)S(1)} %get-tuple-element.17.grad_ref), custom_call_target="tpu_custom_call" | custom-call | tf_op jit(solution)/shard_map/spread/pallas_call | solution.py:36
  32.9 3.0 %all-to-all-start.1 = ((bf16[32,8,512]{2,1,0:T(8,128)(2,1)}), bf16[32,8,512]{2,1,0:T(8,128)(2,1)S(1)}, u32[]{:S(2)}, u32[]{:S(2)}) async-start(bf16[32,8,512]{2,1,0:T(8,128)(2,1)} %bitcast.3), calls=%async_computation.1 | async-start | bytes 524288 | tf_op jit(solution)/shard_map/all_to_all | solution.py:326
  35.9 0.3 collective-permute-done.1.refs_1_
  36.2 5.8 %collective-permute-done.2.refs_2_ = bf16[4,32,768]{2,1,0:T(8,128)(2,1)S(1)} collective-permute-done((bf16[4,32,768]{2,1,0:T(8,128)(2,1)S(1)}, bf16[4,32,768]{2,1,0:T(8,128)(2,1)S(1)}, u32[]{:S(2)}, u32[]{:S(2)}) %collective-permute-start.2) | collective-permute-done | bytes 196640 | tf_op jit(solution)/shard_map/ppermute | solution.py:222
  42.1 0.0 collective-permute-done.3.refs_3_
  42.1 0.1 split_ty.1
  42.2 1.2 %collective-permute-start.4 = (bf16[32,768]{1,0:T(8,128)(2,1)S(1)}, bf16[32,768]{1,0:T(8,128)(2,1)S(1)}, u32[]{:S(2)}, u32[]{:S(2)}) collective-permute-start(bf16[32,768]{1,0:T(8,128)(2,1)S(1)} %get-tuple-element.25), channel_id=1, source_target_pairs={{0,4},{4,0},{8,12},{12,8},{1,5},{5,1},{9,13},{13,9},{2,6},{6,2},{1... | collective-permute-start | bytes 147464 | tf_op jit(solution)/shard_map/ppermute | solution.py:222
  43.4 0.0 collective-permute-start.5
  43.4 3.2 %collective-permute-start.6 = (bf16[32,768]{1,0:T(8,128)(2,1)S(1)}, bf16[32,768]{1,0:T(8,128)(2,1)S(1)}, u32[]{:S(2)}, u32[]{:S(2)}) collective-permute-start(bf16[32,768]{1,0:T(8,128)(2,1)S(1)} %get-tuple-element.27), channel_id=1, source_target_pairs={{0,12},{4,8},{8,4},{12,0},{1,13},{5,9},{9,5},{13,1},{2,14},{6,10},... | collective-permute-start | bytes 147464 | tf_op jit(solution)/shard_map/ppermute | solution.py:222
  46.6 0.0 collective-permute-done.4
  46.7 2.8 %collective-permute-done.5 = bf16[32,768]{1,0:T(8,128)(2,1)S(1)} collective-permute-done((bf16[32,768]{1,0:T(8,128)(2,1)S(1)}, bf16[32,768]{1,0:T(8,128)(2,1)S(1)}, u32[]{:S(2)}, u32[]{:S(2)}) %collective-permute-start.5) | collective-permute-done | bytes 49184 | tf_op jit(solution)/shard_map/ppermute | solution.py:222
  49.5 0.0 collective-permute-done.6
  49.5 0.1 collective-permute-start.7
  49.6 0.0 all-to-all-done.1.returned_ref
  49.6 0.0 copy-done.1
  49.6 0.0 copy-done.2
  49.6 1.1 %token_grad.1 = bf16[64,4,512]{2,1,0:T(4,128)(2,1)} custom-call(bf16[32,8,512]{2,1,0:T(8,128)(2,1)S(1)} %all-to-all-done.1.returned_ref, bf16[64,4,512]{2,1,0:T(4,128)(2,1)S(1)} %bitcast.10, bf16[64,4,512]{2,1,0:T(4,128)(2,1)S(1)} %bitcast.12), custom_call_target="tpu_custom_call" | custom-call | tf_op jit(solution)/shard_map/token_grad/pallas_call | solution.py:36
  50.7 0.1 collective-permute-done.7.other_ref
  50.9 0.7 %weight_grad.1 = f32[32,1536]{1,0:T(8,128)} custom-call(f32[32,768]{1,0:T(8,128)S(1)} %add_multiply_fusion.own_ref, f32[32,768]{1,0:T(8,128)S(1)} %collective-permute-done.7.other_ref), custom_call_target="tpu_custom_call" | custom-call | tf_op jit(solution)/shard_map/weight_grad/pallas_call | solution.py:36
  (4 shorter events, 0.0 us)
Async XLA Ops:
  0.6 23.6 %copy-start.3 = (s32[1,256]{1,0:T(1,128)S(1)}, s32[1,256]{1,0:T(1,128)}, u32[]{:S(2)}) copy-start(s32[1,256]{1,0:T(1,128)} %constant.5.clone.pos_ref) | copy-start | bytes 3076
  0.6 23.6 %copy-start = (bf16[512,1536]{1,0:T(8,128)(2,1)S(1)}, bf16[512,1536]{1,0:T(8,128)(2,1)}, u32[]{:S(2)}) copy-start(bf16[512,1536]{1,0:T(8,128)(2,1)} %weight_ref.3) | copy-start | bytes 4718596
  25.9 2.4 %collective-permute-start = (bf16[512,768]{1,0:T(8,128)(2,1)S(1)}, bf16[512,768]{1,0:T(8,128)(2,1)S(1)}, u32[]{:S(2)}, u32[]{:S(2)}) collective-permute-start(bf16[512,768]{1,0:T(8,128)(2,1)S(1)} %get-tuple-element.19), channel_id=1, source_target_pairs={{0,16},{16,0},{1,17},{17,1},{2,18},{18,2},{3,19},{19,3},{4,20},{20... | collective-permute-start | bytes 2359304 | tf_op jit(solution)/shard_map/ppermute | solution.py:201
  28.2 21.4 %copy-start.1 = (bf16[1,64,4,512]{3,2,1,0:T(4,128)(2,1)S(1)}, bf16[1,64,4,512]{3,2,1,0:T(4,128)(2,1)}, u32[]{:S(2)}) copy-start(bf16[1,64,4,512]{3,2,1,0:T(4,128)(2,1)} %param.4) | copy-start | bytes 786436
  28.2 21.4 %copy-start.2 = (bf16[1,64,4,512]{3,2,1,0:T(4,128)(2,1)S(1)}, bf16[1,64,4,512]{3,2,1,0:T(4,128)(2,1)}, u32[]{:S(2)}) copy-start(bf16[1,64,4,512]{3,2,1,0:T(4,128)(2,1)} %param.6) | copy-start | bytes 786436
  28.4 7.8 %collective-permute-start.1 = (bf16[4,32,768]{2,1,0:T(8,128)(2,1)S(1)}, bf16[4,32,768]{2,1,0:T(8,128)(2,1)S(1)}, u32[]{:S(2)}, u32[]{:S(2)}) collective-permute-start(bf16[4,32,768]{2,1,0:T(8,128)(2,1)S(1)} %get-tuple-element.21), channel_id=1, source_target_pairs={{0,1},{1,0},{2,3},{3,2},{4,5},{5,4},{6,7},{7,6},{8,9},{9,8},{10,11... | collective-permute-start | bytes 589832 | tf_op jit(solution)/shard_map/ppermute | solution.py:222
  30.0 12.1 %collective-permute-start.2 = (bf16[4,32,768]{2,1,0:T(8,128)(2,1)S(1)}, bf16[4,32,768]{2,1,0:T(8,128)(2,1)S(1)}, u32[]{:S(2)}, u32[]{:S(2)}) collective-permute-start(bf16[4,32,768]{2,1,0:T(8,128)(2,1)S(1)} %get-tuple-element.22), channel_id=1, source_target_pairs={{0,2},{1,3},{2,0},{3,1},{4,6},{5,7},{6,4},{7,5},{8,10},{9,11},{10,... | collective-permute-start | bytes 589832 | tf_op jit(solution)/shard_map/ppermute | solution.py:222
  30.8 11.3 %collective-permute-start.3 = (bf16[4,32,768]{2,1,0:T(8,128)(2,1)S(1)}, bf16[4,32,768]{2,1,0:T(8,128)(2,1)S(1)}, u32[]{:S(2)}, u32[]{:S(2)}) collective-permute-start(bf16[4,32,768]{2,1,0:T(8,128)(2,1)S(1)} %get-tuple-element.23), channel_id=1, source_target_pairs={{0,3},{1,2},{2,1},{3,0},{4,7},{5,6},{6,5},{7,4},{8,11},{9,10},{10,... | collective-permute-start | bytes 589832 | tf_op jit(solution)/shard_map/ppermute | solution.py:222
  32.9 16.6 %all-to-all-start.1 = ((bf16[32,8,512]{2,1,0:T(8,128)(2,1)}), bf16[32,8,512]{2,1,0:T(8,128)(2,1)S(1)}, u32[]{:S(2)}, u32[]{:S(2)}) async-start(bf16[32,8,512]{2,1,0:T(8,128)(2,1)} %bitcast.3), calls=%async_computation.1 | async-start | bytes 524288 | tf_op jit(solution)/shard_map/all_to_all | solution.py:326
  42.2 4.5 %collective-permute-start.4 = (bf16[32,768]{1,0:T(8,128)(2,1)S(1)}, bf16[32,768]{1,0:T(8,128)(2,1)S(1)}, u32[]{:S(2)}, u32[]{:S(2)}) collective-permute-start(bf16[32,768]{1,0:T(8,128)(2,1)S(1)} %get-tuple-element.25), channel_id=1, source_target_pairs={{0,4},{4,0},{8,12},{12,8},{1,5},{5,1},{9,13},{13,9},{2,6},{6,2},{1... | collective-permute-start | bytes 147464 | tf_op jit(solution)/shard_map/ppermute | solution.py:222
  43.4 6.0 %collective-permute-start.5 = (bf16[32,768]{1,0:T(8,128)(2,1)S(1)}, bf16[32,768]{1,0:T(8,128)(2,1)S(1)}, u32[]{:S(2)}, u32[]{:S(2)}) collective-permute-start(bf16[32,768]{1,0:T(8,128)(2,1)S(1)} %get-tuple-element.26), channel_id=1, source_target_pairs={{0,8},{4,12},{8,0},{12,4},{1,9},{5,13},{9,1},{13,5},{2,10},{6,14},... | collective-permute-start | bytes 147464 | tf_op jit(solution)/shard_map/ppermute | solution.py:222
  43.4 6.0 %collective-permute-start.6 = (bf16[32,768]{1,0:T(8,128)(2,1)S(1)}, bf16[32,768]{1,0:T(8,128)(2,1)S(1)}, u32[]{:S(2)}, u32[]{:S(2)}) collective-permute-start(bf16[32,768]{1,0:T(8,128)(2,1)S(1)} %get-tuple-element.27), channel_id=1, source_target_pairs={{0,12},{4,8},{8,4},{12,0},{1,13},{5,9},{9,5},{13,1},{2,14},{6,10},... | collective-permute-start | bytes 147464 | tf_op jit(solution)/shard_map/ppermute | solution.py:222
  49.5 1.4 %collective-permute-start.7 = (f32[32,768]{1,0:T(8,128)S(1)}, f32[32,768]{1,0:T(8,128)S(1)}, u32[]{:S(2)}, u32[]{:S(2)}) collective-permute-start(f32[32,768]{1,0:T(8,128)S(1)} %add_multiply_fusion.own_ref), channel_id=1, source_target_pairs={{0,16},{16,0},{1,17},{17,1},{2,18},{18,2},{3,19},{19,3},{4,20},{20... | collective-permute-start | bytes 294920 | tf_op jit(solution)/shard_map/ppermute | solution.py:201

commit v8 on v7

--- a/solution.py
+++ b/solution.py
@@ -8,7 +8,6 @@
 from jax.experimental.pallas import tpu as pltpu
 from jax.sharding import PartitionSpec as P
 
-HEADS = 16
 HEAD_DIM = 32
 GRID = 8
 EPS = 1e-05
@@ -118,10 +117,11 @@
     ]
     for first in range(0, len(cells), GROUP):
         group = cells[first : first + GROUP]
+        stacks = [(stack(query_ref[row, col]), stack(cot_ref[row, col])) for row, col in group]
         raw = []
-        for row, col in group:
-            scores = matmul(key_ref[row, col], stack(query_ref[row, col]), (1, 1))
-            attn_grad = matmul(value_ref[row, col], stack(cot_ref[row, col]), (1, 1))
+        for (row, col), (queries, cots) in zip(group, stacks):
+            scores = matmul(key_ref[row, col], queries, (1, 1))
+            attn_grad = matmul(value_ref[row, col], cots, (1, 1))
             raw.append((scores, attn_grad))
         low = []
         for scores, attn_grad in raw:
@@ -129,9 +129,9 @@
             probs = exponent * (1.0 / jnp.sum(exponent, axis=0, keepdims=True))
             score_grad = probs * (attn_grad - jnp.sum(probs * attn_grad, axis=0, keepdims=True))
             low.append((probs.astype(BF16), score_grad.astype(BF16)))
-        for (row, col), (probs, score_grad) in zip(group, low):
-            value_grad = matmul(probs, stack(cot_ref[row, col]), (1, 0))
-            key_grad = matmul(score_grad, stack(query_ref[row, col]), (1, 0))
+        for (row, col), (probs, score_grad), (queries, cots) in zip(group, low, stacks):
+            value_grad = matmul(probs, cots, (1, 0))
+            key_grad = matmul(score_grad, queries, (1, 0))
             spread = matmul(score_grad, key_ref[row, col], (0, 0)) * mask
             query_grad = spread[:win_tokens]
             for head in range(1, BLOCK_HEADS):
@@ -316,7 +316,7 @@
             mib=16,
         )
         near = tuple(range(col_tiles))
-        far = (0, 1, 2, 3)
+        far = tuple(range(row_tiles))
         shape = (row_tiles, col_tiles, channels // tile_count, 3 * width)
         parts = split("tx", 1, near, "split_tx", keep.reshape(shape), swap_reps(send).reshape(shape))
     else:

time: 51.8 us -> 51.8 us (level)
  no operation moved by 1% of the time
where the time goes in v8:
time: 51.8 us; the launch traced here: 51.5 us
  blocking collectives  22.2 us (43%)
  starting transfers between devices  11.2 us (22%)
  waiting for transfers between devices  9.56 us (18%)
  Pallas kernels  7.87 us (15%)
  between operations  0.73 us (1%)
    all_to_all x1, blocking collectives, shards(): pixels = exchange(sent)  22.2 us
    ppermute x6, waiting for transfers between devices, travel(): lax.ppermute(part, axis, [(i, i ^ step) for i in range(size)])  8.96 us
    ppermute x6, starting transfers between devices, travel(): lax.ppermute(part, axis, [(i, i ^ step) for i in range(size)])  8.01 us
    pallas_call x8, Pallas kernels, vmem_call(): pl.pallas_call(kernel, out_shape=outs, in_specs=[hbm if index in remote e...  7.87 us
    all_to_all x1, starting transfers between devices, shards(): returned = exchange(spread)  3 us
  transfers between devices with their start and end apart: 9, of which 5 were waited for; matrix products, arithmetic and copies ran while one was open for 0% of the time, Pallas kernels for 8%

profile of v8, /device:TPU:0, one launch (start us, length us, event | category | flops | bytes accessed | tf_op | source)
XLA Modules:
  0.0 51.5 jit_solution(16495781690222070370)
XLA Ops:
  0.6 0.0 copy-start.3
  0.6 0.0 copy-start
  0.7 1.4 %pack.1 = bf16[32,8,1024]{2,1,0:T(8,128)(2,1)S(1)} custom-call(bf16[64,4,512]{2,1,0:T(4,128)(2,1)} %bitcast.9, bf16[64,4,512]{2,1,0:T(4,128)(2,1)} %bitcast.11), custom_call_target="tpu_custom_call" | custom-call | tf_op jit(solution)/shard_map/pack/pallas_call | solution.py:35
  2.0 22.2 %all_to_all.10 = bf16[32,8,1024]{2,1,0:T(8,128)(2,1)S(1)} all-to-all(bf16[32,8,1024]{2,1,0:T(8,128)(2,1)S(1)} %pack.1), channel_id=1, replica_groups={{0,8,16,24,4,12,20,28,1,9,17,25,5,13,21,29,2,10,18,26,6,14,22,30,3,11,1..., dimensions={0} | all-to-all | bytes 1048576 | tf_op jit(solution)/shard_map/all_to_all | solution.py:285
  24.2 0.0 copy-done.3
  24.2 0.0 copy-done
  24.2 1.6 %first_heads.1 = (bf16[256,768]{1,0:T(8,128)(2,1)S(1)}, bf16[256,512]{1,0:T(8,128)(2,1)S(1)}, bf16[512,768]{1,0:T(8,128)(2,1)S(1)}) custom-call(s32[1,256]{1,0:T(1,128)S(1)} %copy-done.3, bf16[256,1024]{1,0:T(8,128)(2,1)S(1)} %bitcast.7, bf16[512,1536]{1,0:T(8,128)(2,1)S(1)} %copy-done), custom_call_target="tpu_custom_call" | custom-call | tf_op jit(solution)/shard_map/first_heads/pallas_call | solution.py:35
  25.9 0.1 collective-permute-start
  25.9 1.8 %second_heads.1 = (bf16[256,512]{1,0:T(8,128)(2,1)S(1)}, bf16[512,768]{1,0:T(8,128)(2,1)S(1)}) custom-call(s32[1,256]{1,0:T(1,128)S(1)} %copy-done.3, bf16[256,1024]{1,0:T(8,128)(2,1)S(1)} %bitcast.8, bf16[512,1536]{1,0:T(8,128)(2,1)S(1)} %copy-done, bf16[256,768]{1,0:T(8,128)(2,1)S(1)} %get-tuple-element.15.first_ref, ...), custom_call_target="tpu_custom_call" | custom-call | tf_op jit(solution)/shard_map/second_heads/pallas_call | solution.py:35
  27.8 0.5 collective-permute-done
  28.2 0.2 split_tx.1
  28.4 1.5 %collective-permute-start.1 = (bf16[4,32,768]{2,1,0:T(8,128)(2,1)S(1)}, bf16[4,32,768]{2,1,0:T(8,128)(2,1)S(1)}, u32[]{:S(2)}, u32[]{:S(2)}) collective-permute-start(bf16[4,32,768]{2,1,0:T(8,128)(2,1)S(1)} %get-tuple-element.21), channel_id=1, source_target_pairs={{0,1},{1,0},{2,3},{3,2},{4,5},{5,4},{6,7},{7,6},{8,9},{9,8},{10,11... | collective-permute-start | bytes 589832 | tf_op jit(solution)/shard_map/ppermute | solution.py:222
  29.9 0.8 %collective-permute-start.2 = (bf16[4,32,768]{2,1,0:T(8,128)(2,1)S(1)}, bf16[4,32,768]{2,1,0:T(8,128)(2,1)S(1)}, u32[]{:S(2)}, u32[]{:S(2)}) collective-permute-start(bf16[4,32,768]{2,1,0:T(8,128)(2,1)S(1)} %get-tuple-element.22), channel_id=1, source_target_pairs={{0,2},{1,3},{2,0},{3,1},{4,6},{5,7},{6,4},{7,5},{8,10},{9,11},{10,... | collective-permute-start | bytes 589832 | tf_op jit(solution)/shard_map/ppermute | solution.py:222
  30.8 1.2 %collective-permute-start.3 = (bf16[4,32,768]{2,1,0:T(8,128)(2,1)S(1)}, bf16[4,32,768]{2,1,0:T(8,128)(2,1)S(1)}, u32[]{:S(2)}, u32[]{:S(2)}) collective-permute-start(bf16[4,32,768]{2,1,0:T(8,128)(2,1)S(1)} %get-tuple-element.23), channel_id=1, source_target_pairs={{0,3},{1,2},{2,1},{3,0},{4,7},{5,6},{6,5},{7,4},{8,11},{9,10},{10,... | collective-permute-start | bytes 589832 | tf_op jit(solution)/shard_map/ppermute | solution.py:222
  32.0 1.0 %spread.1 = bf16[256,512]{1,0:T(8,128)(2,1)} custom-call(s32[1,256]{1,0:T(1,128)S(1)} %copy-done.3, bf16[256,512]{1,0:T(8,128)(2,1)S(1)} %get-tuple-element.17.grad_ref), custom_call_target="tpu_custom_call" | custom-call | tf_op jit(solution)/shard_map/spread/pallas_call | solution.py:35
  32.9 3.0 %all-to-all-start.1 = ((bf16[32,8,512]{2,1,0:T(8,128)(2,1)}), bf16[32,8,512]{2,1,0:T(8,128)(2,1)S(1)}, u32[]{:S(2)}, u32[]{:S(2)}) async-start(bf16[32,8,512]{2,1,0:T(8,128)(2,1)} %bitcast.3), calls=%async_computation.1 | async-start | bytes 524288 | tf_op jit(solution)/shard_map/all_to_all | solution.py:326
  35.9 0.3 collective-permute-done.1.refs_1_
  36.2 5.8 %collective-permute-done.2.refs_2_ = bf16[4,32,768]{2,1,0:T(8,128)(2,1)S(1)} collective-permute-done((bf16[4,32,768]{2,1,0:T(8,128)(2,1)S(1)}, bf16[4,32,768]{2,1,0:T(8,128)(2,1)S(1)}, u32[]{:S(2)}, u32[]{:S(2)}) %collective-permute-start.2) | collective-permute-done | bytes 196640 | tf_op jit(solution)/shard_map/ppermute | solution.py:222
  42.1 0.0 collective-permute-done.3.refs_3_
  42.1 0.1 split_ty.1
  42.2 1.2 %collective-permute-start.4 = (bf16[32,768]{1,0:T(8,128)(2,1)S(1)}, bf16[32,768]{1,0:T(8,128)(2,1)S(1)}, u32[]{:S(2)}, u32[]{:S(2)}) collective-permute-start(bf16[32,768]{1,0:T(8,128)(2,1)S(1)} %get-tuple-element.25), channel_id=1, source_target_pairs={{0,4},{4,0},{8,12},{12,8},{1,5},{5,1},{9,13},{13,9},{2,6},{6,2},{1... | collective-permute-start | bytes 147464 | tf_op jit(solution)/shard_map/ppermute | solution.py:222
  43.4 0.0 collective-permute-start.5
  43.4 3.2 %collective-permute-start.6 = (bf16[32,768]{1,0:T(8,128)(2,1)S(1)}, bf16[32,768]{1,0:T(8,128)(2,1)S(1)}, u32[]{:S(2)}, u32[]{:S(2)}) collective-permute-start(bf16[32,768]{1,0:T(8,128)(2,1)S(1)} %get-tuple-element.27), channel_id=1, source_target_pairs={{0,12},{4,8},{8,4},{12,0},{1,13},{5,9},{9,5},{13,1},{2,14},{6,10},... | collective-permute-start | bytes 147464 | tf_op jit(solution)/shard_map/ppermute | solution.py:222
  46.6 0.0 collective-permute-done.4
  46.6 2.8 %collective-permute-done.5 = bf16[32,768]{1,0:T(8,128)(2,1)S(1)} collective-permute-done((bf16[32,768]{1,0:T(8,128)(2,1)S(1)}, bf16[32,768]{1,0:T(8,128)(2,1)S(1)}, u32[]{:S(2)}, u32[]{:S(2)}) %collective-permute-start.5) | collective-permute-done | bytes 49184 | tf_op jit(solution)/shard_map/ppermute | solution.py:222
  49.4 0.0 collective-permute-done.6
  49.5 0.1 collective-permute-start.7
  49.6 0.0 all-to-all-done.1.returned_ref
  49.6 0.0 copy-done.1
  49.6 1.1 %token_grad.1 = bf16[64,4,512]{2,1,0:T(4,128)(2,1)} custom-call(bf16[32,8,512]{2,1,0:T(8,128)(2,1)S(1)} %all-to-all-done.1.returned_ref, bf16[64,4,512]{2,1,0:T(4,128)(2,1)S(1)} %bitcast.10, bf16[64,4,512]{2,1,0:T(4,128)(2,1)S(1)} %bitcast.12), custom_call_target="tpu_custom_call" | custom-call | tf_op jit(solution)/shard_map/token_grad/pallas_call | solution.py:35
  50.7 0.1 collective-permute-done.7.other_ref
  50.8 0.7 %weight_grad.1 = f32[32,1536]{1,0:T(8,128)} custom-call(f32[32,768]{1,0:T(8,128)S(1)} %add_multiply_fusion.own_ref, f32[32,768]{1,0:T(8,128)S(1)} %collective-permute-done.7.other_ref), custom_call_target="tpu_custom_call" | custom-call | tf_op jit(solution)/shard_map/weight_grad/pallas_call | solution.py:35
  (4 shorter events, 0.0 us)
Async XLA Ops:
  0.6 23.6 %copy-start.3 = (s32[1,256]{1,0:T(1,128)S(1)}, s32[1,256]{1,0:T(1,128)}, u32[]{:S(2)}) copy-start(s32[1,256]{1,0:T(1,128)} %constant.5.clone.pos_ref) | copy-start | bytes 3076
  0.6 23.6 %copy-start = (bf16[512,1536]{1,0:T(8,128)(2,1)S(1)}, bf16[512,1536]{1,0:T(8,128)(2,1)}, u32[]{:S(2)}) copy-start(bf16[512,1536]{1,0:T(8,128)(2,1)} %weight_ref.3) | copy-start | bytes 4718596
  25.9 2.4 %collective-permute-start = (bf16[512,768]{1,0:T(8,128)(2,1)S(1)}, bf16[512,768]{1,0:T(8,128)(2,1)S(1)}, u32[]{:S(2)}, u32[]{:S(2)}) collective-permute-start(bf16[512,768]{1,0:T(8,128)(2,1)S(1)} %get-tuple-element.19), channel_id=1, source_target_pairs={{0,16},{16,0},{1,17},{17,1},{2,18},{18,2},{3,19},{19,3},{4,20},{20... | collective-permute-start | bytes 2359304 | tf_op jit(solution)/shard_map/ppermute | solution.py:201
  28.2 21.4 %copy-start.1 = (bf16[1,64,4,512]{3,2,1,0:T(4,128)(2,1)S(1)}, bf16[1,64,4,512]{3,2,1,0:T(4,128)(2,1)}, u32[]{:S(2)}) copy-start(bf16[1,64,4,512]{3,2,1,0:T(4,128)(2,1)} %param.4) | copy-start | bytes 786436
  28.2 21.4 %copy-start.2 = (bf16[1,64,4,512]{3,2,1,0:T(4,128)(2,1)S(1)}, bf16[1,64,4,512]{3,2,1,0:T(4,128)(2,1)}, u32[]{:S(2)}) copy-start(bf16[1,64,4,512]{3,2,1,0:T(4,128)(2,1)} %param.6) | copy-start | bytes 786436
  28.4 7.8 %collective-permute-start.1 = (bf16[4,32,768]{2,1,0:T(8,128)(2,1)S(1)}, bf16[4,32,768]{2,1,0:T(8,128)(2,1)S(1)}, u32[]{:S(2)}, u32[]{:S(2)}) collective-permute-start(bf16[4,32,768]{2,1,0:T(8,128)(2,1)S(1)} %get-tuple-element.21), channel_id=1, source_target_pairs={{0,1},{1,0},{2,3},{3,2},{4,5},{5,4},{6,7},{7,6},{8,9},{9,8},{10,11... | collective-permute-start | bytes 589832 | tf_op jit(solution)/shard_map/ppermute | solution.py:222
  29.9 12.1 %collective-permute-start.2 = (bf16[4,32,768]{2,1,0:T(8,128)(2,1)S(1)}, bf16[4,32,768]{2,1,0:T(8,128)(2,1)S(1)}, u32[]{:S(2)}, u32[]{:S(2)}) collective-permute-start(bf16[4,32,768]{2,1,0:T(8,128)(2,1)S(1)} %get-tuple-element.22), channel_id=1, source_target_pairs={{0,2},{1,3},{2,0},{3,1},{4,6},{5,7},{6,4},{7,5},{8,10},{9,11},{10,... | collective-permute-start | bytes 589832 | tf_op jit(solution)/shard_map/ppermute | solution.py:222
  30.8 11.3 %collective-permute-start.3 = (bf16[4,32,768]{2,1,0:T(8,128)(2,1)S(1)}, bf16[4,32,768]{2,1,0:T(8,128)(2,1)S(1)}, u32[]{:S(2)}, u32[]{:S(2)}) collective-permute-start(bf16[4,32,768]{2,1,0:T(8,128)(2,1)S(1)} %get-tuple-element.23), channel_id=1, source_target_pairs={{0,3},{1,2},{2,1},{3,0},{4,7},{5,6},{6,5},{7,4},{8,11},{9,10},{10,... | collective-permute-start | bytes 589832 | tf_op jit(solution)/shard_map/ppermute | solution.py:222
  32.9 16.6 %all-to-all-start.1 = ((bf16[32,8,512]{2,1,0:T(8,128)(2,1)}), bf16[32,8,512]{2,1,0:T(8,128)(2,1)S(1)}, u32[]{:S(2)}, u32[]{:S(2)}) async-start(bf16[32,8,512]{2,1,0:T(8,128)(2,1)} %bitcast.3), calls=%async_computation.1 | async-start | bytes 524288 | tf_op jit(solution)/shard_map/all_to_all | solution.py:326
  42.2 4.5 %collective-permute-start.4 = (bf16[32,768]{1,0:T(8,128)(2,1)S(1)}, bf16[32,768]{1,0:T(8,128)(2,1)S(1)}, u32[]{:S(2)}, u32[]{:S(2)}) collective-permute-start(bf16[32,768]{1,0:T(8,128)(2,1)S(1)} %get-tuple-element.25), channel_id=1, source_target_pairs={{0,4},{4,0},{8,12},{12,8},{1,5},{5,1},{9,13},{13,9},{2,6},{6,2},{1... | collective-permute-start | bytes 147464 | tf_op jit(solution)/shard_map/ppermute | solution.py:222
  43.4 6.0 %collective-permute-start.5 = (bf16[32,768]{1,0:T(8,128)(2,1)S(1)}, bf16[32,768]{1,0:T(8,128)(2,1)S(1)}, u32[]{:S(2)}, u32[]{:S(2)}) collective-permute-start(bf16[32,768]{1,0:T(8,128)(2,1)S(1)} %get-tuple-element.26), channel_id=1, source_target_pairs={{0,8},{4,12},{8,0},{12,4},{1,9},{5,13},{9,1},{13,5},{2,10},{6,14},... | collective-permute-start | bytes 147464 | tf_op jit(solution)/shard_map/ppermute | solution.py:222
  43.4 6.0 %collective-permute-start.6 = (bf16[32,768]{1,0:T(8,128)(2,1)S(1)}, bf16[32,768]{1,0:T(8,128)(2,1)S(1)}, u32[]{:S(2)}, u32[]{:S(2)}) collective-permute-start(bf16[32,768]{1,0:T(8,128)(2,1)S(1)} %get-tuple-element.27), channel_id=1, source_target_pairs={{0,12},{4,8},{8,4},{12,0},{1,13},{5,9},{9,5},{13,1},{2,14},{6,10},... | collective-permute-start | bytes 147464 | tf_op jit(solution)/shard_map/ppermute | solution.py:222
  49.5 1.4 %collective-permute-start.7 = (f32[32,768]{1,0:T(8,128)S(1)}, f32[32,768]{1,0:T(8,128)S(1)}, u32[]{:S(2)}, u32[]{:S(2)}) collective-permute-start(f32[32,768]{1,0:T(8,128)S(1)} %add_multiply_fusion.own_ref), channel_id=1, source_target_pairs={{0,16},{16,0},{1,17},{17,1},{2,18},{18,2},{3,19},{19,3},{4,20},{20... | collective-permute-start | bytes 294920 | tf_op jit(solution)/shard_map/ppermute | solution.py:201

commit v9 on v8

--- a/solution.py
+++ b/solution.py
@@ -240,7 +240,7 @@
     group_count = tile_count * samples
     digits = {"rep": samples, "z": row_tiles // 2, "row": 2, "y": col_tiles // 2, "column": 2}
     natural = list(digits)
-    turned = ["y", "column", "row", "rep", "z"] if samples == 2 else natural
+    turned = ["column", "y", "row", "rep", "z"] if samples == 2 else natural
     devices = np.arange(group_count).reshape(list(digits.values()))
     devices = devices.transpose([natural.index(name) for name in turned]).reshape(-1).tolist()
     groups = [[rep * tile_count + device for device in devices] for rep in range(rep_count // samples)]

time: 51.8 us -> 51.7 us (level)
  transfers between devices with their start and end apart: 9 -> 9, of which waited for: 5 -> 7; matrix products, arithmetic and copies ran while one was open for 0% -> 0% of each run, Pallas kernels for 8% -> 8%
where the time goes in v9:
time: 51.7 us; the launch traced here: 51.5 us
  blocking collectives  22.3 us (43%)
  starting transfers between devices  11.1 us (21%)
  waiting for transfers between devices  9.5 us (18%)
  Pallas kernels  7.87 us (15%)
  between operations  0.74 us (1%)
    all_to_all x1, blocking collectives, shards(): pixels = exchange(sent)  22.3 us
    ppermute x6, waiting for transfers between devices, travel(): lax.ppermute(part, axis, [(i, i ^ step) for i in range(size)])  8.9 us
    ppermute x6, starting transfers between devices, travel(): lax.ppermute(part, axis, [(i, i ^ step) for i in range(size)])  8 us
    pallas_call x8, Pallas kernels, vmem_call(): pl.pallas_call(kernel, out_shape=outs, in_specs=[hbm if index in remote e...  7.87 us
    all_to_all x1, starting transfers between devices, shards(): returned = exchange(spread)  2.93 us
  transfers between devices with their start and end apart: 9, of which 7 were waited for; matrix products, arithmetic and copies ran while one was open for 0% of the time, Pallas kernels for 8%

profile of v9, /device:TPU:0, one launch (start us, length us, event | category | flops | bytes accessed | tf_op | source)
XLA Modules:
  0.0 51.5 jit_solution(11168328140308544975)
XLA Ops:
  0.6 0.0 copy-start.3
  0.6 0.0 copy-start
  0.7 1.4 %pack.1 = bf16[32,8,1024]{2,1,0:T(8,128)(2,1)S(1)} custom-call(bf16[64,4,512]{2,1,0:T(4,128)(2,1)} %bitcast.9, bf16[64,4,512]{2,1,0:T(4,128)(2,1)} %bitcast.11), custom_call_target="tpu_custom_call" | custom-call | tf_op jit(solution)/shard_map/pack/pallas_call | solution.py:35
  2.0 22.3 %all_to_all.10 = bf16[32,8,1024]{2,1,0:T(8,128)(2,1)S(1)} all-to-all(bf16[32,8,1024]{2,1,0:T(8,128)(2,1)S(1)} %pack.1), channel_id=1, replica_groups={{0,8,16,24,4,12,20,28,2,10,18,26,6,14,22,30,1,9,17,25,5,13,21,29,3,11,1..., dimensions={0} | all-to-all | bytes 1048576 | tf_op jit(solution)/shard_map/all_to_all | solution.py:285
  24.3 0.0 copy-done.3
  24.3 0.0 copy-done
  24.3 1.6 %first_heads.1 = (bf16[256,768]{1,0:T(8,128)(2,1)S(1)}, bf16[256,512]{1,0:T(8,128)(2,1)S(1)}, bf16[512,768]{1,0:T(8,128)(2,1)S(1)}) custom-call(s32[1,256]{1,0:T(1,128)S(1)} %copy-done.3, bf16[256,1024]{1,0:T(8,128)(2,1)S(1)} %bitcast.7, bf16[512,1536]{1,0:T(8,128)(2,1)S(1)} %copy-done), custom_call_target="tpu_custom_call" | custom-call | tf_op jit(solution)/shard_map/first_heads/pallas_call | solution.py:35
  25.9 0.1 collective-permute-start
  26.0 1.8 %second_heads.1 = (bf16[256,512]{1,0:T(8,128)(2,1)S(1)}, bf16[512,768]{1,0:T(8,128)(2,1)S(1)}) custom-call(s32[1,256]{1,0:T(1,128)S(1)} %copy-done.3, bf16[256,1024]{1,0:T(8,128)(2,1)S(1)} %bitcast.8, bf16[512,1536]{1,0:T(8,128)(2,1)S(1)} %copy-done, bf16[256,768]{1,0:T(8,128)(2,1)S(1)} %get-tuple-element.15.first_ref, ...), custom_call_target="tpu_custom_call" | custom-call | tf_op jit(solution)/shard_map/second_heads/pallas_call | solution.py:35
  27.8 0.5 collective-permute-done
  28.3 0.2 split_tx.1
  28.5 1.5 %collective-permute-start.1 = (bf16[4,32,768]{2,1,0:T(8,128)(2,1)S(1)}, bf16[4,32,768]{2,1,0:T(8,128)(2,1)S(1)}, u32[]{:S(2)}, u32[]{:S(2)}) collective-permute-start(bf16[4,32,768]{2,1,0:T(8,128)(2,1)S(1)} %get-tuple-element.21), channel_id=1, source_target_pairs={{0,1},{1,0},{2,3},{3,2},{4,5},{5,4},{6,7},{7,6},{8,9},{9,8},{10,11... | collective-permute-start | bytes 589832 | tf_op jit(solution)/shard_map/ppermute | solution.py:222
  30.0 0.8 %collective-permute-start.2 = (bf16[4,32,768]{2,1,0:T(8,128)(2,1)S(1)}, bf16[4,32,768]{2,1,0:T(8,128)(2,1)S(1)}, u32[]{:S(2)}, u32[]{:S(2)}) collective-permute-start(bf16[4,32,768]{2,1,0:T(8,128)(2,1)S(1)} %get-tuple-element.22), channel_id=1, source_target_pairs={{0,2},{1,3},{2,0},{3,1},{4,6},{5,7},{6,4},{7,5},{8,10},{9,11},{10,... | collective-permute-start | bytes 589832 | tf_op jit(solution)/shard_map/ppermute | solution.py:222
  30.8 1.3 %collective-permute-start.3 = (bf16[4,32,768]{2,1,0:T(8,128)(2,1)S(1)}, bf16[4,32,768]{2,1,0:T(8,128)(2,1)S(1)}, u32[]{:S(2)}, u32[]{:S(2)}) collective-permute-start(bf16[4,32,768]{2,1,0:T(8,128)(2,1)S(1)} %get-tuple-element.23), channel_id=1, source_target_pairs={{0,3},{1,2},{2,1},{3,0},{4,7},{5,6},{6,5},{7,4},{8,11},{9,10},{10,... | collective-permute-start | bytes 589832 | tf_op jit(solution)/shard_map/ppermute | solution.py:222
  32.0 1.0 %spread.1 = bf16[256,512]{1,0:T(8,128)(2,1)} custom-call(s32[1,256]{1,0:T(1,128)S(1)} %copy-done.3, bf16[256,512]{1,0:T(8,128)(2,1)S(1)} %get-tuple-element.17.grad_ref), custom_call_target="tpu_custom_call" | custom-call | tf_op jit(solution)/shard_map/spread/pallas_call | solution.py:35
  33.0 2.9 %all-to-all-start.1 = ((bf16[32,8,512]{2,1,0:T(8,128)(2,1)}), bf16[32,8,512]{2,1,0:T(8,128)(2,1)S(1)}, u32[]{:S(2)}, u32[]{:S(2)}) async-start(bf16[32,8,512]{2,1,0:T(8,128)(2,1)} %bitcast.3), calls=%async_computation.1 | async-start | bytes 524288 | tf_op jit(solution)/shard_map/all_to_all | solution.py:326
  35.9 0.4 collective-permute-done.1.refs_1_
  36.3 5.8 %collective-permute-done.2.refs_2_ = bf16[4,32,768]{2,1,0:T(8,128)(2,1)S(1)} collective-permute-done((bf16[4,32,768]{2,1,0:T(8,128)(2,1)S(1)}, bf16[4,32,768]{2,1,0:T(8,128)(2,1)S(1)}, u32[]{:S(2)}, u32[]{:S(2)}) %collective-permute-start.2) | collective-permute-done | bytes 196640 | tf_op jit(solution)/shard_map/ppermute | solution.py:222
  42.1 0.0 collective-permute-done.3.refs_3_
  42.1 0.1 split_ty.1
  42.2 0.1 collective-permute-start.4
  42.3 1.0 %collective-permute-start.5 = (bf16[32,768]{1,0:T(8,128)(2,1)S(1)}, bf16[32,768]{1,0:T(8,128)(2,1)S(1)}, u32[]{:S(2)}, u32[]{:S(2)}) collective-permute-start(bf16[32,768]{1,0:T(8,128)(2,1)S(1)} %get-tuple-element.26), channel_id=1, source_target_pairs={{0,8},{4,12},{8,0},{12,4},{1,9},{5,13},{9,1},{13,5},{2,10},{6,14},... | collective-permute-start | bytes 147464 | tf_op jit(solution)/shard_map/ppermute | solution.py:222
  43.3 3.4 %collective-permute-start.6 = (bf16[32,768]{1,0:T(8,128)(2,1)S(1)}, bf16[32,768]{1,0:T(8,128)(2,1)S(1)}, u32[]{:S(2)}, u32[]{:S(2)}) collective-permute-start(bf16[32,768]{1,0:T(8,128)(2,1)S(1)} %get-tuple-element.27), channel_id=1, source_target_pairs={{0,12},{4,8},{8,4},{12,0},{1,13},{5,9},{9,5},{13,1},{2,14},{6,10},... | collective-permute-start | bytes 147464 | tf_op jit(solution)/shard_map/ppermute | solution.py:222
  46.7 0.8 %collective-permute-done.4 = bf16[32,768]{1,0:T(8,128)(2,1)S(1)} collective-permute-done((bf16[32,768]{1,0:T(8,128)(2,1)S(1)}, bf16[32,768]{1,0:T(8,128)(2,1)S(1)}, u32[]{:S(2)}, u32[]{:S(2)}) %collective-permute-start.4) | collective-permute-done | bytes 49184 | tf_op jit(solution)/shard_map/ppermute | solution.py:222
  47.5 0.4 collective-permute-done.5
  47.9 1.4 %collective-permute-done.6 = bf16[32,768]{1,0:T(8,128)(2,1)S(1)} collective-permute-done((bf16[32,768]{1,0:T(8,128)(2,1)S(1)}, bf16[32,768]{1,0:T(8,128)(2,1)S(1)}, u32[]{:S(2)}, u32[]{:S(2)}) %collective-permute-start.6) | collective-permute-done | bytes 49184 | tf_op jit(solution)/shard_map/ppermute | solution.py:222
  49.4 0.1 collective-permute-start.7
  49.5 0.0 all-to-all-done.1.returned_ref
  49.5 0.0 copy-done.1
  49.5 1.1 %token_grad.1 = bf16[64,4,512]{2,1,0:T(4,128)(2,1)} custom-call(bf16[32,8,512]{2,1,0:T(8,128)(2,1)S(1)} %all-to-all-done.1.returned_ref, bf16[64,4,512]{2,1,0:T(4,128)(2,1)S(1)} %bitcast.10, bf16[64,4,512]{2,1,0:T(4,128)(2,1)S(1)} %bitcast.12), custom_call_target="tpu_custom_call" | custom-call | tf_op jit(solution)/shard_map/token_grad/pallas_call | solution.py:35
  50.6 0.1 collective-permute-done.7.other_ref
  50.8 0.7 %weight_grad.1 = f32[32,1536]{1,0:T(8,128)} custom-call(f32[32,768]{1,0:T(8,128)S(1)} %add_multiply_fusion.own_ref, f32[32,768]{1,0:T(8,128)S(1)} %collective-permute-done.7.other_ref), custom_call_target="tpu_custom_call" | custom-call | tf_op jit(solution)/shard_map/weight_grad/pallas_call | solution.py:35
  (4 shorter events, 0.0 us)
Async XLA Ops:
  0.6 23.7 %copy-start.3 = (s32[1,256]{1,0:T(1,128)S(1)}, s32[1,256]{1,0:T(1,128)}, u32[]{:S(2)}) copy-start(s32[1,256]{1,0:T(1,128)} %constant.5.clone.pos_ref) | copy-start | bytes 3076
  0.6 23.7 %copy-start = (bf16[512,1536]{1,0:T(8,128)(2,1)S(1)}, bf16[512,1536]{1,0:T(8,128)(2,1)}, u32[]{:S(2)}) copy-start(bf16[512,1536]{1,0:T(8,128)(2,1)} %weight_ref.3) | copy-start | bytes 4718596
  25.9 2.4 %collective-permute-start = (bf16[512,768]{1,0:T(8,128)(2,1)S(1)}, bf16[512,768]{1,0:T(8,128)(2,1)S(1)}, u32[]{:S(2)}, u32[]{:S(2)}) collective-permute-start(bf16[512,768]{1,0:T(8,128)(2,1)S(1)} %get-tuple-element.19), channel_id=1, source_target_pairs={{0,16},{16,0},{1,17},{17,1},{2,18},{18,2},{3,19},{19,3},{4,20},{20... | collective-permute-start | bytes 2359304 | tf_op jit(solution)/shard_map/ppermute | solution.py:201
  28.3 21.2 %copy-start.1 = (bf16[1,64,4,512]{3,2,1,0:T(4,128)(2,1)S(1)}, bf16[1,64,4,512]{3,2,1,0:T(4,128)(2,1)}, u32[]{:S(2)}) copy-start(bf16[1,64,4,512]{3,2,1,0:T(4,128)(2,1)} %param.4) | copy-start | bytes 786436
  28.3 21.2 %copy-start.2 = (bf16[1,64,4,512]{3,2,1,0:T(4,128)(2,1)S(1)}, bf16[1,64,4,512]{3,2,1,0:T(4,128)(2,1)}, u32[]{:S(2)}) copy-start(bf16[1,64,4,512]{3,2,1,0:T(4,128)(2,1)} %param.6) | copy-start | bytes 786436
  28.5 7.8 %collective-permute-start.1 = (bf16[4,32,768]{2,1,0:T(8,128)(2,1)S(1)}, bf16[4,32,768]{2,1,0:T(8,128)(2,1)S(1)}, u32[]{:S(2)}, u32[]{:S(2)}) collective-permute-start(bf16[4,32,768]{2,1,0:T(8,128)(2,1)S(1)} %get-tuple-element.21), channel_id=1, source_target_pairs={{0,1},{1,0},{2,3},{3,2},{4,5},{5,4},{6,7},{7,6},{8,9},{9,8},{10,11... | collective-permute-start | bytes 589832 | tf_op jit(solution)/shard_map/ppermute | solution.py:222
  30.0 12.2 %collective-permute-start.2 = (bf16[4,32,768]{2,1,0:T(8,128)(2,1)S(1)}, bf16[4,32,768]{2,1,0:T(8,128)(2,1)S(1)}, u32[]{:S(2)}, u32[]{:S(2)}) collective-permute-start(bf16[4,32,768]{2,1,0:T(8,128)(2,1)S(1)} %get-tuple-element.22), channel_id=1, source_target_pairs={{0,2},{1,3},{2,0},{3,1},{4,6},{5,7},{6,4},{7,5},{8,10},{9,11},{10,... | collective-permute-start | bytes 589832 | tf_op jit(solution)/shard_map/ppermute | solution.py:222
  30.8 11.4 %collective-permute-start.3 = (bf16[4,32,768]{2,1,0:T(8,128)(2,1)S(1)}, bf16[4,32,768]{2,1,0:T(8,128)(2,1)S(1)}, u32[]{:S(2)}, u32[]{:S(2)}) collective-permute-start(bf16[4,32,768]{2,1,0:T(8,128)(2,1)S(1)} %get-tuple-element.23), channel_id=1, source_target_pairs={{0,3},{1,2},{2,1},{3,0},{4,7},{5,6},{6,5},{7,4},{8,11},{9,10},{10,... | collective-permute-start | bytes 589832 | tf_op jit(solution)/shard_map/ppermute | solution.py:222
  33.0 16.5 %all-to-all-start.1 = ((bf16[32,8,512]{2,1,0:T(8,128)(2,1)}), bf16[32,8,512]{2,1,0:T(8,128)(2,1)S(1)}, u32[]{:S(2)}, u32[]{:S(2)}) async-start(bf16[32,8,512]{2,1,0:T(8,128)(2,1)} %bitcast.3), calls=%async_computation.1 | async-start | bytes 524288 | tf_op jit(solution)/shard_map/all_to_all | solution.py:326
  42.2 5.3 %collective-permute-start.4 = (bf16[32,768]{1,0:T(8,128)(2,1)S(1)}, bf16[32,768]{1,0:T(8,128)(2,1)S(1)}, u32[]{:S(2)}, u32[]{:S(2)}) collective-permute-start(bf16[32,768]{1,0:T(8,128)(2,1)S(1)} %get-tuple-element.25), channel_id=1, source_target_pairs={{0,4},{4,0},{8,12},{12,8},{1,5},{5,1},{9,13},{13,9},{2,6},{6,2},{1... | collective-permute-start | bytes 147464 | tf_op jit(solution)/shard_map/ppermute | solution.py:222
  42.3 5.6 %collective-permute-start.5 = (bf16[32,768]{1,0:T(8,128)(2,1)S(1)}, bf16[32,768]{1,0:T(8,128)(2,1)S(1)}, u32[]{:S(2)}, u32[]{:S(2)}) collective-permute-start(bf16[32,768]{1,0:T(8,128)(2,1)S(1)} %get-tuple-element.26), channel_id=1, source_target_pairs={{0,8},{4,12},{8,0},{12,4},{1,9},{5,13},{9,1},{13,5},{2,10},{6,14},... | collective-permute-start | bytes 147464 | tf_op jit(solution)/shard_map/ppermute | solution.py:222
  43.3 6.1 %collective-permute-start.6 = (bf16[32,768]{1,0:T(8,128)(2,1)S(1)}, bf16[32,768]{1,0:T(8,128)(2,1)S(1)}, u32[]{:S(2)}, u32[]{:S(2)}) collective-permute-start(bf16[32,768]{1,0:T(8,128)(2,1)S(1)} %get-tuple-element.27), channel_id=1, source_target_pairs={{0,12},{4,8},{8,4},{12,0},{1,13},{5,9},{9,5},{13,1},{2,14},{6,10},... | collective-permute-start | bytes 147464 | tf_op jit(solution)/shard_map/ppermute | solution.py:222
  49.4 1.4 %collective-permute-start.7 = (f32[32,768]{1,0:T(8,128)S(1)}, f32[32,768]{1,0:T(8,128)S(1)}, u32[]{:S(2)}, u32[]{:S(2)}) collective-permute-start(f32[32,768]{1,0:T(8,128)S(1)} %add_multiply_fusion.own_ref), channel_id=1, source_target_pairs={{0,16},{16,0},{1,17},{17,1},{2,18},{18,2},{3,19},{19,3},{4,20},{20... | collective-permute-start | bytes 294920 | tf_op jit(solution)/shard_map/ppermute | solution.py:201

commit v10 on v9

--- a/solution.py
+++ b/solution.py
@@ -60,7 +60,8 @@
     copies[0].wait()
     sent_ref[:, :, :channels] = normalize(in_chunks(shape, tokens_buf[...]))[0].astype(BF16)
     copies[1].wait()
-    sent_ref[:, :, channels:] = in_chunks(shape, cot_buf[...]).astype(BF16)
+    cot = cot_buf[...].reshape(*shape, channels)
+    sent_ref[:, :, channels:] = jnp.concatenate([cot[index] for index in range(shape[0])], axis=1)
 
 
 def unpack_kernel(shape, returned_ref, tokens_ref, cot_ref, grad_ref):

time: 51.7 us -> 51.7 us (level)
  no operation moved by 1% of the time
where the time goes in v10:
time: 51.7 us; the launch traced here: 51.5 us
  blocking collectives  22.3 us (43%)
  starting transfers between devices  11.1 us (21%)
  waiting for transfers between devices  9.48 us (18%)
  Pallas kernels  7.88 us (15%)
  between operations  0.74 us (1%)
    all_to_all x1, blocking collectives, shards(): pixels = exchange(sent)  22.3 us
    ppermute x6, waiting for transfers between devices, travel(): lax.ppermute(part, axis, [(i, i ^ step) for i in range(size)])  8.88 us
    ppermute x6, starting transfers between devices, travel(): lax.ppermute(part, axis, [(i, i ^ step) for i in range(size)])  8 us
    pallas_call x8, Pallas kernels, vmem_call(): pl.pallas_call(kernel, out_shape=outs, in_specs=[hbm if index in remote e...  7.88 us
    all_to_all x1, starting transfers between devices, shards(): returned = exchange(spread)  2.94 us
  transfers between devices with their start and end apart: 9, of which 7 were waited for; matrix products, arithmetic and copies ran while one was open for 0% of the time, Pallas kernels for 8%

profile of v10, /device:TPU:0, one launch (start us, length us, event | category | flops | bytes accessed | tf_op | source)
XLA Modules:
  0.0 51.5 jit_solution(17167501926696020037)
XLA Ops:
  0.6 0.0 copy-start.3
  0.6 0.0 copy-start
  0.7 1.4 %pack.1 = bf16[32,8,1024]{2,1,0:T(8,128)(2,1)S(1)} custom-call(bf16[64,4,512]{2,1,0:T(4,128)(2,1)} %bitcast.9, bf16[64,4,512]{2,1,0:T(4,128)(2,1)} %bitcast.11), custom_call_target="tpu_custom_call" | custom-call | tf_op jit(solution)/shard_map/pack/pallas_call | solution.py:35
  2.1 22.3 %all_to_all.10 = bf16[32,8,1024]{2,1,0:T(8,128)(2,1)S(1)} all-to-all(bf16[32,8,1024]{2,1,0:T(8,128)(2,1)S(1)} %pack.1), channel_id=1, replica_groups={{0,8,16,24,4,12,20,28,2,10,18,26,6,14,22,30,1,9,17,25,5,13,21,29,3,11,1..., dimensions={0} | all-to-all | bytes 1048576 | tf_op jit(solution)/shard_map/all_to_all | solution.py:286
  24.3 0.0 copy-done.3
  24.3 0.0 copy-done
  24.3 1.6 %first_heads.1 = (bf16[256,768]{1,0:T(8,128)(2,1)S(1)}, bf16[256,512]{1,0:T(8,128)(2,1)S(1)}, bf16[512,768]{1,0:T(8,128)(2,1)S(1)}) custom-call(s32[1,256]{1,0:T(1,128)S(1)} %copy-done.3, bf16[256,1024]{1,0:T(8,128)(2,1)S(1)} %bitcast.7, bf16[512,1536]{1,0:T(8,128)(2,1)S(1)} %copy-done), custom_call_target="tpu_custom_call" | custom-call | tf_op jit(solution)/shard_map/first_heads/pallas_call | solution.py:35
  26.0 0.1 collective-permute-start
  26.0 1.8 %second_heads.1 = (bf16[256,512]{1,0:T(8,128)(2,1)S(1)}, bf16[512,768]{1,0:T(8,128)(2,1)S(1)}) custom-call(s32[1,256]{1,0:T(1,128)S(1)} %copy-done.3, bf16[256,1024]{1,0:T(8,128)(2,1)S(1)} %bitcast.8, bf16[512,1536]{1,0:T(8,128)(2,1)S(1)} %copy-done, bf16[256,768]{1,0:T(8,128)(2,1)S(1)} %get-tuple-element.15.first_ref, ...), custom_call_target="tpu_custom_call" | custom-call | tf_op jit(solution)/shard_map/second_heads/pallas_call | solution.py:35
  27.9 0.5 collective-permute-done
  28.3 0.2 split_tx.1
  28.5 1.5 %collective-permute-start.1 = (bf16[4,32,768]{2,1,0:T(8,128)(2,1)S(1)}, bf16[4,32,768]{2,1,0:T(8,128)(2,1)S(1)}, u32[]{:S(2)}, u32[]{:S(2)}) collective-permute-start(bf16[4,32,768]{2,1,0:T(8,128)(2,1)S(1)} %get-tuple-element.21), channel_id=1, source_target_pairs={{0,1},{1,0},{2,3},{3,2},{4,5},{5,4},{6,7},{7,6},{8,9},{9,8},{10,11... | collective-permute-start | bytes 589832 | tf_op jit(solution)/shard_map/ppermute | solution.py:223
  30.0 0.8 %collective-permute-start.2 = (bf16[4,32,768]{2,1,0:T(8,128)(2,1)S(1)}, bf16[4,32,768]{2,1,0:T(8,128)(2,1)S(1)}, u32[]{:S(2)}, u32[]{:S(2)}) collective-permute-start(bf16[4,32,768]{2,1,0:T(8,128)(2,1)S(1)} %get-tuple-element.22), channel_id=1, source_target_pairs={{0,2},{1,3},{2,0},{3,1},{4,6},{5,7},{6,4},{7,5},{8,10},{9,11},{10,... | collective-permute-start | bytes 589832 | tf_op jit(solution)/shard_map/ppermute | solution.py:223
  30.8 1.3 %collective-permute-start.3 = (bf16[4,32,768]{2,1,0:T(8,128)(2,1)S(1)}, bf16[4,32,768]{2,1,0:T(8,128)(2,1)S(1)}, u32[]{:S(2)}, u32[]{:S(2)}) collective-permute-start(bf16[4,32,768]{2,1,0:T(8,128)(2,1)S(1)} %get-tuple-element.23), channel_id=1, source_target_pairs={{0,3},{1,2},{2,1},{3,0},{4,7},{5,6},{6,5},{7,4},{8,11},{9,10},{10,... | collective-permute-start | bytes 589832 | tf_op jit(solution)/shard_map/ppermute | solution.py:223
  32.0 1.0 %spread.1 = bf16[256,512]{1,0:T(8,128)(2,1)} custom-call(s32[1,256]{1,0:T(1,128)S(1)} %copy-done.3, bf16[256,512]{1,0:T(8,128)(2,1)S(1)} %get-tuple-element.17.grad_ref), custom_call_target="tpu_custom_call" | custom-call | tf_op jit(solution)/shard_map/spread/pallas_call | solution.py:35
  33.0 2.9 %all-to-all-start.1 = ((bf16[32,8,512]{2,1,0:T(8,128)(2,1)}), bf16[32,8,512]{2,1,0:T(8,128)(2,1)S(1)}, u32[]{:S(2)}, u32[]{:S(2)}) async-start(bf16[32,8,512]{2,1,0:T(8,128)(2,1)} %bitcast.3), calls=%async_computation.1 | async-start | bytes 524288 | tf_op jit(solution)/shard_map/all_to_all | solution.py:327
  35.9 0.4 collective-permute-done.1.refs_1_
  36.3 5.8 %collective-permute-done.2.refs_2_ = bf16[4,32,768]{2,1,0:T(8,128)(2,1)S(1)} collective-permute-done((bf16[4,32,768]{2,1,0:T(8,128)(2,1)S(1)}, bf16[4,32,768]{2,1,0:T(8,128)(2,1)S(1)}, u32[]{:S(2)}, u32[]{:S(2)}) %collective-permute-start.2) | collective-permute-done | bytes 196640 | tf_op jit(solution)/shard_map/ppermute | solution.py:223
  42.1 0.0 collective-permute-done.3.refs_3_
  42.1 0.1 split_ty.1
  42.2 0.1 collective-permute-start.4
  42.3 1.0 %collective-permute-start.5 = (bf16[32,768]{1,0:T(8,128)(2,1)S(1)}, bf16[32,768]{1,0:T(8,128)(2,1)S(1)}, u32[]{:S(2)}, u32[]{:S(2)}) collective-permute-start(bf16[32,768]{1,0:T(8,128)(2,1)S(1)} %get-tuple-element.26), channel_id=1, source_target_pairs={{0,8},{4,12},{8,0},{12,4},{1,9},{5,13},{9,1},{13,5},{2,10},{6,14},... | collective-permute-start | bytes 147464 | tf_op jit(solution)/shard_map/ppermute | solution.py:223
  43.3 3.4 %collective-permute-start.6 = (bf16[32,768]{1,0:T(8,128)(2,1)S(1)}, bf16[32,768]{1,0:T(8,128)(2,1)S(1)}, u32[]{:S(2)}, u32[]{:S(2)}) collective-permute-start(bf16[32,768]{1,0:T(8,128)(2,1)S(1)} %get-tuple-element.27), channel_id=1, source_target_pairs={{0,12},{4,8},{8,4},{12,0},{1,13},{5,9},{9,5},{13,1},{2,14},{6,10},... | collective-permute-start | bytes 147464 | tf_op jit(solution)/shard_map/ppermute | solution.py:223
  46.7 0.8 %collective-permute-done.4 = bf16[32,768]{1,0:T(8,128)(2,1)S(1)} collective-permute-done((bf16[32,768]{1,0:T(8,128)(2,1)S(1)}, bf16[32,768]{1,0:T(8,128)(2,1)S(1)}, u32[]{:S(2)}, u32[]{:S(2)}) %collective-permute-start.4) | collective-permute-done | bytes 49184 | tf_op jit(solution)/shard_map/ppermute | solution.py:223
  47.5 0.4 collective-permute-done.5
  48.0 1.4 %collective-permute-done.6 = bf16[32,768]{1,0:T(8,128)(2,1)S(1)} collective-permute-done((bf16[32,768]{1,0:T(8,128)(2,1)S(1)}, bf16[32,768]{1,0:T(8,128)(2,1)S(1)}, u32[]{:S(2)}, u32[]{:S(2)}) %collective-permute-start.6) | collective-permute-done | bytes 49184 | tf_op jit(solution)/shard_map/ppermute | solution.py:223
  49.4 0.1 collective-permute-start.7
  49.5 0.0 all-to-all-done.1.returned_ref
  49.5 0.0 copy-done.1
  49.5 1.1 %token_grad.1 = bf16[64,4,512]{2,1,0:T(4,128)(2,1)} custom-call(bf16[32,8,512]{2,1,0:T(8,128)(2,1)S(1)} %all-to-all-done.1.returned_ref, bf16[64,4,512]{2,1,0:T(4,128)(2,1)S(1)} %bitcast.10, bf16[64,4,512]{2,1,0:T(4,128)(2,1)S(1)} %bitcast.12), custom_call_target="tpu_custom_call" | custom-call | tf_op jit(solution)/shard_map/token_grad/pallas_call | solution.py:35
  50.6 0.1 collective-permute-done.7.other_ref
  50.8 0.7 %weight_grad.1 = f32[32,1536]{1,0:T(8,128)} custom-call(f32[32,768]{1,0:T(8,128)S(1)} %add_multiply_fusion.own_ref, f32[32,768]{1,0:T(8,128)S(1)} %collective-permute-done.7.other_ref), custom_call_target="tpu_custom_call" | custom-call | tf_op jit(solution)/shard_map/weight_grad/pallas_call | solution.py:35
  (4 shorter events, 0.0 us)
Async XLA Ops:
  0.6 23.7 %copy-start.3 = (s32[1,256]{1,0:T(1,128)S(1)}, s32[1,256]{1,0:T(1,128)}, u32[]{:S(2)}) copy-start(s32[1,256]{1,0:T(1,128)} %constant.5.clone.pos_ref) | copy-start | bytes 3076
  0.6 23.7 %copy-start = (bf16[512,1536]{1,0:T(8,128)(2,1)S(1)}, bf16[512,1536]{1,0:T(8,128)(2,1)}, u32[]{:S(2)}) copy-start(bf16[512,1536]{1,0:T(8,128)(2,1)} %weight_ref.3) | copy-start | bytes 4718596
  26.0 2.4 %collective-permute-start = (bf16[512,768]{1,0:T(8,128)(2,1)S(1)}, bf16[512,768]{1,0:T(8,128)(2,1)S(1)}, u32[]{:S(2)}, u32[]{:S(2)}) collective-permute-start(bf16[512,768]{1,0:T(8,128)(2,1)S(1)} %get-tuple-element.19), channel_id=1, source_target_pairs={{0,16},{16,0},{1,17},{17,1},{2,18},{18,2},{3,19},{19,3},{4,20},{20... | collective-permute-start | bytes 2359304 | tf_op jit(solution)/shard_map/ppermute | solution.py:202
  28.3 21.2 %copy-start.1 = (bf16[1,64,4,512]{3,2,1,0:T(4,128)(2,1)S(1)}, bf16[1,64,4,512]{3,2,1,0:T(4,128)(2,1)}, u32[]{:S(2)}) copy-start(bf16[1,64,4,512]{3,2,1,0:T(4,128)(2,1)} %param.4) | copy-start | bytes 786436
  28.3 21.2 %copy-start.2 = (bf16[1,64,4,512]{3,2,1,0:T(4,128)(2,1)S(1)}, bf16[1,64,4,512]{3,2,1,0:T(4,128)(2,1)}, u32[]{:S(2)}) copy-start(bf16[1,64,4,512]{3,2,1,0:T(4,128)(2,1)} %param.6) | copy-start | bytes 786436
  28.5 7.8 %collective-permute-start.1 = (bf16[4,32,768]{2,1,0:T(8,128)(2,1)S(1)}, bf16[4,32,768]{2,1,0:T(8,128)(2,1)S(1)}, u32[]{:S(2)}, u32[]{:S(2)}) collective-permute-start(bf16[4,32,768]{2,1,0:T(8,128)(2,1)S(1)} %get-tuple-element.21), channel_id=1, source_target_pairs={{0,1},{1,0},{2,3},{3,2},{4,5},{5,4},{6,7},{7,6},{8,9},{9,8},{10,11... | collective-permute-start | bytes 589832 | tf_op jit(solution)/shard_map/ppermute | solution.py:223
  30.0 12.2 %collective-permute-start.2 = (bf16[4,32,768]{2,1,0:T(8,128)(2,1)S(1)}, bf16[4,32,768]{2,1,0:T(8,128)(2,1)S(1)}, u32[]{:S(2)}, u32[]{:S(2)}) collective-permute-start(bf16[4,32,768]{2,1,0:T(8,128)(2,1)S(1)} %get-tuple-element.22), channel_id=1, source_target_pairs={{0,2},{1,3},{2,0},{3,1},{4,6},{5,7},{6,4},{7,5},{8,10},{9,11},{10,... | collective-permute-start | bytes 589832 | tf_op jit(solution)/shard_map/ppermute | solution.py:223
  30.8 11.4 %collective-permute-start.3 = (bf16[4,32,768]{2,1,0:T(8,128)(2,1)S(1)}, bf16[4,32,768]{2,1,0:T(8,128)(2,1)S(1)}, u32[]{:S(2)}, u32[]{:S(2)}) collective-permute-start(bf16[4,32,768]{2,1,0:T(8,128)(2,1)S(1)} %get-tuple-element.23), channel_id=1, source_target_pairs={{0,3},{1,2},{2,1},{3,0},{4,7},{5,6},{6,5},{7,4},{8,11},{9,10},{10,... | collective-permute-start | bytes 589832 | tf_op jit(solution)/shard_map/ppermute | solution.py:223
  33.0 16.5 %all-to-all-start.1 = ((bf16[32,8,512]{2,1,0:T(8,128)(2,1)}), bf16[32,8,512]{2,1,0:T(8,128)(2,1)S(1)}, u32[]{:S(2)}, u32[]{:S(2)}) async-start(bf16[32,8,512]{2,1,0:T(8,128)(2,1)} %bitcast.3), calls=%async_computation.1 | async-start | bytes 524288 | tf_op jit(solution)/shard_map/all_to_all | solution.py:327
  42.2 5.3 %collective-permute-start.4 = (bf16[32,768]{1,0:T(8,128)(2,1)S(1)}, bf16[32,768]{1,0:T(8,128)(2,1)S(1)}, u32[]{:S(2)}, u32[]{:S(2)}) collective-permute-start(bf16[32,768]{1,0:T(8,128)(2,1)S(1)} %get-tuple-element.25), channel_id=1, source_target_pairs={{0,4},{4,0},{8,12},{12,8},{1,5},{5,1},{9,13},{13,9},{2,6},{6,2},{1... | collective-permute-start | bytes 147464 | tf_op jit(solution)/shard_map/ppermute | solution.py:223
  42.3 5.6 %collective-permute-start.5 = (bf16[32,768]{1,0:T(8,128)(2,1)S(1)}, bf16[32,768]{1,0:T(8,128)(2,1)S(1)}, u32[]{:S(2)}, u32[]{:S(2)}) collective-permute-start(bf16[32,768]{1,0:T(8,128)(2,1)S(1)} %get-tuple-element.26), channel_id=1, source_target_pairs={{0,8},{4,12},{8,0},{12,4},{1,9},{5,13},{9,1},{13,5},{2,10},{6,14},... | collective-permute-start | bytes 147464 | tf_op jit(solution)/shard_map/ppermute | solution.py:223
  43.3 6.1 %collective-permute-start.6 = (bf16[32,768]{1,0:T(8,128)(2,1)S(1)}, bf16[32,768]{1,0:T(8,128)(2,1)S(1)}, u32[]{:S(2)}, u32[]{:S(2)}) collective-permute-start(bf16[32,768]{1,0:T(8,128)(2,1)S(1)} %get-tuple-element.27), channel_id=1, source_target_pairs={{0,12},{4,8},{8,4},{12,0},{1,13},{5,9},{9,5},{13,1},{2,14},{6,10},... | collective-permute-start | bytes 147464 | tf_op jit(solution)/shard_map/ppermute | solution.py:223
  49.4 1.4 %collective-permute-start.7 = (f32[32,768]{1,0:T(8,128)S(1)}, f32[32,768]{1,0:T(8,128)S(1)}, u32[]{:S(2)}, u32[]{:S(2)}) collective-permute-start(f32[32,768]{1,0:T(8,128)S(1)} %add_multiply_fusion.own_ref), channel_id=1, source_target_pairs={{0,16},{16,0},{1,17},{17,1},{2,18},{18,2},{3,19},{19,3},{4,20},{20... | collective-permute-start | bytes 294920 | tf_op jit(solution)/shard_map/ppermute | solution.py:202
